TPU v7x, 128 devices: a whole 4x4x4 slice. The times are simulated.
128 devices in a mesh: seq: 16 (over x, y), head: 8 (over z, core).
Axes of the slice: x: 4, y: 4, z: 4, core: 2. Of those that a mesh axis runs over, the one named last changes fastest.
Arguments:
- attn_queries: float32 [4096, 4096], P('seq', 'head'), may hold values from -6 to 6
- attn_keys: float32 [4096, 4096], P('seq', 'head'), may hold values from -6 to 6
- attn_values: float32 [4096, 4096], P('seq', 'head'), may hold values from -6 to 6
- head_gain: float32 [128], replicated, may hold values from 0.25 to 1.75
- out_weight: bfloat16 [4096, 2048], P('head'), may hold values from -0.09375 to 0.09375
- residual_in: bfloat16 [4096, 2048], P(('seq', 'head')), may hold values from -6 to 6
- norm_gain: float32 [2048], replicated, may hold values from 0.25 to 1.75
- routed_experts: int32 [4096, 8], P(('seq', 'head')), may hold values from 0 to 127, all different within a row; in each aligned block of 32 rows (0 to 31, 32 to 63, ...) at most 5 rows name the same one
- gate_weights: float32 [4096, 8], P(('seq', 'head')), may hold values from 0.05 to 1
- expert_gate: bfloat16 [128, 2048, 768], P(('seq', 'head')), may hold values from -0.125 to 0.125
- expert_up: bfloat16 [128, 2048, 768], P(('seq', 'head')), may hold values from -0.125 to 0.125
- expert_down: bfloat16 [128, 768, 2048], P(('seq', 'head')), may hold values from -0.21875 to 0.21875
Outputs:
- attn_out: bfloat16 [4096, 2048], P(('seq', 'head'))
- moe_out: bfloat16 [4096, 2048], P(('seq', 'head'))
Inputs may be any that keep to these rules, and one draw needn't show every extreme that they name: `routed_experts`: the 8 experts of a token differ. In each aligned block of 32 rows no expert is named by more than 5 rows, and in some block one expert is named by exactly 5 rows.
All inputs are finite; a program needn't handle non-finite values.
Results may differ from a plain program's by a relative error of at most 0.03.
Values may be sent and summed in bfloat16 or wider, within the bound.
No kernel may reach another device: no remote copies, remote signals or barrier semaphores. Data moves between devices by JAX's collectives and lax.ppermute only.
A program may use at most 64 MiB of HBM per device.

v0:
```python
import jax
import jax.numpy as jnp
from jax import lax
from jax.sharding import PartitionSpec as P


def passed_along(value, axis, by):
    peers = lax.axis_size(axis)
    pairs = [(i, i + by) for i in range(peers) if 0 <= i + by < peers]
    return lax.ppermute(value, axis, pairs)


def causal_linear(queries_here, keys_here, values_here, start_state, block_size):
    row_count = queries_here.shape[0]
    head_count = queries_here.shape[1]
    head_size = queries_here.shape[2]
    block_count = row_count // block_size
    lower_mask = jnp.tril(jnp.ones((block_size, block_size), jnp.float32))
    exact_mode = lax.Precision.HIGHEST

    def advance(state_now, inputs):
        query_block, key_block, value_block = inputs
        scores = (
            jnp.einsum("thd,shd->hts", query_block, key_block, precision=exact_mode) * lower_mask
        )
        within = jnp.einsum("hts,she->the", scores, value_block, precision=exact_mode)
        carried = jnp.einsum("thd,hde->the", query_block, state_now, precision=exact_mode)
        state_next = state_now + jnp.einsum(
            "thd,the->hde", key_block, value_block, precision=exact_mode
        )
        return (state_next, within + carried)

    def blocked(tensor):
        return tensor.reshape(block_count, block_size, head_count, head_size)

    state_last, outputs = lax.scan(
        advance, start_state, (blocked(queries_here), blocked(keys_here), blocked(values_here))
    )
    return outputs.reshape(row_count, head_count, head_size)


def rms_scale(tensor, gain_row):
    return tensor * lax.rsqrt(jnp.mean(tensor * tensor, axis=-1, keepdims=True) + 1e-06) * gain_row


def shards(
    attn_queries,
    attn_keys,
    attn_values,
    head_gain,
    out_weight,
    residual_in,
    norm_gain,
    routed_experts,
    gate_weights,
    expert_gate,
    expert_up,
    expert_down,
):
    token_count = attn_queries.shape[0]
    head_size = head_gain.shape[0]
    heads_here = attn_queries.shape[1] // head_size
    block_size = min(512, token_count)
    queries_here = attn_queries.reshape(token_count, heads_here, head_size)
    keys_here = attn_keys.reshape(token_count, heads_here, head_size)
    values_here = attn_values.reshape(token_count, heads_here, head_size)
    totals = jnp.einsum("thd,the->hde", keys_here, values_here, precision=lax.Precision.HIGHEST)

    def relay(stepper, carried_pair):
        moving, summed = carried_pair
        moving = passed_along(moving.astype(jnp.bfloat16), "seq", 1).astype(moving.dtype)
        return (moving, summed + moving)

    moving_last, prefix_state = lax.fori_loop(
        0, lax.axis_size("seq") - 1, relay, (totals, jnp.zeros_like(totals))
    )
    attended = causal_linear(queries_here, keys_here, values_here, prefix_state, block_size)
    head_normed = (
        rms_scale(attended, head_gain)
        .astype(jnp.bfloat16)
        .reshape(token_count, heads_here * head_size)
    )
    row_share = token_count // lax.axis_size("head")
    attn_out = lax.psum_scatter(
        jnp.dot(head_normed, out_weight, preferred_element_type=jnp.float32).astype(jnp.bfloat16),
        "head",
        scatter_dimension=0,
        tiled=True,
    )
    mixed = residual_in.astype(jnp.float32) + attn_out.astype(jnp.float32)
    moe_input = rms_scale(mixed, norm_gain).astype(jnp.bfloat16)
    model_width = moe_input.shape[1]
    top_count = routed_experts.shape[1]
    seq_devices = lax.axis_size("seq")
    head_devices = lax.axis_size("head")
    device_count = seq_devices * head_devices
    local_experts = expert_gate.shape[0]
    expert_count = device_count * local_experts
    capacity = 5 * row_share * top_count // (2 * expert_count)
    flat_experts = routed_experts.reshape(row_share * top_count)
    member = (flat_experts[:, None] == jnp.arange(expert_count, dtype=jnp.int32)[None, :]).astype(
        jnp.int32
    )
    earlier_count = jnp.cumsum(member, axis=0) - member
    position = jnp.sum(earlier_count * member, axis=1)
    target = flat_experts * capacity + position
    slot_ids = jnp.arange(expert_count * capacity, dtype=jnp.int32)
    placing = (
        (slot_ids[:, None] == target[None, :])
        .astype(jnp.bfloat16)
        .reshape(expert_count * capacity, row_share, top_count)
    )
    dispatch_table = jnp.sum(placing, axis=2)
    outgoing = (
        jnp.dot(dispatch_table, moe_input, preferred_element_type=jnp.float32)
        .astype(jnp.bfloat16)
        .reshape(expert_count, capacity, model_width)
    )
    arrived = lax.all_to_all(outgoing, ("seq", "head"), split_axis=0, concat_axis=0, tiled=True)
    slot_count = arrived.shape[1]
    grouped = arrived.reshape(device_count, local_experts, slot_count, model_width)
    gate_part = jnp.einsum(
        "sxcd,xdf->sxcf", grouped, expert_gate, preferred_element_type=jnp.float32
    )
    up_part = jnp.einsum("sxcd,xdf->sxcf", grouped, expert_up, preferred_element_type=jnp.float32)
    hidden_act = (jax.nn.silu(gate_part) * up_part).astype(jnp.bfloat16)
    produced = jnp.einsum(
        "sxcf,xfd->sxcd", hidden_act, expert_down, preferred_element_type=jnp.float32
    ).astype(jnp.bfloat16)
    returned = lax.all_to_all(
        produced.reshape(expert_count, slot_count, model_width),
        ("seq", "head"),
        split_axis=0,
        concat_axis=0,
        tiled=True,
    )
    back_rows = returned.reshape(expert_count * capacity, model_width)
    picked_rows = back_rows[target].reshape(row_share, top_count, model_width)
    moe_out = jnp.sum(gate_weights[:, :, None] * picked_rows.astype(jnp.float32), axis=1).astype(
        jnp.bfloat16
    )
    return (attn_out, moe_out)


def solution(mesh):
    return jax.shard_map(
        shards,
        mesh=mesh,
        in_specs=(
            P("seq", "head"),
            P("seq", "head"),
            P("seq", "head"),
            P(),
            P("head", None),
            P(("seq", "head"), None),
            P(),
            P(("seq", "head"), None),
            P(("seq", "head"), None),
            P(("seq", "head"), None, None),
            P(("seq", "head"), None, None),
            P(("seq", "head"), None, None),
        ),
        out_specs=(P(("seq", "head"), None), P(("seq", "head"), None)),
        check_vma=False,
    )
```

profile of v0, /device:TPU:1, one launch (start us, length us, event | category | flops | bytes accessed | tf_op | source)
XLA Modules:
  0.0 378.9 jit_solution(15708043928141960280)
XLA Ops:
  8.0 2.3 copy.64
  10.2 2.5 fusion.27
  12.7 124.0 %while.3 = (s32[]{:T(128)}, bf16[4,128,128]{2,1,0:T(8,128)(2,1)}, f32[4,128,128]{2,1,0:T(8,128)S(1)}, s32[]{:T(128)}, s32[]{:T(128)}) while((s32[]{:T(128)}, bf16[4,128,128]{2,1,0:T(8,128)(2,1)}, f32[4,128,128]{2,1,0:T(8,128)S(1)}, s32[]{:T(128)}, s32[]{:T(128)}) %tuple.34), condition=%wide.region_1.0_spmd.clone, body=%wide.region_0.0_spmd.clone.sunk | while | flops 262147 | bytes 1310831 | solution.py:74
  12.7 4.0 %collective-permute-start = (bf16[4,128,128]{2,1,0:T(8,128)(2,1)}, bf16[4,128,128]{2,1,0:T(8,128)(2,1)S(1)}, u32[]{:S(2)}, u32[]{:S(2)}) collective-permute-start(bf16[4,128,128]{2,1,0:T(8,128)(2,1)} %get-tuple-element.96), channel_id=1, source_target_pairs={{0,8},{8,16},{16,24},{24,32},{32,40},{40,48},{48,56},{56,64},{64,7... | collective-permute-start | bytes 393224 | tf_op jit(solution)/shard_map/while/body/eval_jaxpr/ppermute | solution.py:10
  16.8 2.5 collective-permute-done
  19.9 4.0 %collective-permute-start = (bf16[4,128,128]{2,1,0:T(8,128)(2,1)}, bf16[4,128,128]{2,1,0:T(8,128)(2,1)S(1)}, u32[]{:S(2)}, u32[]{:S(2)}) collective-permute-start(bf16[4,128,128]{2,1,0:T(8,128)(2,1)} %get-tuple-element.96), channel_id=1, source_target_pairs={{0,8},{8,16},{16,24},{24,32},{32,40},{40,48},{48,56},{56,64},{64,7... | collective-permute-start | bytes 393224 | tf_op jit(solution)/shard_map/while/body/eval_jaxpr/ppermute | solution.py:10
  24.0 2.2 collective-permute-done
  26.9 3.7 collective-permute-start
  30.6 2.2 collective-permute-done
  33.5 3.7 collective-permute-start
  37.2 2.2 collective-permute-done
  40.2 3.7 collective-permute-start
  43.8 2.2 collective-permute-done
  46.8 5.8 %collective-permute-start = (bf16[4,128,128]{2,1,0:T(8,128)(2,1)}, bf16[4,128,128]{2,1,0:T(8,128)(2,1)S(1)}, u32[]{:S(2)}, u32[]{:S(2)}) collective-permute-start(bf16[4,128,128]{2,1,0:T(8,128)(2,1)} %get-tuple-element.96), channel_id=1, source_target_pairs={{0,8},{8,16},{16,24},{24,32},{32,40},{40,48},{48,56},{56,64},{64,7... | collective-permute-start | bytes 393224 | tf_op jit(solution)/shard_map/while/body/eval_jaxpr/ppermute | solution.py:10
  52.6 2.2 collective-permute-done
  55.5 5.8 %collective-permute-start = (bf16[4,128,128]{2,1,0:T(8,128)(2,1)}, bf16[4,128,128]{2,1,0:T(8,128)(2,1)S(1)}, u32[]{:S(2)}, u32[]{:S(2)}) collective-permute-start(bf16[4,128,128]{2,1,0:T(8,128)(2,1)} %get-tuple-element.96), channel_id=1, source_target_pairs={{0,8},{8,16},{16,24},{24,32},{32,40},{40,48},{48,56},{56,64},{64,7... | collective-permute-start | bytes 393224 | tf_op jit(solution)/shard_map/while/body/eval_jaxpr/ppermute | solution.py:10
  61.3 2.2 collective-permute-done
  64.3 5.8 %collective-permute-start = (bf16[4,128,128]{2,1,0:T(8,128)(2,1)}, bf16[4,128,128]{2,1,0:T(8,128)(2,1)S(1)}, u32[]{:S(2)}, u32[]{:S(2)}) collective-permute-start(bf16[4,128,128]{2,1,0:T(8,128)(2,1)} %get-tuple-element.96), channel_id=1, source_target_pairs={{0,8},{8,16},{16,24},{24,32},{32,40},{40,48},{48,56},{56,64},{64,7... | collective-permute-start | bytes 393224 | tf_op jit(solution)/shard_map/while/body/eval_jaxpr/ppermute | solution.py:10
  70.0 2.2 collective-permute-done
  73.0 5.8 %collective-permute-start = (bf16[4,128,128]{2,1,0:T(8,128)(2,1)}, bf16[4,128,128]{2,1,0:T(8,128)(2,1)S(1)}, u32[]{:S(2)}, u32[]{:S(2)}) collective-permute-start(bf16[4,128,128]{2,1,0:T(8,128)(2,1)} %get-tuple-element.96), channel_id=1, source_target_pairs={{0,8},{8,16},{16,24},{24,32},{32,40},{40,48},{48,56},{56,64},{64,7... | collective-permute-start | bytes 393224 | tf_op jit(solution)/shard_map/while/body/eval_jaxpr/ppermute | solution.py:10
  78.8 2.9 collective-permute-done
  82.4 6.1 %collective-permute-start = (bf16[4,128,128]{2,1,0:T(8,128)(2,1)}, bf16[4,128,128]{2,1,0:T(8,128)(2,1)S(1)}, u32[]{:S(2)}, u32[]{:S(2)}) collective-permute-start(bf16[4,128,128]{2,1,0:T(8,128)(2,1)} %get-tuple-element.96), channel_id=1, source_target_pairs={{0,8},{8,16},{16,24},{24,32},{32,40},{40,48},{48,56},{56,64},{64,7... | collective-permute-start | bytes 393224 | tf_op jit(solution)/shard_map/while/body/eval_jaxpr/ppermute | solution.py:10
  88.5 3.2 collective-permute-done
  92.4 6.1 %collective-permute-start = (bf16[4,128,128]{2,1,0:T(8,128)(2,1)}, bf16[4,128,128]{2,1,0:T(8,128)(2,1)S(1)}, u32[]{:S(2)}, u32[]{:S(2)}) collective-permute-start(bf16[4,128,128]{2,1,0:T(8,128)(2,1)} %get-tuple-element.96), channel_id=1, source_target_pairs={{0,8},{8,16},{16,24},{24,32},{32,40},{40,48},{48,56},{56,64},{64,7... | collective-permute-start | bytes 393224 | tf_op jit(solution)/shard_map/while/body/eval_jaxpr/ppermute | solution.py:10
  98.6 2.2 collective-permute-done
  101.5 5.4 %collective-permute-start = (bf16[4,128,128]{2,1,0:T(8,128)(2,1)}, bf16[4,128,128]{2,1,0:T(8,128)(2,1)S(1)}, u32[]{:S(2)}, u32[]{:S(2)}) collective-permute-start(bf16[4,128,128]{2,1,0:T(8,128)(2,1)} %get-tuple-element.96), channel_id=1, source_target_pairs={{0,8},{8,16},{16,24},{24,32},{32,40},{40,48},{48,56},{56,64},{64,7... | collective-permute-start | bytes 393224 | tf_op jit(solution)/shard_map/while/body/eval_jaxpr/ppermute | solution.py:10
  107.0 2.2 collective-permute-done
  109.9 6.1 %collective-permute-start = (bf16[4,128,128]{2,1,0:T(8,128)(2,1)}, bf16[4,128,128]{2,1,0:T(8,128)(2,1)S(1)}, u32[]{:S(2)}, u32[]{:S(2)}) collective-permute-start(bf16[4,128,128]{2,1,0:T(8,128)(2,1)} %get-tuple-element.96), channel_id=1, source_target_pairs={{0,8},{8,16},{16,24},{24,32},{32,40},{40,48},{48,56},{56,64},{64,7... | collective-permute-start | bytes 393224 | tf_op jit(solution)/shard_map/while/body/eval_jaxpr/ppermute | solution.py:10
  116.0 2.2 collective-permute-done
  119.0 6.1 %collective-permute-start = (bf16[4,128,128]{2,1,0:T(8,128)(2,1)}, bf16[4,128,128]{2,1,0:T(8,128)(2,1)S(1)}, u32[]{:S(2)}, u32[]{:S(2)}) collective-permute-start(bf16[4,128,128]{2,1,0:T(8,128)(2,1)} %get-tuple-element.96), channel_id=1, source_target_pairs={{0,8},{8,16},{16,24},{24,32},{32,40},{40,48},{48,56},{56,64},{64,7... | collective-permute-start | bytes 393224 | tf_op jit(solution)/shard_map/while/body/eval_jaxpr/ppermute | solution.py:10
  125.1 2.2 collective-permute-done
  128.1 5.8 %collective-permute-start = (bf16[4,128,128]{2,1,0:T(8,128)(2,1)}, bf16[4,128,128]{2,1,0:T(8,128)(2,1)S(1)}, u32[]{:S(2)}, u32[]{:S(2)}) collective-permute-start(bf16[4,128,128]{2,1,0:T(8,128)(2,1)} %get-tuple-element.96), channel_id=1, source_target_pairs={{0,8},{8,16},{16,24},{24,32},{32,40},{40,48},{48,56},{56,64},{64,7... | collective-permute-start | bytes 393224 | tf_op jit(solution)/shard_map/while/body/eval_jaxpr/ppermute | solution.py:10
  133.8 2.2 collective-permute-done
  138.5 2.4 convolution_multiply_fusion
  142.4 1.7 convolution_convert_fusion.2
  145.4 55.2 %reduce-scatter.2.cloned.1.call-done = bf16[32,2048]{1,0:T(8,128)(2,1)} async-done(((bf16[256,2048]{1,0:T(8,128)(2,1)}), bf16[32,2048]{1,0:T(8,128)(2,1)}) %reduce-scatter.2.cloned.1.call-update) | async-done | bytes 131088 | tf_op jit(solution)/shard_map/reduce_scatter | solution.py:84
  201.7 3.3 convolution_convert_fusion.1
  205.0 5.5 %reshape.137 = bf16[128,5,2048]{2,1,0:T(8,128)(2,1)} reshape(bf16[640,2048]{1,0:T(8,128)(2,1)} %convolution_convert_fusion.1) | data formatting | bytes 5242880 | tf_op jit(solution)/shard_map/reshape | solution.py:117
  210.5 63.1 %all_to_all.10 = bf16[128,5,2048]{2,1,0:T(8,128)(2,1)S(1)} all-to-all(bf16[128,5,2048]{2,1,0:T(8,128)(2,1)} %reshape.137), channel_id=1, replica_groups=mesh['seq'=16,'head'=8] {'seq','head'}, dimensions={0} | all-to-all | bytes 5242880 | tf_op jit(solution)/shard_map/all_to_all | solution.py:119
  273.6 2.0 copy-done.1
  275.6 6.5 %fusion.3 = f32[128,5,768]{2,0,1:T(8,128)} fusion(bf16[1,2048,768]{2,1,0:T(8,128)(2,1)S(1)} %copy-done.9, bf16[128,5,2048]{2,1,0:T(8,128)(2,1)S(1)} %all_to_all.10), kind=kOutput, calls=%fused_computation.7 | convolution fusion | flops 2013265920 | bytes 7733248 | tf_op jit(solution)/shard_map/sxcd,xdf->sxcf/dot_general | solution.py:122
  282.0 12.0 %convolution_convert_fusion = bf16[128,5,2048]{2,0,1:T(8,128)(2,1)} fusion(bf16[1,768,2048]{2,1,0:T(8,128)(2,1)S(1)} %copy-done, bf16[1,2048,768]{2,1,0:T(8,128)(2,1)} %param.24, bf16[128,5,2048]{2,1,0:T(8,128)(2,1)} %copy-done.1, f32[128,5,768]{2,0,1:T(8,128)} %fusion.3), kind=kOutput, calls=%fused_computation.2 | convolution fusion | flops 4030791680 | bytes 13500416 | tf_op jit(solution)/shard_map/sxcf,xfd->sxcd/dot_general | solution.py:127
  294.0 5.4 %copy.62 = bf16[128,5,2048]{2,1,0:T(8,128)(2,1)} copy(bf16[128,5,2048]{2,0,1:T(8,128)(2,1)} %convolution_convert_fusion) | data formatting | bytes 5242880 | tf_op jit(solution)/shard_map/convert_element_type | solution.py:129
  299.5 5.9 %all-to-all-start.1 = ((bf16[128,5,2048]{2,1,0:T(8,128)(2,1)}), bf16[128,5,2048]{2,1,0:T(8,128)(2,1)}, u32[]{:S(2)}, u32[]{:S(2)}) async-start(bf16[128,5,2048]{2,1,0:T(8,128)(2,1)} %copy.62), calls=%async_computation.2 | async-start | bytes 8388608 | tf_op jit(solution)/shard_map/all_to_all | solution.py:130
  305.5 52.6 %all-to-all-done.1 = bf16[128,5,2048]{2,1,0:T(8,128)(2,1)} async-done(((bf16[128,5,2048]{2,1,0:T(8,128)(2,1)}), bf16[128,5,2048]{2,1,0:T(8,128)(2,1)}, u32[]{:S(2)}, u32[]{:S(2)}) %all-to-all-start.1) | async-done | bytes 2621472 | tf_op jit(solution)/shard_map/all_to_all | solution.py:130
  358.2 5.6 %reshape.142 = bf16[640,2048]{1,0:T(8,128)(2,1)} reshape(bf16[128,5,2048]{2,1,0:T(8,128)(2,1)} %all-to-all-done.1) | data formatting | bytes 5242880 | tf_op jit(solution)/shard_map/reshape | solution.py:137
  363.8 5.4 %gather_fusion = bf16[256,2048]{1,0:T(8,128)(2,1)} fusion(bf16[640,2048]{1,0:T(8,128)(2,1)} %reshape.142, s32[1024]{0:T(1024)S(1)} %pad_clamp_fusion), kind=kCustom, calls=%fused_computation | custom fusion | bytes 2098176 | tf_op jit(solution)/shard_map/gather | solution.py:138
  369.2 2.9 fusion.5
  (63 shorter events, 17.1 us)
Async XLA Ops:
  7.2 274.9 %copy-start = (bf16[1,768,2048]{2,1,0:T(8,128)(2,1)S(1)}, bf16[1,768,2048]{2,1,0:T(8,128)(2,1)}, u32[]{:S(2)}) copy-start(bf16[1,768,2048]{2,1,0:T(8,128)(2,1)} %param.25) | copy-start | bytes 9437188
  7.2 193.4 %reduce-scatter.2.cloned.1.call-start = ((), (), s32[]{:S(2)}) async-start(), calls=%async_computation.3 | async-start | bytes 1179648 | tf_op jit(solution)/shard_map/reduce_scatter | solution.py:84
  12.7 6.5 %collective-permute-start = (bf16[4,128,128]{2,1,0:T(8,128)(2,1)}, bf16[4,128,128]{2,1,0:T(8,128)(2,1)S(1)}, u32[]{:S(2)}, u32[]{:S(2)}) collective-permute-start(bf16[4,128,128]{2,1,0:T(8,128)(2,1)} %get-tuple-element.96), channel_id=1, source_target_pairs={{0,8},{8,16},{16,24},{24,32},{32,40},{40,48},{48,56},{56,64},{64,7... | collective-permute-start | bytes 393224 | tf_op jit(solution)/shard_map/while/body/eval_jaxpr/ppermute | solution.py:10
  19.9 6.2 %collective-permute-start = (bf16[4,128,128]{2,1,0:T(8,128)(2,1)}, bf16[4,128,128]{2,1,0:T(8,128)(2,1)S(1)}, u32[]{:S(2)}, u32[]{:S(2)}) collective-permute-start(bf16[4,128,128]{2,1,0:T(8,128)(2,1)} %get-tuple-element.96), channel_id=1, source_target_pairs={{0,8},{8,16},{16,24},{24,32},{32,40},{40,48},{48,56},{56,64},{64,7... | collective-permute-start | bytes 393224 | tf_op jit(solution)/shard_map/while/body/eval_jaxpr/ppermute | solution.py:10
  26.9 5.9 %collective-permute-start = (bf16[4,128,128]{2,1,0:T(8,128)(2,1)}, bf16[4,128,128]{2,1,0:T(8,128)(2,1)S(1)}, u32[]{:S(2)}, u32[]{:S(2)}) collective-permute-start(bf16[4,128,128]{2,1,0:T(8,128)(2,1)} %get-tuple-element.96), channel_id=1, source_target_pairs={{0,8},{8,16},{16,24},{24,32},{32,40},{40,48},{48,56},{56,64},{64,7... | collective-permute-start | bytes 393224 | tf_op jit(solution)/shard_map/while/body/eval_jaxpr/ppermute | solution.py:10
  33.5 5.9 %collective-permute-start = (bf16[4,128,128]{2,1,0:T(8,128)(2,1)}, bf16[4,128,128]{2,1,0:T(8,128)(2,1)S(1)}, u32[]{:S(2)}, u32[]{:S(2)}) collective-permute-start(bf16[4,128,128]{2,1,0:T(8,128)(2,1)} %get-tuple-element.96), channel_id=1, source_target_pairs={{0,8},{8,16},{16,24},{24,32},{32,40},{40,48},{48,56},{56,64},{64,7... | collective-permute-start | bytes 393224 | tf_op jit(solution)/shard_map/while/body/eval_jaxpr/ppermute | solution.py:10
  40.2 5.9 %collective-permute-start = (bf16[4,128,128]{2,1,0:T(8,128)(2,1)}, bf16[4,128,128]{2,1,0:T(8,128)(2,1)S(1)}, u32[]{:S(2)}, u32[]{:S(2)}) collective-permute-start(bf16[4,128,128]{2,1,0:T(8,128)(2,1)} %get-tuple-element.96), channel_id=1, source_target_pairs={{0,8},{8,16},{16,24},{24,32},{32,40},{40,48},{48,56},{56,64},{64,7... | collective-permute-start | bytes 393224 | tf_op jit(solution)/shard_map/while/body/eval_jaxpr/ppermute | solution.py:10
  46.8 8.0 %collective-permute-start = (bf16[4,128,128]{2,1,0:T(8,128)(2,1)}, bf16[4,128,128]{2,1,0:T(8,128)(2,1)S(1)}, u32[]{:S(2)}, u32[]{:S(2)}) collective-permute-start(bf16[4,128,128]{2,1,0:T(8,128)(2,1)} %get-tuple-element.96), channel_id=1, source_target_pairs={{0,8},{8,16},{16,24},{24,32},{32,40},{40,48},{48,56},{56,64},{64,7... | collective-permute-start | bytes 393224 | tf_op jit(solution)/shard_map/while/body/eval_jaxpr/ppermute | solution.py:10
  55.5 8.0 %collective-permute-start = (bf16[4,128,128]{2,1,0:T(8,128)(2,1)}, bf16[4,128,128]{2,1,0:T(8,128)(2,1)S(1)}, u32[]{:S(2)}, u32[]{:S(2)}) collective-permute-start(bf16[4,128,128]{2,1,0:T(8,128)(2,1)} %get-tuple-element.96), channel_id=1, source_target_pairs={{0,8},{8,16},{16,24},{24,32},{32,40},{40,48},{48,56},{56,64},{64,7... | collective-permute-start | bytes 393224 | tf_op jit(solution)/shard_map/while/body/eval_jaxpr/ppermute | solution.py:10
  64.3 8.0 %collective-permute-start = (bf16[4,128,128]{2,1,0:T(8,128)(2,1)}, bf16[4,128,128]{2,1,0:T(8,128)(2,1)S(1)}, u32[]{:S(2)}, u32[]{:S(2)}) collective-permute-start(bf16[4,128,128]{2,1,0:T(8,128)(2,1)} %get-tuple-element.96), channel_id=1, source_target_pairs={{0,8},{8,16},{16,24},{24,32},{32,40},{40,48},{48,56},{56,64},{64,7... | collective-permute-start | bytes 393224 | tf_op jit(solution)/shard_map/while/body/eval_jaxpr/ppermute | solution.py:10
  73.0 8.7 %collective-permute-start = (bf16[4,128,128]{2,1,0:T(8,128)(2,1)}, bf16[4,128,128]{2,1,0:T(8,128)(2,1)S(1)}, u32[]{:S(2)}, u32[]{:S(2)}) collective-permute-start(bf16[4,128,128]{2,1,0:T(8,128)(2,1)} %get-tuple-element.96), channel_id=1, source_target_pairs={{0,8},{8,16},{16,24},{24,32},{32,40},{40,48},{48,56},{56,64},{64,7... | collective-permute-start | bytes 393224 | tf_op jit(solution)/shard_map/while/body/eval_jaxpr/ppermute | solution.py:10
  82.4 9.3 %collective-permute-start = (bf16[4,128,128]{2,1,0:T(8,128)(2,1)}, bf16[4,128,128]{2,1,0:T(8,128)(2,1)S(1)}, u32[]{:S(2)}, u32[]{:S(2)}) collective-permute-start(bf16[4,128,128]{2,1,0:T(8,128)(2,1)} %get-tuple-element.96), channel_id=1, source_target_pairs={{0,8},{8,16},{16,24},{24,32},{32,40},{40,48},{48,56},{56,64},{64,7... | collective-permute-start | bytes 393224 | tf_op jit(solution)/shard_map/while/body/eval_jaxpr/ppermute | solution.py:10
  92.4 8.4 %collective-permute-start = (bf16[4,128,128]{2,1,0:T(8,128)(2,1)}, bf16[4,128,128]{2,1,0:T(8,128)(2,1)S(1)}, u32[]{:S(2)}, u32[]{:S(2)}) collective-permute-start(bf16[4,128,128]{2,1,0:T(8,128)(2,1)} %get-tuple-element.96), channel_id=1, source_target_pairs={{0,8},{8,16},{16,24},{24,32},{32,40},{40,48},{48,56},{56,64},{64,7... | collective-permute-start | bytes 393224 | tf_op jit(solution)/shard_map/while/body/eval_jaxpr/ppermute | solution.py:10
  101.5 7.7 %collective-permute-start = (bf16[4,128,128]{2,1,0:T(8,128)(2,1)}, bf16[4,128,128]{2,1,0:T(8,128)(2,1)S(1)}, u32[]{:S(2)}, u32[]{:S(2)}) collective-permute-start(bf16[4,128,128]{2,1,0:T(8,128)(2,1)} %get-tuple-element.96), channel_id=1, source_target_pairs={{0,8},{8,16},{16,24},{24,32},{32,40},{40,48},{48,56},{56,64},{64,7... | collective-permute-start | bytes 393224 | tf_op jit(solution)/shard_map/while/body/eval_jaxpr/ppermute | solution.py:10
  109.9 8.3 %collective-permute-start = (bf16[4,128,128]{2,1,0:T(8,128)(2,1)}, bf16[4,128,128]{2,1,0:T(8,128)(2,1)S(1)}, u32[]{:S(2)}, u32[]{:S(2)}) collective-permute-start(bf16[4,128,128]{2,1,0:T(8,128)(2,1)} %get-tuple-element.96), channel_id=1, source_target_pairs={{0,8},{8,16},{16,24},{24,32},{32,40},{40,48},{48,56},{56,64},{64,7... | collective-permute-start | bytes 393224 | tf_op jit(solution)/shard_map/while/body/eval_jaxpr/ppermute | solution.py:10
  119.0 8.3 %collective-permute-start = (bf16[4,128,128]{2,1,0:T(8,128)(2,1)}, bf16[4,128,128]{2,1,0:T(8,128)(2,1)S(1)}, u32[]{:S(2)}, u32[]{:S(2)}) collective-permute-start(bf16[4,128,128]{2,1,0:T(8,128)(2,1)} %get-tuple-element.96), channel_id=1, source_target_pairs={{0,8},{8,16},{16,24},{24,32},{32,40},{40,48},{48,56},{56,64},{64,7... | collective-permute-start | bytes 393224 | tf_op jit(solution)/shard_map/while/body/eval_jaxpr/ppermute | solution.py:10
  128.1 8.0 %collective-permute-start = (bf16[4,128,128]{2,1,0:T(8,128)(2,1)}, bf16[4,128,128]{2,1,0:T(8,128)(2,1)S(1)}, u32[]{:S(2)}, u32[]{:S(2)}) collective-permute-start(bf16[4,128,128]{2,1,0:T(8,128)(2,1)} %get-tuple-element.96), channel_id=1, source_target_pairs={{0,8},{8,16},{16,24},{24,32},{32,40},{40,48},{48,56},{56,64},{64,7... | collective-permute-start | bytes 393224 | tf_op jit(solution)/shard_map/while/body/eval_jaxpr/ppermute | solution.py:10
  136.8 4.2 %copy-start.2 = (f32[256,512]{1,0:T(8,128)S(1)}, f32[256,512]{1,0:T(8,128)}, u32[]{:S(2)}) copy-start(f32[256,512]{1,0:T(8,128)} %param.16) | copy-start | bytes 1572868
  138.5 3.7 copy-start.8
  138.5 3.9 %copy-start.3 = (bf16[512,2048]{1,0:T(8,128)(2,1)S(1)}, bf16[512,2048]{1,0:T(8,128)(2,1)}, u32[]{:S(2)}) copy-start(bf16[512,2048]{1,0:T(8,128)(2,1)} %param.18) | copy-start | bytes 6291460
  142.3 1.9 copy-start.6
  142.4 58.2 %copy-start.4 = (bf16[32,2048]{1,0:T(8,128)(2,1)S(1)}, bf16[32,2048]{1,0:T(8,128)(2,1)}, u32[]{:S(2)}) copy-start(bf16[32,2048]{1,0:T(8,128)(2,1)} %param.19) | copy-start | bytes 393220
  142.4 59.3 %copy-start.5 = (f32[2048]{0:T(1024)S(1)}, f32[2048]{0:T(1024)}, u32[]{:S(2)}) copy-start(f32[2048]{0:T(1024)} %param.20) | copy-start | bytes 24580
  210.5 65.1 %copy-start.9 = (bf16[1,2048,768]{2,1,0:T(8,128)(2,1)S(1)}, bf16[1,2048,768]{2,1,0:T(8,128)(2,1)}, u32[]{:S(2)}) copy-start(bf16[1,2048,768]{2,1,0:T(8,128)(2,1)} %param.23) | copy-start | bytes 9437188
  273.6 2.0 copy-start.1
  299.5 6.0 %copy-start.7 = (f32[32,8]{0,1:T(8,128)S(1)}, f32[32,8]{0,1:T(8,128)}, u32[]{:S(2)}) copy-start(f32[32,8]{0,1:T(8,128)} %param.22) | copy-start | bytes 3076
  299.5 58.7 %all-to-all-start.1 = ((bf16[128,5,2048]{2,1,0:T(8,128)(2,1)}), bf16[128,5,2048]{2,1,0:T(8,128)(2,1)}, u32[]{:S(2)}, u32[]{:S(2)}) async-start(bf16[128,5,2048]{2,1,0:T(8,128)(2,1)} %copy.62), calls=%async_computation.2 | async-start | bytes 8388608 | tf_op jit(solution)/shard_map/all_to_all | solution.py:130
Sparse Core Ops, SparseCore 0:
  144.3 56.2 reduce-scatter.1
where the time goes:
time: 380 us; the launch traced here: 379 us
  waiting for transfers between devices  143 us (38%)
  starting transfers between devices  83.6 us (22%)
  blocking collectives  63.1 us (17%)
  matrix products  31.4 us (8%)
  local copies, waits for them, and re-layouts  26.9 us (7%)
  other arithmetic  16.3 us (4%)
  between operations  14.2 us (4%)
    ppermute x15, starting transfers between devices, passed_along(): return lax.ppermute(value, axis, pairs)  77.7 us
    all_to_all x1, blocking collectives, shards(): lax.all_to_all(outgoing, ('seq', 'head'), split_axis=0, concat_axis=0, ti...  63.1 us
    reduce_scatter x1, waiting for transfers between devices, shards(): lax.psum_scatter(jnp.dot(head_normed, out_weight, preferred_element_type=...  55.2 us
    all_to_all x1, waiting for transfers between devices, shards(): lax.all_to_all(produced.reshape(expert_count, slot_count, model_width), (...  52.6 us
    ppermute x15, waiting for transfers between devices, passed_along(): return lax.ppermute(value, axis, pairs)  35.4 us
    dot_general x1, matrix products, shards(): jnp.einsum('sxcf,xfd->sxcd', hidden_act, expert_down, preferred_element_t...  12 us
    add x15, other arithmetic, relay(): return (moving, summed + moving)  10.8 us
  transfers between devices with their start and end apart: 17, of which 17 were waited for; matrix products, arithmetic and copies ran while one was open for 0% of the time, Pallas kernels for 0%

commit v1 on v0

v1 whole, which is shorter than its diff:
```python
import functools
import jax
import jax.numpy as jnp
from jax import lax
from jax.experimental import pallas as pl
from jax.experimental.pallas import tpu as pltpu
from jax.sharding import PartitionSpec as P

EXACT = lax.Precision.HIGHEST
F32 = jnp.float32
BF16 = jnp.bfloat16
CAP = 5
VM = pl.BlockSpec(memory_space=pltpu.VMEM)
SM = pl.BlockSpec(memory_space=pltpu.SMEM)
HB = pl.BlockSpec(memory_space=pl.ANY)
MIB = 1 << 20


def params(mib):
    return pltpu.CompilerParams(vmem_limit_bytes=mib * MIB)


def cost(flops, moved):
    return pl.CostEstimate(flops=flops, bytes_accessed=moved, transcendentals=0)


def totals_kernel(heads, hd, k_ref, v_ref, out_ref):
    for h in range(heads):
        cols = slice(h * hd, (h + 1) * hd)
        out_ref[h] = lax.dot_general(
            k_ref[:, cols], v_ref[:, cols], (((0,), (0,)), ((), ())),
            precision=EXACT, preferred_element_type=F32,
        ).astype(BF16)


def within_kernel(heads, hd, q_ref, k_ref, v_ref, out_ref):
    rows = q_ref.shape[0]
    keep = lax.broadcasted_iota(jnp.int32, (rows, rows), 0) >= lax.broadcasted_iota(
        jnp.int32, (rows, rows), 1
    )
    for h in range(heads):
        cols = slice(h * hd, (h + 1) * hd)
        scores = lax.dot_general(
            q_ref[:, cols], k_ref[:, cols], (((1,), (1,)), ((), ())),
            precision=EXACT, preferred_element_type=F32,
        )
        scores = jnp.where(keep, scores, 0.0)
        out_ref[:, cols] = jnp.dot(
            scores, v_ref[:, cols], precision=EXACT, preferred_element_type=F32
        )


def project_kernel(
    heads, hd, parts, core_ref, q_ref, in_ref, base_ref, s1_ref, s2_ref, s3_ref, gain_ref, w_ref,
    mine_ref, theirs_ref, normed_ref,
):
    rows = q_ref.shape[0]
    step = rows // parts
    core = core_ref[0]
    gain = gain_ref[...]
    for h in range(heads):
        cols = slice(h * hd, (h + 1) * hd)
        state = (
            base_ref[h] + s1_ref[h].astype(F32) + s2_ref[h].astype(F32) + s3_ref[h].astype(F32)
        )
        att = in_ref[:, cols] + jnp.dot(
            q_ref[:, cols], state, precision=EXACT, preferred_element_type=F32
        )
        mean = jnp.mean(att * att, axis=-1, keepdims=True)
        norm = (att * lax.rsqrt(mean + 1e-06) * gain).astype(BF16)
        normed_ref[:, :, cols] = norm.reshape(parts, step, hd)
    weight = w_ref[...]
    half = parts // 2

    def rows_for(which):
        return jnp.concatenate([normed_ref[2 * z + which] for z in range(half)], axis=0)

    theirs = jnp.dot(rows_for(1 - core), weight, preferred_element_type=F32)
    theirs_ref[...] = theirs.astype(BF16).reshape(theirs_ref.shape)
    mine = jnp.dot(rows_for(core), weight, preferred_element_type=F32)
    mine_ref[...] = mine.reshape(mine_ref.shape)


def pair_kernel(zs, z_ref, mine_ref, got_ref, *outs):
    z = z_ref[0]
    for k in range(zs):
        block = lax.rem(z + k, zs)
        total = mine_ref[block] + got_ref[block].astype(F32)
        outs[k][...] = total.astype(outs[k].dtype)


def routing_kernel(cap, routed_ref, slots_ref, tokens_ref):
    routed = routed_ref[...]
    top, rows = routed.shape
    experts = tokens_ref.shape[1]
    expert = lax.broadcasted_iota(jnp.int32, (experts, rows), 0)
    named = [expert == routed[k : k + 1, :] for k in range(top)]
    member = jnp.zeros((experts, rows), F32)
    for hit in named:
        member = jnp.where(hit, 1.0, member)
    earlier_token = lax.broadcasted_iota(jnp.int32, (rows, rows), 0) < lax.broadcasted_iota(
        jnp.int32, (rows, rows), 1
    )
    earlier = jnp.dot(
        member, earlier_token.astype(F32), precision=EXACT, preferred_element_type=F32
    )
    for k in range(top):
        place = jnp.sum(jnp.where(named[k], earlier, 0.0), axis=0, keepdims=True)
        slots_ref[k : k + 1, :] = place.astype(jnp.int32)
    token = lax.broadcasted_iota(jnp.int32, (8, rows), 1).astype(F32)
    for s in range(cap):
        here = jnp.where((member > 0.5) & (earlier == float(s)), 1.0, 0.0)
        found = lax.dot_general(
            token, here, (((1,), (1,)), ((), ())), precision=EXACT, preferred_element_type=F32
        )
        tokens_ref[s : s + 1, :] = found[0:1, :].astype(jnp.int32)


def dispatch_kernel(
    cap, tokens_ref, o0_ref, o1_ref, o2_ref, o3_ref, res_ref, gain_ref, attn_ref, out_ref,
    wide_ref, tile_ref,
):
    rows, width = res_ref.shape
    per = width // 128
    step = pl.program_id(0)
    group = out_ref.shape[0]

    @pl.when(step == 0)
    def _():
        total = (
            o0_ref[...] + o1_ref[...].astype(F32) + o2_ref[...].astype(F32) + o3_ref[...].astype(F32)
        )
        attn = total.astype(BF16)
        attn_ref[...] = attn
        mixed = res_ref[...].astype(F32) + attn.astype(F32)
        mean = jnp.mean(mixed * mixed, axis=-1, keepdims=True)
        normed = mixed * lax.rsqrt(mean + 1e-06) * gain_ref[...]
        for j in range(per):
            wide_ref[pl.ds(j, rows, stride=per), :] = normed[:, j * 128 : (j + 1) * 128]
        tile_ref[...] = wide_ref[...].astype(BF16).reshape(rows, per, 128)

    for d in range(group):
        for s in range(cap):
            token = tokens_ref[s, step * group + d]
            out_ref[d, :, s * 128 : (s + 1) * 128] = tile_ref[token]


def expert_kernel(
    cap, in_hbm, gate_hbm, up_hbm, down_hbm, out_hbm,
    got, rows_ref, gate_ref, up_ref, down_ref, act_ref, turned, back,
    in_sem, gate_sem, up_sem, down_sem, out_sem,
):
    peers, per, _ = got.shape
    groups = peers // 16
    span = per * 16
    width = rows_ref.shape[1]
    hidden = act_ref.shape[1]
    tile = 256

    in_copies = [
        pltpu.make_async_copy(
            in_hbm.at[pl.ds(g * 16, 16)], got.at[pl.ds(g * 16, 16)], in_sem.at[g]
        )
        for g in range(groups)
    ]
    for copy in in_copies:
        copy.start()
    gate_copies, up_copies = [], []
    for n in range(hidden // tile):
        cols = pl.ds(n * tile, tile)
        gate_copies.append(
            pltpu.make_async_copy(gate_hbm.at[0, :, cols], gate_ref.at[:, cols], gate_sem.at[n])
        )
        up_copies.append(
            pltpu.make_async_copy(up_hbm.at[0, :, cols], up_ref.at[:, cols], up_sem.at[n])
        )
        gate_copies[-1].start()
        up_copies[-1].start()
    down_copies = []
    for n in range(width // 1024):
        cols = pl.ds(n * 1024, 1024)
        down_copies.append(
            pltpu.make_async_copy(down_hbm.at[0, :, cols], down_ref.at[:, cols], down_sem.at[n])
        )
        down_copies[-1].start()

    to = lax.broadcasted_iota(jnp.int32, (span, span), 0)
    fro = lax.broadcasted_iota(jnp.int32, (span, span), 1)
    swap = (fro == (to & 15) * 16 + (to >> 4)).astype(BF16)

    for g in range(groups):
        in_copies[g].wait()
        flat = got[g * 16 : (g + 1) * 16].reshape(span, cap * 128)
        moved = jnp.dot(swap, flat, preferred_element_type=F32).astype(BF16)
        for j in range(per):
            for s in range(cap):
                rows_ref[s * peers + g * 16 : s * peers + g * 16 + 16, j * 128 : (j + 1) * 128] = (
                    moved[j * 16 : (j + 1) * 16, s * 128 : (s + 1) * 128]
                )

    for n in range(hidden // tile):
        cols = slice(n * tile, (n + 1) * tile)
        gate_copies[n].wait()
        gate = jnp.dot(rows_ref[...], gate_ref[:, cols], preferred_element_type=F32)
        up_copies[n].wait()
        up = jnp.dot(rows_ref[...], up_ref[:, cols], preferred_element_type=F32)
        act_ref[:, cols] = (gate / (1.0 + jnp.exp(-gate)) * up).astype(BF16)

    for n in range(width // tile):
        if n % (1024 // tile) == 0:
            down_copies[n // (1024 // tile)].wait()
        made = jnp.dot(
            act_ref[...], down_ref[:, n * tile : (n + 1) * tile], preferred_element_type=F32
        ).astype(BF16)
        for jj in range(tile // 128):
            j = n * (tile // 128) + jj
            for g in range(groups):
                for s in range(cap):
                    turned[g, j * 16 : (j + 1) * 16, s * 128 : (s + 1) * 128] = made[
                        s * peers + g * 16 : s * peers + g * 16 + 16, jj * 128 : (jj + 1) * 128
                    ]

    out_copies = []
    for g in range(groups):
        back[g * 16 : (g + 1) * 16] = (
            jnp.dot(swap, turned[g], preferred_element_type=F32)
            .astype(BF16)
            .reshape(16, per, cap * 128)
        )
        out_copies.append(
            pltpu.make_async_copy(
                back.at[pl.ds(g * 16, 16)], out_hbm.at[pl.ds(g * 16, 16)], out_sem.at[g]
            )
        )
        out_copies[-1].start()
    for copy in out_copies:
        copy.wait()


def combine_kernel(routed_ref, slots_ref, weights_ref, back_ref, out_ref, wide_ref):
    top, rows = routed_ref.shape
    per = back_ref.shape[1]
    for t in range(rows):
        total = jnp.zeros((per, 128), F32)
        for k in range(top):
            slot = pl.multiple_of(slots_ref[k, t] * 128, 128)
            tile = back_ref[routed_ref[k, t], :, pl.ds(slot, 128)]
            total = total + weights_ref[k, t] * tile.astype(F32)
        wide_ref[t * per : (t + 1) * per, :] = total
    for j in range(per):
        out_ref[:, j * 128 : (j + 1) * 128] = wide_ref[pl.ds(j, rows, stride=per), :].astype(
            out_ref.dtype
        )


def shards(
    ys,
    attn_queries,
    attn_keys,
    attn_values,
    head_gain,
    out_weight,
    residual_in,
    norm_gain,
    routed_experts,
    gate_weights,
    expert_gate,
    expert_up,
    expert_down,
):
    rows, local = attn_queries.shape
    hd = head_gain.shape[0]
    heads = local // hd
    width = out_weight.shape[1]
    seqs = lax.axis_size("seq")
    parts = lax.axis_size("head")
    xs, zs = seqs // ys, parts // 2
    peers = seqs * parts
    hidden = expert_gate.shape[2]
    own_rows, top = routed_experts.shape
    per = width // 128
    cap = CAP
    y = lax.rem(lax.axis_index("seq"), ys)
    head = lax.axis_index("head")
    core = lax.rem(head, 2).reshape(1)
    z = (head // 2).reshape(1)

    state_shape = (heads, hd, hd)
    totals = pl.pallas_call(
        functools.partial(totals_kernel, heads, hd),
        out_shape=jax.ShapeDtypeStruct(state_shape, BF16),
        in_specs=[VM] * 2,
        out_specs=VM,
        compiler_params=params(16),
        name="totals",
    )(attn_keys, attn_values)

    from_y = [
        lax.ppermute(
            totals, "seq", [(i, (i // ys) * ys + (i + k) % ys) for i in range(seqs)]
        )
        for k in range(1, ys)
    ]
    within = pl.pallas_call(
        functools.partial(within_kernel, heads, hd),
        out_shape=jax.ShapeDtypeStruct((rows, local), F32),
        in_specs=[VM] * 3,
        out_specs=VM,
        compiler_params=params(24),
        cost_estimate=cost(12 * heads * rows * rows * hd * 2, 16 * rows * local),
        name="within",
    )(attn_queries, attn_keys, attn_values)
    routed = routed_experts.T
    slots, tokens = pl.pallas_call(
        functools.partial(routing_kernel, cap),
        out_shape=(
            jax.ShapeDtypeStruct((top, own_rows), jnp.int32),
            jax.ShapeDtypeStruct((8, peers), jnp.int32),
        ),
        in_specs=[VM],
        out_specs=(VM, VM),
        compiler_params=params(8),
        name="routing",
    )(routed)

    plane = totals.astype(F32)
    base = jnp.zeros(state_shape, F32)
    for k, part in enumerate(from_y, 1):
        wide = part.astype(F32)
        plane = plane + wide
        base = base + jnp.where(y >= k, wide, 0.0)
    plane = plane.astype(BF16)
    from_x = [
        lax.ppermute(plane, "seq", [(i, i + k * ys) for i in range(seqs - k * ys)])
        for k in range(1, xs)
    ]

    mine, theirs = pl.pallas_call(
        functools.partial(project_kernel, heads, hd, parts),
        out_shape=(
            jax.ShapeDtypeStruct((zs, own_rows, width), F32),
            jax.ShapeDtypeStruct((zs, own_rows, width), BF16),
        ),
        in_specs=[SM] + [VM] * 8,
        out_specs=(VM, VM),
        scratch_shapes=[pltpu.VMEM((parts, own_rows, local), BF16)],
        compiler_params=params(32),
        name="project",
    )(
        core, attn_queries, within, base, *from_x, head_gain.reshape(1, hd), out_weight
    )
    got = lax.ppermute(theirs, "head", [(i, i ^ 1) for i in range(parts)])
    blocks = pl.pallas_call(
        functools.partial(pair_kernel, zs),
        out_shape=tuple(
            jax.ShapeDtypeStruct((own_rows, width), F32 if k == 0 else BF16) for k in range(zs)
        ),
        in_specs=[SM, VM, VM],
        out_specs=(VM,) * zs,
        compiler_params=params(16),
        name="pair",
    )(z, mine, got)
    from_z = [
        lax.ppermute(blocks[k], "head", [(i, (i + 2 * k) % parts) for i in range(parts)])
        for k in range(1, zs)
    ]

    groups = 4
    whole = pl.BlockSpec((own_rows, width), lambda i: (0, 0))
    attn_out, outgoing = pl.pallas_call(
        functools.partial(dispatch_kernel, cap),
        out_shape=(
            jax.ShapeDtypeStruct((own_rows, width), BF16),
            jax.ShapeDtypeStruct((peers, per, cap * 128), BF16),
        ),
        grid=(groups,),
        in_specs=[SM] + [whole] * 5 + [pl.BlockSpec((1, width), lambda i: (0, 0))],
        out_specs=(whole, pl.BlockSpec((peers // groups, per, cap * 128), lambda i: (i, 0, 0))),
        scratch_shapes=[
            pltpu.VMEM((own_rows * per, 128), F32),
            pltpu.VMEM((own_rows, per, 128), BF16),
        ],
        compiler_params=params(16),
        name="dispatch",
    )(tokens, blocks[0], *from_z, residual_in, norm_gain.reshape(1, width))

    arrived = lax.all_to_all(outgoing, ("seq", "head"), split_axis=0, concat_axis=0, tiled=True)

    groups16 = peers // 16
    produced = pl.pallas_call(
        functools.partial(expert_kernel, cap),
        out_shape=jax.ShapeDtypeStruct((peers, per, cap * 128), BF16),
        in_specs=[HB] * 4,
        out_specs=HB,
        scratch_shapes=[
            pltpu.VMEM((peers, per, cap * 128), BF16),
            pltpu.VMEM((cap * peers, width), BF16),
            pltpu.VMEM((width, hidden), BF16),
            pltpu.VMEM((width, hidden), BF16),
            pltpu.VMEM((hidden, width), BF16),
            pltpu.VMEM((cap * peers, hidden), BF16),
            pltpu.VMEM((groups16, per * 16, cap * 128), BF16),
            pltpu.VMEM((peers, per, cap * 128), BF16),
            pltpu.SemaphoreType.DMA((groups16,)),
            pltpu.SemaphoreType.DMA((hidden // 256,)),
            pltpu.SemaphoreType.DMA((hidden // 256,)),
            pltpu.SemaphoreType.DMA((width // 1024,)),
            pltpu.SemaphoreType.DMA((groups16,)),
        ],
        compiler_params=params(48),
        name="expert",
    )(arrived, expert_gate, expert_up, expert_down)

    returned = lax.all_to_all(produced, ("seq", "head"), split_axis=0, concat_axis=0, tiled=True)

    moe_out = pl.pallas_call(
        combine_kernel,
        out_shape=jax.ShapeDtypeStruct((own_rows, width), BF16),
        in_specs=[SM, SM, SM, VM],
        out_specs=VM,
        scratch_shapes=[pltpu.VMEM((own_rows * per, 128), F32)],
        compiler_params=params(16),
        name="combine",
    )(routed, slots, gate_weights.T, returned)
    return (attn_out, moe_out)


def solution(mesh):
    return jax.shard_map(
        functools.partial(shards, 4),
        mesh=mesh,
        in_specs=(
            P("seq", "head"),
            P("seq", "head"),
            P("seq", "head"),
            P(),
            P("head", None),
            P(("seq", "head"), None),
            P(),
            P(("seq", "head"), None),
            P(("seq", "head"), None),
            P(("seq", "head"), None, None),
            P(("seq", "head"), None, None),
            P(("seq", "head"), None, None),
        ),
        out_specs=(P(("seq", "head"), None), P(("seq", "head"), None)),
        check_vma=False,
    )
```

time: 380 us -> 155 us (0.41)
  waiting for transfers between devices: 143 us -> 14.7 us
  starting transfers between devices: 83.6 us -> 19.7 us
  matrix products: 31.4 us -> 0 us
  Pallas kernels: 0 us -> 28.4 us
  blocking collectives: 63.1 us -> 80.5 us
  local copies, waits for them, and re-layouts: 26.9 us -> 10 us
  other arithmetic: 16.3 us -> 0.12 us
  between operations: 14.2 us -> 0.76 us
    ppermute x15 -> x10, starting transfers between devices: 77.7 us -> 19.7 us  [the longest x3 8.17 us: shards(): lax.ppermute(plane, 'seq', [(i, i + k * ys) for i in range(seqs - k * ys)])]
    reduce_scatter x1 -> x0, waiting for transfers between devices: 55.2 us -> none  [shards(): lax.psum_scatter(jnp.dot(head_normed, out_weight, preferred_element_type=...]
    all_to_all x1 -> x0, waiting for transfers between devices: 52.6 us -> none  [shards(): lax.all_to_all(produced.reshape(expert_count, slot_count, model_width), (...]
    all_to_all x0 -> x1, blocking collectives: none -> 40.2 us  [shards(): lax.all_to_all(produced, ('seq', 'head'), split_axis=0, concat_axis=0, ti...]
    dot_general x8 -> x0, matrix products: 31.4 us -> none  [the longest x1 12 us: shards(): jnp.einsum('sxcf,xfd->sxcd', hidden_act, expert_down, preferred_element_t...]
    pallas_call x0 -> x8, Pallas kernels: none -> 28.4 us  [the longest x1 17.9 us: shards(): pl.pallas_call(functools.partial(expert_kernel, cap), out_shape=jax.Shape...]
    all_to_all x1, blocking collectives: 63.1 us -> 40.3 us  [shards(): lax.all_to_all(outgoing, ('seq', 'head'), split_axis=0, concat_axis=0, ti...]
    ppermute x15 -> x10, waiting for transfers between devices: 35.4 us -> 14.7 us  [the longest x3 8.58 us: shards(): lax.ppermute(totals, 'seq', [(i, i // ys * ys + (i + k) % ys) for i in ra...]
  transfers between devices with their start and end apart: 17 -> 10, of which waited for: 17 -> 6; matrix products, arithmetic and copies ran while one was open for 0% -> 0% of each run, Pallas kernels for 0% -> 2%
where the time goes in v1:
time: 155 us; the launch traced here: 154 us
  blocking collectives  80.5 us (52%)
  Pallas kernels  28.4 us (18%)
  starting transfers between devices  19.7 us (13%)
  waiting for transfers between devices  14.7 us (9%)
  local copies, waits for them, and re-layouts  10 us (6%)
    all_to_all x1, blocking collectives, shards(): lax.all_to_all(outgoing, ('seq', 'head'), split_axis=0, concat_axis=0, ti...  40.3 us
    all_to_all x1, blocking collectives, shards(): lax.all_to_all(produced, ('seq', 'head'), split_axis=0, concat_axis=0, ti...  40.2 us
    pallas_call x1, Pallas kernels, shards(): pl.pallas_call(functools.partial(expert_kernel, cap), out_shape=jax.Shape...  17.9 us
    unnamed x36, local copies, waits for them, and re-layouts  10 us
    ppermute x3, waiting for transfers between devices, shards(): lax.ppermute(totals, 'seq', [(i, i // ys * ys + (i + k) % ys) for i in ra...  8.58 us
    ppermute x3, starting transfers between devices, shards(): lax.ppermute(plane, 'seq', [(i, i + k * ys) for i in range(seqs - k * ys)])  8.17 us
    ppermute x3, starting transfers between devices, shards(): lax.ppermute(blocks[k], 'head', [(i, (i + 2 * k) % parts) for i in range(...  5.74 us
    ppermute x3, starting transfers between devices, shards(): lax.ppermute(totals, 'seq', [(i, i // ys * ys + (i + k) % ys) for i in ra...  4.67 us
  transfers between devices with their start and end apart: 10, of which 6 were waited for; matrix products, arithmetic and copies ran while one was open for 0% of the time, Pallas kernels for 2%

profile of v1, /device:TPU:1, one launch (start us, length us, event | category | flops | bytes accessed | tf_op | source)
XLA Modules:
  0.0 154.3 jit_solution(10888637936161044637)
XLA Ops:
  0.6 0.0 copy-start
  0.6 0.0 copy-start.1
  0.7 1.2 copy-done.1
  1.8 1.0 copy-done.3
  2.9 0.6 totals.1
  3.5 3.6 %collective-permute-start.2 = (bf16[4,128,128]{2,1,0:T(8,128)(2,1)S(1)}, bf16[4,128,128]{2,1,0:T(8,128)(2,1)S(1)}, u32[]{:S(2)}, u32[]{:S(2)}) collective-permute-start(bf16[4,128,128]{2,1,0:T(8,128)(2,1)S(1)} %totals.1), channel_id=1, source_target_pairs={{0,24},{8,0},{16,8},{24,16},{32,56},{40,32},{48,40},{56,48},{64,88... | collective-permute-start | bytes 393224 | tf_op jit(solution)/shard_map/ppermute | solution.py:299
  7.1 0.3 collective-permute-start.1
  7.5 0.7 collective-permute-start
  8.2 4.0 %collective-permute-done.2 = bf16[4,128,128]{2,1,0:T(8,128)(2,1)S(1)} collective-permute-done((bf16[4,128,128]{2,1,0:T(8,128)(2,1)S(1)}, bf16[4,128,128]{2,1,0:T(8,128)(2,1)S(1)}, u32[]{:S(2)}, u32[]{:S(2)}) %collective-permute-start.2) | collective-permute-done | bytes 131104 | tf_op jit(solution)/shard_map/ppermute | solution.py:299
  12.1 0.4 collective-permute-done.1
  12.6 4.2 %collective-permute-done = bf16[4,128,128]{2,1,0:T(8,128)(2,1)S(1)} collective-permute-done((bf16[4,128,128]{2,1,0:T(8,128)(2,1)S(1)}, bf16[4,128,128]{2,1,0:T(8,128)(2,1)S(1)}, u32[]{:S(2)}, u32[]{:S(2)}) %collective-permute-start) | collective-permute-done | bytes 131104 | tf_op jit(solution)/shard_map/ppermute | solution.py:299
  16.8 0.1 fusion.2
  16.9 4.4 %collective-permute-start.5 = (bf16[4,128,128]{2,1,0:T(8,128)(2,1)S(1)}, bf16[4,128,128]{2,1,0:T(8,128)(2,1)S(1)}, u32[]{:S(2)}, u32[]{:S(2)}) collective-permute-start(bf16[4,128,128]{2,1,0:T(8,128)(2,1)S(1)} %get-tuple-element.22), channel_id=1, source_target_pairs={{0,96},{8,104},{16,112},{24,120},{1,97},{9,105},{17,113},{25,121},... | collective-permute-start | bytes 393224 | tf_op jit(solution)/shard_map/ppermute | solution.py:334
  21.3 1.3 collective-permute-start.4
  22.6 2.5 %collective-permute-start.3 = (bf16[4,128,128]{2,1,0:T(8,128)(2,1)S(1)}, bf16[4,128,128]{2,1,0:T(8,128)(2,1)S(1)}, u32[]{:S(2)}, u32[]{:S(2)}) collective-permute-start(bf16[4,128,128]{2,1,0:T(8,128)(2,1)S(1)} %get-tuple-element.22), channel_id=1, source_target_pairs={{0,32},{8,40},{16,48},{24,56},{32,64},{40,72},{48,80},{56,88},{64,... | collective-permute-start | bytes 393224 | tf_op jit(solution)/shard_map/ppermute | solution.py:334
  25.1 0.0 copy-start.2
  25.1 1.0 copy-done.2
  26.1 1.0 copy-done.4
  27.2 1.0 copy-done.5
  28.2 2.2 %within.1.in_ref = f32[256,512]{1,0:T(8,128)S(1)} custom-call(f32[256,512]{1,0:T(8,128)S(1)} %copy-done.5, f32[256,512]{1,0:T(8,128)S(1)} %copy-done.2, f32[256,512]{1,0:T(8,128)S(1)} %copy-done.4), custom_call_target="tpu_custom_call" | custom-call | flops 805306368 | bytes 2097152 | tf_op jit(solution)/shard_map/within/pallas_call | solution.py:304
  30.4 0.0 collective-permute-done.5.s3_ref
  30.5 0.0 copy-start.8
  30.5 0.6 copy-done.8
  31.1 0.0 collective-permute-done.4.s2_ref
  31.1 0.7 copy-done.10
  31.8 0.0 collective-permute-done.3.s1_ref
  31.8 0.7 copy-done.12
  32.4 0.0 copy-done.6
  32.4 0.9 copy-done.9
  33.3 0.9 copy-done.11
  34.2 0.9 copy-done.13
  35.2 2.0 %project.1 = (f32[4,32,2048]{2,1,0:T(8,128)S(1)}, bf16[4,32,2048]{2,1,0:T(8,128)(2,1)}) custom-call(s32[1]{0:T(128)} %bitcast.2.core_ref, f32[256,512]{1,0:T(8,128)S(1)} %copy-done.6, f32[256,512]{1,0:T(8,128)S(1)} %within.1.in_ref, f32[4,128,128]{2,1,0:T(8,128)S(1)} %get-tuple-element.23.base_ref, bf16[4,128,128]{2,1,0:T(8,128)(2,1)S(1)} %copy-done.13, ...), custom_call_target="tpu_custom_call" | custom-call | tf_op jit(solution)/shard_map/project/pallas_call | solution.py:338
  37.1 1.2 collective-permute-start.6
  38.3 1.7 %collective-permute-done.6.got_ref = bf16[4,32,2048]{2,1,0:T(8,128)(2,1)S(1)} collective-permute-done((bf16[4,32,2048]{2,1,0:T(8,128)(2,1)}, bf16[4,32,2048]{2,1,0:T(8,128)(2,1)S(1)}, u32[]{:S(2)}, u32[]{:S(2)}) %collective-permute-start.6) | collective-permute-done | bytes 524320 | tf_op jit(solution)/shard_map/ppermute | solution.py:352
  40.0 0.1 pair.1
  40.1 1.7 %collective-permute-start.7 = (bf16[32,2048]{1,0:T(8,128)(2,1)S(1)}, bf16[32,2048]{1,0:T(8,128)(2,1)S(1)}, u32[]{:S(2)}, u32[]{:S(2)}) collective-permute-start(bf16[32,2048]{1,0:T(8,128)(2,1)S(1)} %get-tuple-element.16), channel_id=1, source_target_pairs={{0,2},{1,3},{2,4},{3,5},{4,6},{5,7},{6,0},{7,1},{8,10},{9,11},{10,... | collective-permute-start | bytes 393224 | tf_op jit(solution)/shard_map/ppermute | solution.py:364
  41.8 3.3 %collective-permute-start.8 = (bf16[32,2048]{1,0:T(8,128)(2,1)S(1)}, bf16[32,2048]{1,0:T(8,128)(2,1)S(1)}, u32[]{:S(2)}, u32[]{:S(2)}) collective-permute-start(bf16[32,2048]{1,0:T(8,128)(2,1)S(1)} %get-tuple-element.17), channel_id=1, source_target_pairs={{0,4},{1,5},{2,6},{3,7},{4,0},{5,1},{6,2},{7,3},{8,12},{9,13},{10,... | collective-permute-start | bytes 393224 | tf_op jit(solution)/shard_map/ppermute | solution.py:364
  45.1 0.7 collective-permute-start.9
  45.9 1.0 routing.1
  46.8 0.7 collective-permute-done.7.o1_ref
  47.5 3.7 %collective-permute-done.8.o2_ref = bf16[32,2048]{1,0:T(8,128)(2,1)S(1)} collective-permute-done((bf16[32,2048]{1,0:T(8,128)(2,1)S(1)}, bf16[32,2048]{1,0:T(8,128)(2,1)S(1)}, u32[]{:S(2)}, u32[]{:S(2)}) %collective-permute-start.8) | collective-permute-done | bytes 131104 | tf_op jit(solution)/shard_map/ppermute | solution.py:364
  51.2 0.0 collective-permute-done.9.o3_ref
  51.2 2.6 %dispatch.1 = (bf16[32,2048]{1,0:T(8,128)(2,1)}, bf16[128,16,640]{2,1,0:T(8,128)(2,1)S(1)}) custom-call(s32[8,128]{1,0:T(8,128)S(1)} %get-tuple-element.12.tokens_ref, f32[32,2048]{1,0:T(8,128)S(1)} %get-tuple-element.15.o0_ref, bf16[32,2048]{1,0:T(8,128)(2,1)S(1)} %collective-permute-done.7.o1_ref, bf16[32,2048]{1,0:T(8,128)(2,1)S(1)} %collective-permute-done.8.o2_ref, ...), custom_call_target="tpu_custom_call" | custom-call | tf_op jit(solution)/shard_map/dispatch/pallas_call | solution.py:370
  53.8 40.3 %all_to_all.10.in_hbm = bf16[128,16,640]{2,1,0:T(8,128)(2,1)S(1)} all-to-all(bf16[128,16,640]{2,1,0:T(8,128)(2,1)S(1)} %get-tuple-element.21), channel_id=1, replica_groups=mesh['seq'=16,'head'=8] {'seq','head'}, dimensions={0} | all-to-all | bytes 5242880 | tf_op jit(solution)/shard_map/all_to_all | solution.py:387
  94.1 17.9 %expert.1 = bf16[128,16,640]{2,1,0:T(8,128)(2,1)S(1)} custom-call(bf16[128,16,640]{2,1,0:T(8,128)(2,1)S(1)} %all_to_all.10.in_hbm, bf16[1,2048,768]{2,1,0:T(8,128)(2,1)} %gate_hbm.1, bf16[1,2048,768]{2,1,0:T(8,128)(2,1)} %up_hbm.1, bf16[1,768,2048]{2,1,0:T(8,128)(2,1)} %down_hbm.1), custom_call_target="tpu_custom_call" | custom-call | tf_op jit(solution)/shard_map/expert/pallas_call | solution.py:390
  112.0 0.0 copy-start.16
  112.0 40.2 %all_to_all.11.back_ref = bf16[128,16,640]{2,1,0:T(8,128)(2,1)S(1)} all-to-all(bf16[128,16,640]{2,1,0:T(8,128)(2,1)S(1)} %expert.1), channel_id=1, replica_groups=mesh['seq'=16,'head'=8] {'seq','head'}, dimensions={0} | all-to-all | bytes 5242880 | tf_op jit(solution)/shard_map/all_to_all | solution.py:414
  152.3 2.1 %combine.1 = bf16[32,2048]{1,0:T(8,128)(2,1)} custom-call(s32[8,32]{1,0:T(8,128)S(1)} %bitcast.7, s32[8,32]{1,0:T(8,128)S(1)} %get-tuple-element.20.slots_ref, f32[8,32]{1,0:T(8,128)S(1)} %bitcast.9, bf16[128,16,640]{2,1,0:T(8,128)(2,1)S(1)} %all_to_all.11.back_ref), custom_call_target="tpu_custom_call" | custom-call | tf_op jit(solution)/shard_map/combine/pallas_call | solution.py:416
  (19 shorter events, 0.0 us)
Async XLA Ops:
  0.6 31.8 %copy-start = (bf16[512,2048]{1,0:T(8,128)(2,1)S(1)}, bf16[512,2048]{1,0:T(8,128)(2,1)}, u32[]{:S(2)}) copy-start(bf16[512,2048]{1,0:T(8,128)(2,1)} %w_ref.1) | copy-start | bytes 6291460
  0.6 1.2 copy-start.1
  1.8 1.0 copy-start.3
  2.9 29.6 %copy-start.17 = (f32[128]{0:T(128)S(1)}, f32[128]{0:T(128)}, u32[]{:S(2)}) copy-start(f32[128]{0:T(128)} %param.15) | copy-start | bytes 1540
  3.5 8.6 %collective-permute-start.2 = (bf16[4,128,128]{2,1,0:T(8,128)(2,1)S(1)}, bf16[4,128,128]{2,1,0:T(8,128)(2,1)S(1)}, u32[]{:S(2)}, u32[]{:S(2)}) collective-permute-start(bf16[4,128,128]{2,1,0:T(8,128)(2,1)S(1)} %totals.1), channel_id=1, source_target_pairs={{0,24},{8,0},{16,8},{24,16},{32,56},{40,32},{48,40},{56,48},{64,88... | collective-permute-start | bytes 393224 | tf_op jit(solution)/shard_map/ppermute | solution.py:299
  7.1 5.4 %collective-permute-start.1 = (bf16[4,128,128]{2,1,0:T(8,128)(2,1)S(1)}, bf16[4,128,128]{2,1,0:T(8,128)(2,1)S(1)}, u32[]{:S(2)}, u32[]{:S(2)}) collective-permute-start(bf16[4,128,128]{2,1,0:T(8,128)(2,1)S(1)} %totals.1), channel_id=1, source_target_pairs={{0,16},{8,24},{16,0},{24,8},{32,48},{40,56},{48,32},{56,40},{64,80... | collective-permute-start | bytes 393224 | tf_op jit(solution)/shard_map/ppermute | solution.py:299
  7.5 9.3 %collective-permute-start = (bf16[4,128,128]{2,1,0:T(8,128)(2,1)S(1)}, bf16[4,128,128]{2,1,0:T(8,128)(2,1)S(1)}, u32[]{:S(2)}, u32[]{:S(2)}) collective-permute-start(bf16[4,128,128]{2,1,0:T(8,128)(2,1)S(1)} %totals.1), channel_id=1, source_target_pairs={{0,8},{8,16},{16,24},{24,0},{32,40},{40,48},{48,56},{56,32},{64,72... | collective-permute-start | bytes 393224 | tf_op jit(solution)/shard_map/ppermute | solution.py:299
  16.9 13.6 %collective-permute-start.5 = (bf16[4,128,128]{2,1,0:T(8,128)(2,1)S(1)}, bf16[4,128,128]{2,1,0:T(8,128)(2,1)S(1)}, u32[]{:S(2)}, u32[]{:S(2)}) collective-permute-start(bf16[4,128,128]{2,1,0:T(8,128)(2,1)S(1)} %get-tuple-element.22), channel_id=1, source_target_pairs={{0,96},{8,104},{16,112},{24,120},{1,97},{9,105},{17,113},{25,121},... | collective-permute-start | bytes 393224 | tf_op jit(solution)/shard_map/ppermute | solution.py:334
  21.3 9.8 %collective-permute-start.4 = (bf16[4,128,128]{2,1,0:T(8,128)(2,1)S(1)}, bf16[4,128,128]{2,1,0:T(8,128)(2,1)S(1)}, u32[]{:S(2)}, u32[]{:S(2)}) collective-permute-start(bf16[4,128,128]{2,1,0:T(8,128)(2,1)S(1)} %get-tuple-element.22), channel_id=1, source_target_pairs={{0,64},{8,72},{16,80},{24,88},{32,96},{40,104},{48,112},{56,120},{... | collective-permute-start | bytes 393224 | tf_op jit(solution)/shard_map/ppermute | solution.py:334
  22.6 9.2 %collective-permute-start.3 = (bf16[4,128,128]{2,1,0:T(8,128)(2,1)S(1)}, bf16[4,128,128]{2,1,0:T(8,128)(2,1)S(1)}, u32[]{:S(2)}, u32[]{:S(2)}) collective-permute-start(bf16[4,128,128]{2,1,0:T(8,128)(2,1)S(1)} %get-tuple-element.22), channel_id=1, source_target_pairs={{0,32},{8,40},{16,48},{24,56},{32,64},{40,72},{48,80},{56,88},{64,... | collective-permute-start | bytes 393224 | tf_op jit(solution)/shard_map/ppermute | solution.py:334
  25.1 1.0 copy-start.2
  26.1 1.0 copy-start.4
  27.2 1.0 copy-start.5
  28.2 4.2 %copy-start.6 = (f32[256,512]{1,0:T(8,128)S(1)}, f32[256,512]{1,0:T(8,128)}, u32[]{:S(2)}) copy-start(f32[256,512]{1,0:T(8,128)} %q_ref.3) | copy-start | bytes 1572868
  30.5 0.7 copy-start.8
  31.1 0.7 copy-start.10
  31.8 0.7 copy-start.12
  32.4 0.9 copy-start.9
  33.3 0.9 copy-start.11
  34.2 0.9 copy-start.13
  35.1 10.7 %copy-start.14 = (s32[32,8]{0,1:T(8,128)S(1)}, s32[32,8]{0,1:T(8,128)}, u32[]{:S(2)}) copy-start(s32[32,8]{0,1:T(8,128)} %param.19) | copy-start | bytes 3076
  35.2 16.0 %copy-start.7 = (bf16[32,2048]{1,0:T(8,128)(2,1)S(1)}, bf16[32,2048]{1,0:T(8,128)(2,1)}, u32[]{:S(2)}) copy-start(bf16[32,2048]{1,0:T(8,128)(2,1)} %res_ref.1) | copy-start | bytes 393220
  35.2 16.0 %copy-start.15 = (f32[2048]{0:T(1024)S(1)}, f32[2048]{0:T(1024)}, u32[]{:S(2)}) copy-start(f32[2048]{0:T(1024)} %param.18) | copy-start | bytes 24580
  37.1 2.9 %collective-permute-start.6 = (bf16[4,32,2048]{2,1,0:T(8,128)(2,1)}, bf16[4,32,2048]{2,1,0:T(8,128)(2,1)S(1)}, u32[]{:S(2)}, u32[]{:S(2)}) collective-permute-start(bf16[4,32,2048]{2,1,0:T(8,128)(2,1)} %get-tuple-element.14), channel_id=1, source_target_pairs={{0,1},{1,0},{2,3},{3,2},{4,5},{5,4},{6,7},{7,6},{8,9},{9,8},{10,11... | collective-permute-start | bytes 1572872 | tf_op jit(solution)/shard_map/ppermute | solution.py:352
  40.1 7.4 %collective-permute-start.7 = (bf16[32,2048]{1,0:T(8,128)(2,1)S(1)}, bf16[32,2048]{1,0:T(8,128)(2,1)S(1)}, u32[]{:S(2)}, u32[]{:S(2)}) collective-permute-start(bf16[32,2048]{1,0:T(8,128)(2,1)S(1)} %get-tuple-element.16), channel_id=1, source_target_pairs={{0,2},{1,3},{2,4},{3,5},{4,6},{5,7},{6,0},{7,1},{8,10},{9,11},{10,... | collective-permute-start | bytes 393224 | tf_op jit(solution)/shard_map/ppermute | solution.py:364
  41.8 9.4 %collective-permute-start.8 = (bf16[32,2048]{1,0:T(8,128)(2,1)S(1)}, bf16[32,2048]{1,0:T(8,128)(2,1)S(1)}, u32[]{:S(2)}, u32[]{:S(2)}) collective-permute-start(bf16[32,2048]{1,0:T(8,128)(2,1)S(1)} %get-tuple-element.17), channel_id=1, source_target_pairs={{0,4},{1,5},{2,6},{3,7},{4,0},{5,1},{6,2},{7,3},{8,12},{9,13},{10,... | collective-permute-start | bytes 393224 | tf_op jit(solution)/shard_map/ppermute | solution.py:364
  45.1 6.1 %collective-permute-start.9 = (bf16[32,2048]{1,0:T(8,128)(2,1)S(1)}, bf16[32,2048]{1,0:T(8,128)(2,1)S(1)}, u32[]{:S(2)}, u32[]{:S(2)}) collective-permute-start(bf16[32,2048]{1,0:T(8,128)(2,1)S(1)} %get-tuple-element.18), channel_id=1, source_target_pairs={{0,6},{1,7},{2,0},{3,1},{4,2},{5,3},{6,4},{7,5},{8,14},{9,15},{10,... | collective-permute-start | bytes 393224 | tf_op jit(solution)/shard_map/ppermute | solution.py:364
  112.0 40.2 %copy-start.16 = (f32[32,8]{0,1:T(8,128)S(1)}, f32[32,8]{0,1:T(8,128)}, u32[]{:S(2)}) copy-start(f32[32,8]{0,1:T(8,128)} %param.20) | copy-start | bytes 3076

commit v2 on v1

v2 whole, which is shorter than its diff:
```python
import functools
import jax
import jax.numpy as jnp
from jax import lax
from jax.experimental import pallas as pl
from jax.experimental.pallas import tpu as pltpu
from jax.sharding import PartitionSpec as P

EXACT = lax.Precision.HIGHEST
F32 = jnp.float32
BF16 = jnp.bfloat16
CAP = 5
VM = pl.BlockSpec(memory_space=pltpu.VMEM)
SM = pl.BlockSpec(memory_space=pltpu.SMEM)
HB = pl.BlockSpec(memory_space=pltpu.HBM)
MIB = 1 << 20


def in_hbm(array):
    return pltpu.with_memory_space_constraint(array, pltpu.HBM)


def params(mib):
    return pltpu.CompilerParams(vmem_limit_bytes=mib * MIB)


def cost(flops, moved):
    return pl.CostEstimate(flops=flops, bytes_accessed=moved, transcendentals=0)


def totals_kernel(heads, hd, q_hbm, k_hbm, v_hbm, out_ref, q_ref, k_ref, v_ref, sems):
    copies = [
        pltpu.make_async_copy(src, dst, sems.at[n])
        for n, (src, dst) in enumerate([(k_hbm, k_ref), (v_hbm, v_ref), (q_hbm, q_ref)])
    ]
    for copy in copies:
        copy.start()
    copies[0].wait()
    copies[1].wait()
    for h in range(heads):
        cols = slice(h * hd, (h + 1) * hd)
        out_ref[h] = lax.dot_general(
            k_ref[:, cols], v_ref[:, cols], (((0,), (0,)), ((), ())),
            precision=EXACT, preferred_element_type=F32,
        ).astype(BF16)
    copies[2].wait()


def within_kernel(heads, hd, q_ref, k_ref, v_ref, out_ref):
    rows = q_ref.shape[0]
    keep = lax.broadcasted_iota(jnp.int32, (rows, rows), 0) >= lax.broadcasted_iota(
        jnp.int32, (rows, rows), 1
    )
    for h in range(heads):
        cols = slice(h * hd, (h + 1) * hd)
        scores = lax.dot_general(
            q_ref[:, cols], k_ref[:, cols], (((1,), (1,)), ((), ())),
            precision=EXACT, preferred_element_type=F32,
        )
        scores = jnp.where(keep, scores, 0.0)
        out_ref[:, cols] = jnp.dot(
            scores, v_ref[:, cols], precision=EXACT, preferred_element_type=F32
        )


def plane_kernel(own_ref, *refs):
    parts, plane_ref, base_ref = refs[:-3], refs[-2], refs[-1]
    y = lax.rem(lax.axis_index("seq"), len(parts) + 1)
    plane = own_ref[...].astype(F32)
    base = jnp.zeros(own_ref.shape, F32)
    for k, part in enumerate(parts, 1):
        wide = part[...].astype(F32)
        plane = plane + wide
        base = base + jnp.where(y >= k, wide, 0.0)
    plane_ref[...] = plane.astype(BF16)
    base_ref[...] = base


def project_kernel(
    heads, hd, parts, q_ref, in_ref, base_ref, s1_ref, s2_ref, s3_ref, gain_ref, w_ref,
    normed_ref, theirs_ref,
):
    rows = q_ref.shape[0]
    step = rows // parts
    core = lax.rem(lax.axis_index("head"), 2)
    gain = gain_ref[...]
    for h in range(heads):
        cols = slice(h * hd, (h + 1) * hd)
        state = (
            base_ref[h] + s1_ref[h].astype(F32) + s2_ref[h].astype(F32) + s3_ref[h].astype(F32)
        )
        att = in_ref[:, cols] + jnp.dot(
            q_ref[:, cols], state, precision=EXACT, preferred_element_type=F32
        )
        mean = jnp.mean(att * att, axis=-1, keepdims=True)
        norm = (att * lax.rsqrt(mean + 1e-06) * gain).astype(BF16)
        normed_ref[:, :, cols] = norm.reshape(parts, step, hd)
    theirs_ref[...] = projected(normed_ref, w_ref, 1 - core).astype(BF16)


def projected(normed_ref, w_ref, which):
    half = normed_ref.shape[0] // 2
    picked = jnp.concatenate([normed_ref[2 * z + which] for z in range(half)], axis=0)
    made = jnp.dot(picked, w_ref[...], preferred_element_type=F32)
    return made.reshape(half, normed_ref.shape[1], w_ref.shape[1])


def keep_kernel(normed_ref, w_ref, mine_ref):
    mine_ref[...] = projected(normed_ref, w_ref, lax.rem(lax.axis_index("head"), 2))


def pair_kernel(zs, mine_ref, got_ref, *outs):
    z = lax.div(lax.axis_index("head"), 2)
    for k in range(zs):
        block = lax.rem(z + k, zs)
        total = mine_ref[block] + got_ref[block].astype(F32)
        outs[k][...] = total.astype(outs[k].dtype)


def routing_kernel(cap, routed_ref, slots_ref, tokens_ref):
    routed = routed_ref[...]
    top, rows = routed.shape
    experts = tokens_ref.shape[1]
    expert = lax.broadcasted_iota(jnp.int32, (experts, rows), 0)
    named = [expert == routed[k : k + 1, :] for k in range(top)]
    member = jnp.zeros((experts, rows), F32)
    for hit in named:
        member = jnp.where(hit, 1.0, member)
    earlier_token = lax.broadcasted_iota(jnp.int32, (rows, rows), 0) < lax.broadcasted_iota(
        jnp.int32, (rows, rows), 1
    )
    earlier = jnp.dot(
        member, earlier_token.astype(F32), precision=EXACT, preferred_element_type=F32
    )
    for k in range(top):
        place = jnp.sum(jnp.where(named[k], earlier, 0.0), axis=0, keepdims=True)
        slots_ref[k : k + 1, :] = place.astype(jnp.int32)
    token = lax.broadcasted_iota(jnp.int32, (8, rows), 1).astype(F32)
    for s in range(cap):
        here = jnp.where((member > 0.5) & (earlier == float(s)), 1.0, 0.0)
        found = lax.dot_general(
            token, here, (((1,), (1,)), ((), ())), precision=EXACT, preferred_element_type=F32
        )
        tokens_ref[s : s + 1, :] = found[0:1, :].astype(jnp.int32)


def dispatch_kernel(
    cap, tokens_ref, o0_ref, o1_ref, o2_ref, o3_ref, res_ref, gain_ref, attn_ref, out_ref,
    wide_ref, tile_ref,
):
    rows, width = res_ref.shape
    per = width // 128
    total = (
        o0_ref[...] + o1_ref[...].astype(F32) + o2_ref[...].astype(F32) + o3_ref[...].astype(F32)
    )
    attn = total.astype(BF16)
    attn_ref[...] = attn
    mixed = res_ref[...].astype(F32) + attn.astype(F32)
    mean = jnp.mean(mixed * mixed, axis=-1, keepdims=True)
    normed = mixed * lax.rsqrt(mean + 1e-06) * gain_ref[...]
    for j in range(per):
        wide_ref[pl.ds(j, rows, stride=per), :] = normed[:, j * 128 : (j + 1) * 128]
    tile_ref[...] = wide_ref[...].astype(BF16).reshape(rows, per, 128)

    for d in range(out_ref.shape[0]):
        for s in range(cap):
            out_ref[d, :, s * 128 : (s + 1) * 128] = tile_ref[tokens_ref[s, d]]


def expert_kernel(
    cap, in_ref, gate_ref, up_ref, down_ref, out_ref, rows_ref, act_ref, turned
):
    peers, per, _ = in_ref.shape
    groups = peers // 16
    span = per * 16
    width = rows_ref.shape[1]
    hidden = act_ref.shape[1]
    tile = 256

    to = lax.broadcasted_iota(jnp.int32, (span, span), 0)
    fro = lax.broadcasted_iota(jnp.int32, (span, span), 1)
    swap = (fro == (to & 15) * 16 + (to >> 4)).astype(BF16)

    for g in range(groups):
        flat = in_ref[g * 16 : (g + 1) * 16].reshape(span, cap * 128)
        moved = jnp.dot(swap, flat, preferred_element_type=F32).astype(BF16)
        for j in range(per):
            for s in range(cap):
                rows_ref[s * peers + g * 16 : s * peers + g * 16 + 16, j * 128 : (j + 1) * 128] = (
                    moved[j * 16 : (j + 1) * 16, s * 128 : (s + 1) * 128]
                )

    for n in range(hidden // tile):
        cols = slice(n * tile, (n + 1) * tile)
        gate = jnp.dot(rows_ref[...], gate_ref[0, :, cols], preferred_element_type=F32)
        up = jnp.dot(rows_ref[...], up_ref[0, :, cols], preferred_element_type=F32)
        act_ref[:, cols] = (gate / (1.0 + jnp.exp(-gate)) * up).astype(BF16)

    for n in range(width // tile):
        made = jnp.dot(
            act_ref[...], down_ref[0, :, n * tile : (n + 1) * tile], preferred_element_type=F32
        ).astype(BF16)
        for jj in range(tile // 128):
            j = n * (tile // 128) + jj
            for g in range(groups):
                for s in range(cap):
                    turned[g, j * 16 : (j + 1) * 16, s * 128 : (s + 1) * 128] = made[
                        s * peers + g * 16 : s * peers + g * 16 + 16, jj * 128 : (jj + 1) * 128
                    ]

    for g in range(groups):
        out_ref[g * 16 : (g + 1) * 16] = (
            jnp.dot(swap, turned[g], preferred_element_type=F32)
            .astype(BF16)
            .reshape(16, per, cap * 128)
        )


def combine_kernel(routed_ref, slots_ref, weights_ref, back_ref, out_ref, wide_ref):
    top, rows = routed_ref.shape
    per = back_ref.shape[1]
    for t in range(rows):
        total = jnp.zeros((per, 128), F32)
        for k in range(top):
            slot = pl.multiple_of(slots_ref[k, t] * 128, 128)
            tile = back_ref[routed_ref[k, t], :, pl.ds(slot, 128)]
            total = total + weights_ref[k, t] * tile.astype(F32)
        wide_ref[t * per : (t + 1) * per, :] = total
    for j in range(per):
        out_ref[:, j * 128 : (j + 1) * 128] = wide_ref[pl.ds(j, rows, stride=per), :].astype(
            out_ref.dtype
        )


def shards(
    ys,
    attn_queries,
    attn_keys,
    attn_values,
    head_gain,
    out_weight,
    residual_in,
    norm_gain,
    routed_experts,
    gate_weights,
    expert_gate,
    expert_up,
    expert_down,
):
    rows, local = attn_queries.shape
    hd = head_gain.shape[0]
    heads = local // hd
    width = out_weight.shape[1]
    seqs = lax.axis_size("seq")
    parts = lax.axis_size("head")
    xs, zs = seqs // ys, parts // 2
    peers = seqs * parts
    hidden = expert_gate.shape[2]
    own_rows, top = routed_experts.shape
    per = width // 128
    cap = CAP

    state_shape = (heads, hd, hd)
    totals, queries, keys, values = pl.pallas_call(
        functools.partial(totals_kernel, heads, hd),
        out_shape=(jax.ShapeDtypeStruct(state_shape, BF16),)
        + (jax.ShapeDtypeStruct((rows, local), F32),) * 3,
        in_specs=[HB] * 3,
        out_specs=(VM,) * 4,
        scratch_shapes=[pltpu.SemaphoreType.DMA((3,))],
        compiler_params=params(2),
        name="totals",
    )(*(in_hbm(part) for part in (attn_queries, attn_keys, attn_values)))

    from_y = [
        lax.ppermute(
            totals, "seq", [(i, (i // ys) * ys + (i + k) % ys) for i in range(seqs)]
        )
        for k in range(1, ys)
    ]
    within = pl.pallas_call(
        functools.partial(within_kernel, heads, hd),
        out_shape=jax.ShapeDtypeStruct((rows, local), F32),
        in_specs=[VM] * 3,
        out_specs=VM,
        compiler_params=params(2),
        cost_estimate=cost(12 * heads * rows * rows * hd * 2, 16 * rows * local),
        name="within",
    )(queries, keys, values)
    routed = routed_experts.T
    slots, tokens = pl.pallas_call(
        functools.partial(routing_kernel, cap),
        out_shape=(
            jax.ShapeDtypeStruct((top, own_rows), jnp.int32),
            jax.ShapeDtypeStruct((8, peers), jnp.int32),
        ),
        in_specs=[VM],
        out_specs=(VM, VM),
        compiler_params=params(2),
        name="routing",
    )(routed)

    plane, base = pl.pallas_call(
        plane_kernel,
        out_shape=(
            jax.ShapeDtypeStruct(state_shape, BF16),
            jax.ShapeDtypeStruct(state_shape, F32),
        ),
        in_specs=[VM] * ys + [pl.BlockSpec(memory_space=pl.ANY)],
        out_specs=(VM, VM),
        compiler_params=params(2),
        name="plane",
    )(totals, *from_y, within)
    from_x = [
        lax.ppermute(plane, "seq", [(i, i + k * ys) for i in range(seqs - k * ys)])
        for k in range(1, xs)
    ]

    normed, theirs = pl.pallas_call(
        functools.partial(project_kernel, heads, hd, parts),
        out_shape=(
            jax.ShapeDtypeStruct((parts, own_rows, local), BF16),
            jax.ShapeDtypeStruct((zs, own_rows, width), BF16),
        ),
        in_specs=[VM] * 8,
        out_specs=(VM, VM),
        compiler_params=params(2),
        name="project",
    )(
        queries, within, base, *from_x, head_gain.reshape(1, hd), out_weight
    )
    got = lax.ppermute(theirs, "head", [(i, i ^ 1) for i in range(parts)])
    mine = pl.pallas_call(
        keep_kernel,
        out_shape=jax.ShapeDtypeStruct((zs, own_rows, width), F32),
        in_specs=[VM, VM],
        out_specs=VM,
        compiler_params=params(2),
        name="keep",
    )(normed, out_weight)
    blocks = pl.pallas_call(
        functools.partial(pair_kernel, zs),
        out_shape=tuple(
            jax.ShapeDtypeStruct((own_rows, width), F32 if k == 0 else BF16) for k in range(zs)
        ),
        in_specs=[VM, VM],
        out_specs=(VM,) * zs,
        compiler_params=params(2),
        name="pair",
    )(mine, got)
    from_z = [
        lax.ppermute(blocks[k], "head", [(i, (i + 2 * k) % parts) for i in range(parts)])
        for k in range(1, zs)
    ]

    attn_out, outgoing = pl.pallas_call(
        functools.partial(dispatch_kernel, cap),
        out_shape=(
            jax.ShapeDtypeStruct((own_rows, width), BF16),
            jax.ShapeDtypeStruct((peers, per, cap * 128), BF16),
        ),
        in_specs=[SM] + [VM] * 6,
        out_specs=(VM, VM),
        scratch_shapes=[
            pltpu.VMEM((own_rows * per, 128), F32),
            pltpu.VMEM((own_rows, per, 128), BF16),
        ],
        compiler_params=params(2),
        name="dispatch",
    )(tokens, blocks[0], *from_z, residual_in, norm_gain.reshape(1, width))

    arrived = lax.all_to_all(outgoing, ("seq", "head"), split_axis=0, concat_axis=0, tiled=True)

    produced = pl.pallas_call(
        functools.partial(expert_kernel, cap),
        out_shape=jax.ShapeDtypeStruct((peers, per, cap * 128), BF16),
        in_specs=[VM] * 4,
        out_specs=VM,
        scratch_shapes=[
            pltpu.VMEM((cap * peers, width), BF16),
            pltpu.VMEM((cap * peers, hidden), BF16),
            pltpu.VMEM((peers // 16, per * 16, cap * 128), BF16),
        ],
        compiler_params=params(8),
        name="expert",
    )(arrived, expert_gate, expert_up, expert_down)

    returned = lax.all_to_all(produced, ("seq", "head"), split_axis=0, concat_axis=0, tiled=True)

    moe_out = pl.pallas_call(
        combine_kernel,
        out_shape=jax.ShapeDtypeStruct((own_rows, width), BF16),
        in_specs=[SM, SM, SM, VM],
        out_specs=VM,
        scratch_shapes=[pltpu.VMEM((own_rows * per, 128), F32)],
        compiler_params=params(2),
        name="combine",
    )(routed, slots, gate_weights.T, returned)
    return (attn_out, moe_out)


def solution(mesh):
    return jax.shard_map(
        functools.partial(shards, 4),
        mesh=mesh,
        in_specs=(
            P("seq", "head"),
            P("seq", "head"),
            P("seq", "head"),
            P(),
            P("head", None),
            P(("seq", "head"), None),
            P(),
            P(("seq", "head"), None),
            P(("seq", "head"), None),
            P(("seq", "head"), None, None),
            P(("seq", "head"), None, None),
            P(("seq", "head"), None, None),
        ),
        out_specs=(P(("seq", "head"), None), P(("seq", "head"), None)),
        check_vma=False,
    )
```

time: 155 us -> 139 us (0.90)
  local copies, waits for them, and re-layouts: 10 us -> 0.04 us
  Pallas kernels: 28.4 us -> 19.3 us
  blocking collectives: 80.5 us -> 83.9 us
    unnamed x36 -> x18, local copies, waits for them, and re-layouts: 10 us -> 0.04 us
    pallas_call x1, Pallas kernels: 17.9 us -> 8.03 us  [shards(): pl.pallas_call(functools.partial(expert_kernel, cap), out_shape=jax.Shape...]
    all_to_all x1, blocking collectives: 40.3 us -> 43.7 us  [shards(): lax.all_to_all(outgoing, ('seq', 'head'), split_axis=0, concat_axis=0, ti...]
    ppermute x3, waiting for transfers between devices: 0.01 us -> 2.52 us  [shards(): lax.ppermute(plane, 'seq', [(i, i + k * ys) for i in range(seqs - k * ys)])]
    ppermute x3, waiting for transfers between devices: 8.58 us -> 6.35 us  [shards(): lax.ppermute(totals, 'seq', [(i, i // ys * ys + (i + k) % ys) for i in ra...]
    pallas_call x1 -> x3, Pallas kernels: 0.63 us -> 2.63 us  [the longest x1 2.01 us: shards(): pl.pallas_call(functools.partial(totals_kernel, heads, hd), out_shape=(ja...]
  transfers between devices with their start and end apart: 10 -> 10, of which waited for: 6 -> 7; matrix products, arithmetic and copies ran while one was open for 0% -> 0% of each run, Pallas kernels for 2% -> 3%
where the time goes in v2:
time: 139 us; the launch traced here: 138 us
  blocking collectives  83.9 us (60%)
  starting transfers between devices  20.1 us (14%)
  Pallas kernels  19.3 us (14%)
  waiting for transfers between devices  14.3 us (10%)
    all_to_all x1, blocking collectives, shards(): lax.all_to_all(outgoing, ('seq', 'head'), split_axis=0, concat_axis=0, ti...  43.7 us
    all_to_all x1, blocking collectives, shards(): lax.all_to_all(produced, ('seq', 'head'), split_axis=0, concat_axis=0, ti...  40.2 us
    ppermute x3, starting transfers between devices, shards(): lax.ppermute(plane, 'seq', [(i, i + k * ys) for i in range(seqs - k * ys)])  8.17 us
    pallas_call x1, Pallas kernels, shards(): pl.pallas_call(functools.partial(expert_kernel, cap), out_shape=jax.Shape...  8.03 us
    ppermute x3, waiting for transfers between devices, shards(): lax.ppermute(totals, 'seq', [(i, i // ys * ys + (i + k) % ys) for i in ra...  6.35 us
    ppermute x3, starting transfers between devices, shards(): lax.ppermute(blocks[k], 'head', [(i, (i + 2 * k) % parts) for i in range(...  5.75 us
    ppermute x3, starting transfers between devices, shards(): lax.ppermute(totals, 'seq', [(i, i // ys * ys + (i + k) % ys) for i in ra...  4.67 us
    ppermute x3, waiting for transfers between devices, shards(): lax.ppermute(blocks[k], 'head', [(i, (i + 2 * k) % parts) for i in range(...  4.37 us
  transfers between devices with their start and end apart: 10, of which 7 were waited for; matrix products, arithmetic and copies ran while one was open for 0% of the time, Pallas kernels for 3%

profile of v2, /device:TPU:1, one launch (start us, length us, event | category | flops | bytes accessed | tf_op | source)
XLA Modules:
  0.0 138.5 jit_solution(13180794257811214089)
XLA Ops:
  0.6 0.0 copy-start
  0.6 0.0 copy-start.8
  0.7 2.0 %totals.1 = (bf16[4,128,128]{2,1,0:T(8,128)(2,1)S(1)}, f32[256,512]{1,0:T(8,128)S(1)}, f32[256,512]{1,0:T(8,128)S(1)}, f32[256,512]{1,0:T(8,128)S(1)}) custom-call(f32[256,512]{1,0:T(8,128)} %q_hbm.1, f32[256,512]{1,0:T(8,128)} %k_hbm.1, f32[256,512]{1,0:T(8,128)} %v_hbm.1), custom_call_target="tpu_custom_call" | custom-call | tf_op jit(solution)/shard_map/totals/pallas_call | solution.py:264
  2.7 3.6 %collective-permute-start.2 = (bf16[4,128,128]{2,1,0:T(8,128)(2,1)S(1)}, bf16[4,128,128]{2,1,0:T(8,128)(2,1)S(1)}, u32[]{:S(2)}, u32[]{:S(2)}) collective-permute-start(bf16[4,128,128]{2,1,0:T(8,128)(2,1)S(1)} %get-tuple-element.22.own_ref), channel_id=1, source_target_pairs={{0,24},{8,0},{16,8},{24,16},{32,56},{40,32},{48,40},{56,48},{64,88... | collective-permute-start | bytes 393224 | tf_op jit(solution)/shard_map/ppermute | solution.py:276
  6.3 0.4 collective-permute-start.1
  6.7 0.7 collective-permute-start
  7.3 2.2 %within.1.refs_3_.in_ref = f32[256,512]{1,0:T(8,128)S(1)} custom-call(f32[256,512]{1,0:T(8,128)S(1)} %get-tuple-element.19.q_ref, f32[256,512]{1,0:T(8,128)S(1)} %get-tuple-element.20.k_ref, f32[256,512]{1,0:T(8,128)S(1)} %get-tuple-element.21.v_ref), custom_call_target="tpu_custom_call" | custom-call | flops 805306368 | bytes 2097152 | tf_op jit(solution)/shard_map/within/pallas_call | solution.py:281
  9.6 1.7 %collective-permute-done.2.refs_2_ = bf16[4,128,128]{2,1,0:T(8,128)(2,1)S(1)} collective-permute-done((bf16[4,128,128]{2,1,0:T(8,128)(2,1)S(1)}, bf16[4,128,128]{2,1,0:T(8,128)(2,1)S(1)}, u32[]{:S(2)}, u32[]{:S(2)}) %collective-permute-start.2) | collective-permute-done | bytes 131104 | tf_op jit(solution)/shard_map/ppermute | solution.py:276
  11.3 0.4 collective-permute-done.1.refs_1_
  11.7 4.2 %collective-permute-done.refs_0_ = bf16[4,128,128]{2,1,0:T(8,128)(2,1)S(1)} collective-permute-done((bf16[4,128,128]{2,1,0:T(8,128)(2,1)S(1)}, bf16[4,128,128]{2,1,0:T(8,128)(2,1)S(1)}, u32[]{:S(2)}, u32[]{:S(2)}) %collective-permute-start) | collective-permute-done | bytes 131104 | tf_op jit(solution)/shard_map/ppermute | solution.py:276
  15.9 0.1 plane.1
  16.1 4.4 %collective-permute-start.5 = (bf16[4,128,128]{2,1,0:T(8,128)(2,1)S(1)}, bf16[4,128,128]{2,1,0:T(8,128)(2,1)S(1)}, u32[]{:S(2)}, u32[]{:S(2)}) collective-permute-start(bf16[4,128,128]{2,1,0:T(8,128)(2,1)S(1)} %get-tuple-element.24), channel_id=1, source_target_pairs={{0,96},{8,104},{16,112},{24,120},{1,97},{9,105},{17,113},{25,121},... | collective-permute-start | bytes 393224 | tf_op jit(solution)/shard_map/ppermute | solution.py:315
  20.5 1.3 collective-permute-start.4
  21.8 2.5 %collective-permute-start.3 = (bf16[4,128,128]{2,1,0:T(8,128)(2,1)S(1)}, bf16[4,128,128]{2,1,0:T(8,128)(2,1)S(1)}, u32[]{:S(2)}, u32[]{:S(2)}) collective-permute-start(bf16[4,128,128]{2,1,0:T(8,128)(2,1)S(1)} %get-tuple-element.24), channel_id=1, source_target_pairs={{0,32},{8,40},{16,48},{24,56},{32,64},{40,72},{48,80},{56,88},{64,... | collective-permute-start | bytes 393224 | tf_op jit(solution)/shard_map/ppermute | solution.py:315
  24.3 0.0 collective-permute-done.5.s3_ref
  24.3 0.0 collective-permute-done.4.s2_ref
  24.3 2.5 %collective-permute-done.3.s1_ref = bf16[4,128,128]{2,1,0:T(8,128)(2,1)S(1)} collective-permute-done((bf16[4,128,128]{2,1,0:T(8,128)(2,1)S(1)}, bf16[4,128,128]{2,1,0:T(8,128)(2,1)S(1)}, u32[]{:S(2)}, u32[]{:S(2)}) %collective-permute-start.3) | collective-permute-done | bytes 131104 | tf_op jit(solution)/shard_map/ppermute | solution.py:315
  26.8 0.0 copy-done
  26.8 0.0 copy-done.8
  26.8 1.1 project.1
  27.9 0.0 copy-start.5
  27.9 0.0 copy-start.4
  27.9 0.0 copy-start.6
  28.0 1.5 %collective-permute-start.6 = (bf16[4,32,2048]{2,1,0:T(8,128)(2,1)S(1)}, bf16[4,32,2048]{2,1,0:T(8,128)(2,1)S(1)}, u32[]{:S(2)}, u32[]{:S(2)}) collective-permute-start(bf16[4,32,2048]{2,1,0:T(8,128)(2,1)S(1)} %get-tuple-element.26), channel_id=1, source_target_pairs={{0,1},{1,0},{2,3},{3,2},{4,5},{5,4},{6,7},{7,6},{8,9},{9,8},{10,11... | collective-permute-start | bytes 1572872 | tf_op jit(solution)/shard_map/ppermute | solution.py:332
  29.5 0.0 copy-start.3
  29.5 0.5 keep.1.mine_ref
  30.0 1.1 collective-permute-done.6.got_ref
  31.0 0.1 pair.1
  31.1 1.7 %collective-permute-start.7 = (bf16[32,2048]{1,0:T(8,128)(2,1)S(1)}, bf16[32,2048]{1,0:T(8,128)(2,1)S(1)}, u32[]{:S(2)}, u32[]{:S(2)}) collective-permute-start(bf16[32,2048]{1,0:T(8,128)(2,1)S(1)} %get-tuple-element.28), channel_id=1, source_target_pairs={{0,2},{1,3},{2,4},{3,5},{4,6},{5,7},{6,0},{7,1},{8,10},{9,11},{10,... | collective-permute-start | bytes 393224 | tf_op jit(solution)/shard_map/ppermute | solution.py:352
  32.9 3.3 %collective-permute-start.8 = (bf16[32,2048]{1,0:T(8,128)(2,1)S(1)}, bf16[32,2048]{1,0:T(8,128)(2,1)S(1)}, u32[]{:S(2)}, u32[]{:S(2)}) collective-permute-start(bf16[32,2048]{1,0:T(8,128)(2,1)S(1)} %get-tuple-element.29), channel_id=1, source_target_pairs={{0,4},{1,5},{2,6},{3,7},{4,0},{5,1},{6,2},{7,3},{8,12},{9,13},{10,... | collective-permute-start | bytes 393224 | tf_op jit(solution)/shard_map/ppermute | solution.py:352
  36.2 0.7 collective-permute-start.9
  36.9 0.0 copy-done.5
  36.9 1.0 routing.1
  37.8 0.7 collective-permute-done.7.o1_ref
  38.5 3.7 %collective-permute-done.8.o2_ref = bf16[32,2048]{1,0:T(8,128)(2,1)S(1)} collective-permute-done((bf16[32,2048]{1,0:T(8,128)(2,1)S(1)}, bf16[32,2048]{1,0:T(8,128)(2,1)S(1)}, u32[]{:S(2)}, u32[]{:S(2)}) %collective-permute-start.8) | collective-permute-done | bytes 131104 | tf_op jit(solution)/shard_map/ppermute | solution.py:352
  42.2 0.0 collective-permute-done.9.o3_ref
  42.2 0.0 copy-done.4
  42.2 0.0 copy-done.6
  42.2 2.2 %dispatch.1 = (bf16[32,2048]{1,0:T(8,128)(2,1)}, bf16[128,16,640]{2,1,0:T(8,128)(2,1)S(1)}) custom-call(s32[8,128]{1,0:T(8,128)S(1)} %get-tuple-element.18.tokens_ref, f32[32,2048]{1,0:T(8,128)S(1)} %get-tuple-element.27.o0_ref, bf16[32,2048]{1,0:T(8,128)(2,1)S(1)} %collective-permute-done.7.o1_ref, bf16[32,2048]{1,0:T(8,128)(2,1)S(1)} %collective-permute-done.8.o2_ref, ...), custom_call_target="tpu_custom_call" | custom-call | tf_op jit(solution)/shard_map/dispatch/pallas_call | solution.py:356
  44.5 43.7 %all_to_all.10.in_ref = bf16[128,16,640]{2,1,0:T(8,128)(2,1)S(1)} all-to-all(bf16[128,16,640]{2,1,0:T(8,128)(2,1)S(1)} %get-tuple-element.33), channel_id=1, replica_groups=mesh['seq'=16,'head'=8] {'seq','head'}, dimensions={0} | all-to-all | bytes 5242880 | tf_op jit(solution)/shard_map/all_to_all | solution.py:372
  88.1 0.0 copy-done.3
  88.1 0.0 copy-done.2
  88.1 0.0 copy-done.1
  88.1 8.0 %expert.1 = bf16[128,16,640]{2,1,0:T(8,128)(2,1)S(1)} custom-call(bf16[128,16,640]{2,1,0:T(8,128)(2,1)S(1)} %all_to_all.10.in_ref, bf16[1,2048,768]{2,1,0:T(8,128)(2,1)S(1)} %copy-done.1, bf16[1,2048,768]{2,1,0:T(8,128)(2,1)S(1)} %copy-done.2, bf16[1,768,2048]{2,1,0:T(8,128)(2,1)S(1)} %copy-done.3), custom_call_target="tpu_custom_call" | custom-call | tf_op jit(solution)/shard_map/expert/pallas_call | solution.py:374
  96.2 0.0 copy-start.7
  96.2 40.2 %all_to_all.11.back_ref = bf16[128,16,640]{2,1,0:T(8,128)(2,1)S(1)} all-to-all(bf16[128,16,640]{2,1,0:T(8,128)(2,1)S(1)} %expert.1), channel_id=1, replica_groups=mesh['seq'=16,'head'=8] {'seq','head'}, dimensions={0} | all-to-all | bytes 5242880 | tf_op jit(solution)/shard_map/all_to_all | solution.py:388
  136.4 0.0 copy-done.7
  136.4 2.1 %combine.1 = bf16[32,2048]{1,0:T(8,128)(2,1)} custom-call(s32[8,32]{1,0:T(8,128)S(1)} %bitcast.5, s32[8,32]{1,0:T(8,128)S(1)} %get-tuple-element.32.slots_ref, f32[8,32]{1,0:T(8,128)S(1)} %bitcast.7, bf16[128,16,640]{2,1,0:T(8,128)(2,1)S(1)} %all_to_all.11.back_ref), custom_call_target="tpu_custom_call" | custom-call | tf_op jit(solution)/shard_map/combine/pallas_call | solution.py:390
  (2 shorter events, 0.0 us)
Async XLA Ops:
  0.6 26.2 %copy-start = (bf16[512,2048]{1,0:T(8,128)(2,1)S(1)}, bf16[512,2048]{1,0:T(8,128)(2,1)}, u32[]{:S(2)}) copy-start(bf16[512,2048]{1,0:T(8,128)(2,1)} %w_ref.3) | copy-start | bytes 6291460
  0.6 26.2 %copy-start.8 = (f32[128]{0:T(128)S(1)}, f32[128]{0:T(128)}, u32[]{:S(2)}) copy-start(f32[128]{0:T(128)} %param.15) | copy-start | bytes 1540
  2.7 8.6 %collective-permute-start.2 = (bf16[4,128,128]{2,1,0:T(8,128)(2,1)S(1)}, bf16[4,128,128]{2,1,0:T(8,128)(2,1)S(1)}, u32[]{:S(2)}, u32[]{:S(2)}) collective-permute-start(bf16[4,128,128]{2,1,0:T(8,128)(2,1)S(1)} %get-tuple-element.22.own_ref), channel_id=1, source_target_pairs={{0,24},{8,0},{16,8},{24,16},{32,56},{40,32},{48,40},{56,48},{64,88... | collective-permute-start | bytes 393224 | tf_op jit(solution)/shard_map/ppermute | solution.py:276
  6.3 5.4 %collective-permute-start.1 = (bf16[4,128,128]{2,1,0:T(8,128)(2,1)S(1)}, bf16[4,128,128]{2,1,0:T(8,128)(2,1)S(1)}, u32[]{:S(2)}, u32[]{:S(2)}) collective-permute-start(bf16[4,128,128]{2,1,0:T(8,128)(2,1)S(1)} %get-tuple-element.22.own_ref), channel_id=1, source_target_pairs={{0,16},{8,24},{16,0},{24,8},{32,48},{40,56},{48,32},{56,40},{64,80... | collective-permute-start | bytes 393224 | tf_op jit(solution)/shard_map/ppermute | solution.py:276
  6.7 9.3 %collective-permute-start = (bf16[4,128,128]{2,1,0:T(8,128)(2,1)S(1)}, bf16[4,128,128]{2,1,0:T(8,128)(2,1)S(1)}, u32[]{:S(2)}, u32[]{:S(2)}) collective-permute-start(bf16[4,128,128]{2,1,0:T(8,128)(2,1)S(1)} %get-tuple-element.22.own_ref), channel_id=1, source_target_pairs={{0,8},{8,16},{16,24},{24,0},{32,40},{40,48},{48,56},{56,32},{64,72... | collective-permute-start | bytes 393224 | tf_op jit(solution)/shard_map/ppermute | solution.py:276
  16.1 8.2 %collective-permute-start.5 = (bf16[4,128,128]{2,1,0:T(8,128)(2,1)S(1)}, bf16[4,128,128]{2,1,0:T(8,128)(2,1)S(1)}, u32[]{:S(2)}, u32[]{:S(2)}) collective-permute-start(bf16[4,128,128]{2,1,0:T(8,128)(2,1)S(1)} %get-tuple-element.24), channel_id=1, source_target_pairs={{0,96},{8,104},{16,112},{24,120},{1,97},{9,105},{17,113},{25,121},... | collective-permute-start | bytes 393224 | tf_op jit(solution)/shard_map/ppermute | solution.py:315
  20.5 3.8 %collective-permute-start.4 = (bf16[4,128,128]{2,1,0:T(8,128)(2,1)S(1)}, bf16[4,128,128]{2,1,0:T(8,128)(2,1)S(1)}, u32[]{:S(2)}, u32[]{:S(2)}) collective-permute-start(bf16[4,128,128]{2,1,0:T(8,128)(2,1)S(1)} %get-tuple-element.24), channel_id=1, source_target_pairs={{0,64},{8,72},{16,80},{24,88},{32,96},{40,104},{48,112},{56,120},{... | collective-permute-start | bytes 393224 | tf_op jit(solution)/shard_map/ppermute | solution.py:315
  21.8 5.0 %collective-permute-start.3 = (bf16[4,128,128]{2,1,0:T(8,128)(2,1)S(1)}, bf16[4,128,128]{2,1,0:T(8,128)(2,1)S(1)}, u32[]{:S(2)}, u32[]{:S(2)}) collective-permute-start(bf16[4,128,128]{2,1,0:T(8,128)(2,1)S(1)} %get-tuple-element.24), channel_id=1, source_target_pairs={{0,32},{8,40},{16,48},{24,56},{32,64},{40,72},{48,80},{56,88},{64,... | collective-permute-start | bytes 393224 | tf_op jit(solution)/shard_map/ppermute | solution.py:315
  27.9 9.0 %copy-start.5 = (s32[32,8]{0,1:T(8,128)S(1)}, s32[32,8]{0,1:T(8,128)}, u32[]{:S(2)}) copy-start(s32[32,8]{0,1:T(8,128)} %param.19) | copy-start | bytes 3076
  27.9 14.3 %copy-start.4 = (bf16[32,2048]{1,0:T(8,128)(2,1)S(1)}, bf16[32,2048]{1,0:T(8,128)(2,1)}, u32[]{:S(2)}) copy-start(bf16[32,2048]{1,0:T(8,128)(2,1)} %res_ref.1) | copy-start | bytes 393220
  27.9 14.3 %copy-start.6 = (f32[2048]{0:T(1024)S(1)}, f32[2048]{0:T(1024)}, u32[]{:S(2)}) copy-start(f32[2048]{0:T(1024)} %param.18) | copy-start | bytes 24580
  28.0 3.1 %collective-permute-start.6 = (bf16[4,32,2048]{2,1,0:T(8,128)(2,1)S(1)}, bf16[4,32,2048]{2,1,0:T(8,128)(2,1)S(1)}, u32[]{:S(2)}, u32[]{:S(2)}) collective-permute-start(bf16[4,32,2048]{2,1,0:T(8,128)(2,1)S(1)} %get-tuple-element.26), channel_id=1, source_target_pairs={{0,1},{1,0},{2,3},{3,2},{4,5},{5,4},{6,7},{7,6},{8,9},{9,8},{10,11... | collective-permute-start | bytes 1572872 | tf_op jit(solution)/shard_map/ppermute | solution.py:332
  29.5 58.6 %copy-start.3 = (bf16[1,768,2048]{2,1,0:T(8,128)(2,1)S(1)}, bf16[1,768,2048]{2,1,0:T(8,128)(2,1)}, u32[]{:S(2)}) copy-start(bf16[1,768,2048]{2,1,0:T(8,128)(2,1)} %down_ref.1) | copy-start | bytes 9437188
  31.0 57.1 %copy-start.2 = (bf16[1,2048,768]{2,1,0:T(8,128)(2,1)S(1)}, bf16[1,2048,768]{2,1,0:T(8,128)(2,1)}, u32[]{:S(2)}) copy-start(bf16[1,2048,768]{2,1,0:T(8,128)(2,1)} %up_ref.1) | copy-start | bytes 9437188
  31.1 7.4 %collective-permute-start.7 = (bf16[32,2048]{1,0:T(8,128)(2,1)S(1)}, bf16[32,2048]{1,0:T(8,128)(2,1)S(1)}, u32[]{:S(2)}, u32[]{:S(2)}) collective-permute-start(bf16[32,2048]{1,0:T(8,128)(2,1)S(1)} %get-tuple-element.28), channel_id=1, source_target_pairs={{0,2},{1,3},{2,4},{3,5},{4,6},{5,7},{6,0},{7,1},{8,10},{9,11},{10,... | collective-permute-start | bytes 393224 | tf_op jit(solution)/shard_map/ppermute | solution.py:352
  32.9 9.4 %collective-permute-start.8 = (bf16[32,2048]{1,0:T(8,128)(2,1)S(1)}, bf16[32,2048]{1,0:T(8,128)(2,1)S(1)}, u32[]{:S(2)}, u32[]{:S(2)}) collective-permute-start(bf16[32,2048]{1,0:T(8,128)(2,1)S(1)} %get-tuple-element.29), channel_id=1, source_target_pairs={{0,4},{1,5},{2,6},{3,7},{4,0},{5,1},{6,2},{7,3},{8,12},{9,13},{10,... | collective-permute-start | bytes 393224 | tf_op jit(solution)/shard_map/ppermute | solution.py:352
  36.2 6.1 %collective-permute-start.9 = (bf16[32,2048]{1,0:T(8,128)(2,1)S(1)}, bf16[32,2048]{1,0:T(8,128)(2,1)S(1)}, u32[]{:S(2)}, u32[]{:S(2)}) collective-permute-start(bf16[32,2048]{1,0:T(8,128)(2,1)S(1)} %get-tuple-element.30), channel_id=1, source_target_pairs={{0,6},{1,7},{2,0},{3,1},{4,2},{5,3},{6,4},{7,5},{8,14},{9,15},{10,... | collective-permute-start | bytes 393224 | tf_op jit(solution)/shard_map/ppermute | solution.py:352
  44.5 43.7 %copy-start.1 = (bf16[1,2048,768]{2,1,0:T(8,128)(2,1)S(1)}, bf16[1,2048,768]{2,1,0:T(8,128)(2,1)}, u32[]{:S(2)}) copy-start(bf16[1,2048,768]{2,1,0:T(8,128)(2,1)} %gate_ref.1) | copy-start | bytes 9437188
  96.2 40.2 %copy-start.7 = (f32[32,8]{0,1:T(8,128)S(1)}, f32[32,8]{0,1:T(8,128)}, u32[]{:S(2)}) copy-start(f32[32,8]{0,1:T(8,128)} %param.20) | copy-start | bytes 3076

commit v3 on v2

--- a/solution.py
+++ b/solution.py
@@ -71,24 +71,25 @@
     for k, part in enumerate(parts, 1):
         wide = part[...].astype(F32)
         plane = plane + wide
-        base = base + jnp.where(y >= k, wide, 0.0)
+        base = base + jnp.where((y ^ k) < y, wide, 0.0)
     plane_ref[...] = plane.astype(BF16)
     base_ref[...] = base
 
 
 def project_kernel(
-    heads, hd, parts, q_ref, in_ref, base_ref, s1_ref, s2_ref, s3_ref, gain_ref, w_ref,
+    heads, hd, parts, ys, q_ref, in_ref, base_ref, s1_ref, s2_ref, s3_ref, gain_ref, w_ref,
     normed_ref, theirs_ref,
 ):
     rows = q_ref.shape[0]
     step = rows // parts
     core = lax.rem(lax.axis_index("head"), 2)
+    x = lax.div(lax.axis_index("seq"), ys)
     gain = gain_ref[...]
     for h in range(heads):
         cols = slice(h * hd, (h + 1) * hd)
-        state = (
-            base_ref[h] + s1_ref[h].astype(F32) + s2_ref[h].astype(F32) + s3_ref[h].astype(F32)
-        )
+        state = base_ref[h]
+        for k, part in enumerate((s1_ref, s2_ref, s3_ref), 1):
+            state = state + jnp.where((x ^ k) < x, part[h].astype(F32), 0.0)
         att = in_ref[:, cols] + jnp.dot(
             q_ref[:, cols], state, precision=EXACT, preferred_element_type=F32
         )
@@ -112,7 +113,7 @@
 def pair_kernel(zs, mine_ref, got_ref, *outs):
     z = lax.div(lax.axis_index("head"), 2)
     for k in range(zs):
-        block = lax.rem(z + k, zs)
+        block = z ^ k
         total = mine_ref[block] + got_ref[block].astype(F32)
         outs[k][...] = total.astype(outs[k].dtype)
 
@@ -274,7 +275,7 @@
 
     from_y = [
         lax.ppermute(
-            totals, "seq", [(i, (i // ys) * ys + (i + k) % ys) for i in range(seqs)]
+            totals, "seq", [(i, i ^ k) for i in range(seqs)]
         )
         for k in range(1, ys)
     ]
@@ -312,12 +313,12 @@
         name="plane",
     )(totals, *from_y, within)
     from_x = [
-        lax.ppermute(plane, "seq", [(i, i + k * ys) for i in range(seqs - k * ys)])
+        lax.ppermute(plane, "seq", [(i, i ^ (k * ys)) for i in range(seqs)])
         for k in range(1, xs)
     ]
 
     normed, theirs = pl.pallas_call(
-        functools.partial(project_kernel, heads, hd, parts),
+        functools.partial(project_kernel, heads, hd, parts, ys),
         out_shape=(
             jax.ShapeDtypeStruct((parts, own_rows, local), BF16),
             jax.ShapeDtypeStruct((zs, own_rows, width), BF16),
@@ -349,7 +350,7 @@
         name="pair",
     )(mine, got)
     from_z = [
-        lax.ppermute(blocks[k], "head", [(i, (i + 2 * k) % parts) for i in range(parts)])
+        lax.ppermute(blocks[k], "head", [(i, i ^ (2 * k)) for i in range(parts)])
         for k in range(1, zs)
     ]
 

time: 139 us -> 136 us (0.978)
  starting transfers between devices: 20.1 us -> 16.6 us
  waiting for transfers between devices: 14.3 us -> 16.8 us
  blocking collectives: 83.9 us -> 82.3 us
    ppermute x9, starting transfers between devices: 18.6 us -> 12.7 us  [the longest x3 5.03 us: shards(): lax.ppermute(blocks[k], 'head', [(i, i ^ 2 * k) for i in range(parts)])]
    ppermute x9, waiting for transfers between devices: 13.2 us -> 15.7 us  [the longest x3 7.62 us: shards(): lax.ppermute(blocks[k], 'head', [(i, i ^ 2 * k) for i in range(parts)])]
    ppermute x1, starting transfers between devices: 1.55 us -> 3.91 us  [shards(): got = lax.ppermute(theirs, 'head', [(i, i ^ 1) for i in range(parts)])]
    all_to_all x1, blocking collectives: 43.7 us -> 42.1 us  [shards(): lax.all_to_all(outgoing, ('seq', 'head'), split_axis=0, concat_axis=0, ti...]
where the time goes in v3:
time: 136 us
  blocking collectives  82.3 us (61%)
  Pallas kernels  19.3 us (14%)
  waiting for transfers between devices  16.8 us (12%)
  starting transfers between devices  16.6 us (12%)
    all_to_all x1, blocking collectives, shards(): lax.all_to_all(outgoing, ('seq', 'head'), split_axis=0, concat_axis=0, ti...  42.1 us
    all_to_all x1, blocking collectives, shards(): lax.all_to_all(produced, ('seq', 'head'), split_axis=0, concat_axis=0, ti...  40.2 us
    pallas_call x1, Pallas kernels, shards(): pl.pallas_call(functools.partial(expert_kernel, cap), out_shape=jax.Shape...  8.03 us
    ppermute x3, waiting for transfers between devices, shards(): lax.ppermute(blocks[k], 'head', [(i, i ^ 2 * k) for i in range(parts)])  7.62 us
    ppermute x3, starting transfers between devices, shards(): lax.ppermute(blocks[k], 'head', [(i, i ^ 2 * k) for i in range(parts)])  5.03 us
    ppermute x3, waiting for transfers between devices, shards(): lax.ppermute(plane, 'seq', [(i, i ^ k * ys) for i in range(seqs)])  4.55 us
    ppermute x3, starting transfers between devices, shards(): lax.ppermute(totals, 'seq', [(i, i ^ k) for i in range(seqs)])  4.31 us
    ppermute x1, starting transfers between devices, shards(): got = lax.ppermute(theirs, 'head', [(i, i ^ 1) for i in range(parts)])  3.91 us
  transfers between devices with their start and end apart: 10, of which 7 were waited for; matrix products, arithmetic and copies ran while one was open for 0% of the time, Pallas kernels for 3%

profile of v3, /device:TPU:1, one launch (start us, length us, event | category | flops | bytes accessed | tf_op | source)
XLA Modules:
  0.0 135.8 jit_solution(12851653996039013417)
XLA Ops:
  0.6 0.0 copy-start
  0.6 0.0 copy-start.8
  0.7 2.0 %totals.1 = (bf16[4,128,128]{2,1,0:T(8,128)(2,1)S(1)}, f32[256,512]{1,0:T(8,128)S(1)}, f32[256,512]{1,0:T(8,128)S(1)}, f32[256,512]{1,0:T(8,128)S(1)}) custom-call(f32[256,512]{1,0:T(8,128)} %q_hbm.1, f32[256,512]{1,0:T(8,128)} %k_hbm.1, f32[256,512]{1,0:T(8,128)} %v_hbm.1), custom_call_target="tpu_custom_call" | custom-call | tf_op jit(solution)/shard_map/totals/pallas_call | solution.py:265
  2.7 3.6 %collective-permute-start.2 = (bf16[4,128,128]{2,1,0:T(8,128)(2,1)S(1)}, bf16[4,128,128]{2,1,0:T(8,128)(2,1)S(1)}, u32[]{:S(2)}, u32[]{:S(2)}) collective-permute-start(bf16[4,128,128]{2,1,0:T(8,128)(2,1)S(1)} %get-tuple-element.22.own_ref), channel_id=1, source_target_pairs={{0,24},{8,16},{16,8},{24,0},{32,56},{40,48},{48,40},{56,32},{64,88... | collective-permute-start | bytes 393224 | tf_op jit(solution)/shard_map/ppermute | solution.py:277
  6.3 0.4 collective-permute-start.1
  6.7 0.3 collective-permute-start
  7.0 2.2 %within.1.refs_3_.in_ref = f32[256,512]{1,0:T(8,128)S(1)} custom-call(f32[256,512]{1,0:T(8,128)S(1)} %get-tuple-element.19.q_ref, f32[256,512]{1,0:T(8,128)S(1)} %get-tuple-element.20.k_ref, f32[256,512]{1,0:T(8,128)S(1)} %get-tuple-element.21.v_ref), custom_call_target="tpu_custom_call" | custom-call | flops 805306368 | bytes 2097152 | tf_op jit(solution)/shard_map/within/pallas_call | solution.py:282
  9.2 2.6 %collective-permute-done.2.refs_2_ = bf16[4,128,128]{2,1,0:T(8,128)(2,1)S(1)} collective-permute-done((bf16[4,128,128]{2,1,0:T(8,128)(2,1)S(1)}, bf16[4,128,128]{2,1,0:T(8,128)(2,1)S(1)}, u32[]{:S(2)}, u32[]{:S(2)}) %collective-permute-start.2) | collective-permute-done | bytes 131104 | tf_op jit(solution)/shard_map/ppermute | solution.py:277
  11.8 0.0 collective-permute-done.1.refs_1_
  11.8 0.9 collective-permute-done.refs_0_
  12.7 0.1 plane.1
  12.9 2.5 %collective-permute-start.5 = (bf16[4,128,128]{2,1,0:T(8,128)(2,1)S(1)}, bf16[4,128,128]{2,1,0:T(8,128)(2,1)S(1)}, u32[]{:S(2)}, u32[]{:S(2)}) collective-permute-start(bf16[4,128,128]{2,1,0:T(8,128)(2,1)S(1)} %get-tuple-element.24), channel_id=1, source_target_pairs={{0,96},{8,104},{16,112},{24,120},{32,64},{40,72},{48,80},{56,88},{... | collective-permute-start | bytes 393224 | tf_op jit(solution)/shard_map/ppermute | solution.py:316
  15.3 0.5 collective-permute-start.4
  15.9 0.3 collective-permute-start.3
  16.2 2.4 %collective-permute-done.5.s3_ref = bf16[4,128,128]{2,1,0:T(8,128)(2,1)S(1)} collective-permute-done((bf16[4,128,128]{2,1,0:T(8,128)(2,1)S(1)}, bf16[4,128,128]{2,1,0:T(8,128)(2,1)S(1)}, u32[]{:S(2)}, u32[]{:S(2)}) %collective-permute-start.5) | collective-permute-done | bytes 131104 | tf_op jit(solution)/shard_map/ppermute | solution.py:316
  18.6 2.1 %collective-permute-done.4.s2_ref = bf16[4,128,128]{2,1,0:T(8,128)(2,1)S(1)} collective-permute-done((bf16[4,128,128]{2,1,0:T(8,128)(2,1)S(1)}, bf16[4,128,128]{2,1,0:T(8,128)(2,1)S(1)}, u32[]{:S(2)}, u32[]{:S(2)}) %collective-permute-start.4) | collective-permute-done | bytes 131104 | tf_op jit(solution)/shard_map/ppermute | solution.py:316
  20.7 0.0 collective-permute-done.3.s1_ref
  20.8 0.0 copy-done
  20.8 0.0 copy-done.8
  20.8 1.2 project.1
  21.9 0.0 copy-start.5
  21.9 0.0 copy-start.4
  21.9 0.0 copy-start.6
  22.0 3.9 %collective-permute-start.6 = (bf16[4,32,2048]{2,1,0:T(8,128)(2,1)S(1)}, bf16[4,32,2048]{2,1,0:T(8,128)(2,1)S(1)}, u32[]{:S(2)}, u32[]{:S(2)}) collective-permute-start(bf16[4,32,2048]{2,1,0:T(8,128)(2,1)S(1)} %get-tuple-element.26), channel_id=1, source_target_pairs={{0,1},{1,0},{2,3},{3,2},{4,5},{5,4},{6,7},{7,6},{8,9},{9,8},{10,11... | collective-permute-start | bytes 1572872 | tf_op jit(solution)/shard_map/ppermute | solution.py:333
  25.9 0.0 copy-start.3
  25.9 0.5 keep.1.mine_ref
  26.3 1.1 collective-permute-done.6.got_ref
  27.4 0.1 pair.1
  27.5 1.7 %collective-permute-start.7 = (bf16[32,2048]{1,0:T(8,128)(2,1)S(1)}, bf16[32,2048]{1,0:T(8,128)(2,1)S(1)}, u32[]{:S(2)}, u32[]{:S(2)}) collective-permute-start(bf16[32,2048]{1,0:T(8,128)(2,1)S(1)} %get-tuple-element.28), channel_id=1, source_target_pairs={{0,2},{1,3},{2,0},{3,1},{4,6},{5,7},{6,4},{7,5},{8,10},{9,11},{10,... | collective-permute-start | bytes 393224 | tf_op jit(solution)/shard_map/ppermute | solution.py:353
  29.2 3.3 %collective-permute-start.8 = (bf16[32,2048]{1,0:T(8,128)(2,1)S(1)}, bf16[32,2048]{1,0:T(8,128)(2,1)S(1)}, u32[]{:S(2)}, u32[]{:S(2)}) collective-permute-start(bf16[32,2048]{1,0:T(8,128)(2,1)S(1)} %get-tuple-element.29), channel_id=1, source_target_pairs={{0,4},{1,5},{2,6},{3,7},{4,0},{5,1},{6,2},{7,3},{8,12},{9,13},{10,... | collective-permute-start | bytes 393224 | tf_op jit(solution)/shard_map/ppermute | solution.py:353
  32.5 0.0 collective-permute-start.9
  32.5 0.0 copy-done.5
  32.5 1.0 routing.1
  33.5 0.0 collective-permute-done.7.o1_ref
  33.5 5.1 %collective-permute-done.8.o2_ref = bf16[32,2048]{1,0:T(8,128)(2,1)S(1)} collective-permute-done((bf16[32,2048]{1,0:T(8,128)(2,1)S(1)}, bf16[32,2048]{1,0:T(8,128)(2,1)S(1)}, u32[]{:S(2)}, u32[]{:S(2)}) %collective-permute-start.8) | collective-permute-done | bytes 131104 | tf_op jit(solution)/shard_map/ppermute | solution.py:353
  38.6 2.5 %collective-permute-done.9.o3_ref = bf16[32,2048]{1,0:T(8,128)(2,1)S(1)} collective-permute-done((bf16[32,2048]{1,0:T(8,128)(2,1)S(1)}, bf16[32,2048]{1,0:T(8,128)(2,1)S(1)}, u32[]{:S(2)}, u32[]{:S(2)}) %collective-permute-start.9) | collective-permute-done | bytes 131104 | tf_op jit(solution)/shard_map/ppermute | solution.py:353
  41.1 0.0 copy-done.4
  41.1 0.0 copy-done.6
  41.1 2.2 %dispatch.1 = (bf16[32,2048]{1,0:T(8,128)(2,1)}, bf16[128,16,640]{2,1,0:T(8,128)(2,1)S(1)}) custom-call(s32[8,128]{1,0:T(8,128)S(1)} %get-tuple-element.18.tokens_ref, f32[32,2048]{1,0:T(8,128)S(1)} %get-tuple-element.27.o0_ref, bf16[32,2048]{1,0:T(8,128)(2,1)S(1)} %collective-permute-done.7.o1_ref, bf16[32,2048]{1,0:T(8,128)(2,1)S(1)} %collective-permute-done.8.o2_ref, ...), custom_call_target="tpu_custom_call" | custom-call | tf_op jit(solution)/shard_map/dispatch/pallas_call | solution.py:357
  43.3 42.1 %all_to_all.10.in_ref = bf16[128,16,640]{2,1,0:T(8,128)(2,1)S(1)} all-to-all(bf16[128,16,640]{2,1,0:T(8,128)(2,1)S(1)} %get-tuple-element.33), channel_id=1, replica_groups=mesh['seq'=16,'head'=8] {'seq','head'}, dimensions={0} | all-to-all | bytes 5242880 | tf_op jit(solution)/shard_map/all_to_all | solution.py:373
  85.4 0.0 copy-done.3
  85.4 0.0 copy-done.2
  85.4 0.0 copy-done.1
  85.4 8.0 %expert.1 = bf16[128,16,640]{2,1,0:T(8,128)(2,1)S(1)} custom-call(bf16[128,16,640]{2,1,0:T(8,128)(2,1)S(1)} %all_to_all.10.in_ref, bf16[1,2048,768]{2,1,0:T(8,128)(2,1)S(1)} %copy-done.1, bf16[1,2048,768]{2,1,0:T(8,128)(2,1)S(1)} %copy-done.2, bf16[1,768,2048]{2,1,0:T(8,128)(2,1)S(1)} %copy-done.3), custom_call_target="tpu_custom_call" | custom-call | tf_op jit(solution)/shard_map/expert/pallas_call | solution.py:375
  93.5 0.0 copy-start.7
  93.5 40.2 %all_to_all.11.back_ref = bf16[128,16,640]{2,1,0:T(8,128)(2,1)S(1)} all-to-all(bf16[128,16,640]{2,1,0:T(8,128)(2,1)S(1)} %expert.1), channel_id=1, replica_groups=mesh['seq'=16,'head'=8] {'seq','head'}, dimensions={0} | all-to-all | bytes 5242880 | tf_op jit(solution)/shard_map/all_to_all | solution.py:389
  133.7 0.0 copy-done.7
  133.7 2.1 %combine.1 = bf16[32,2048]{1,0:T(8,128)(2,1)} custom-call(s32[8,32]{1,0:T(8,128)S(1)} %bitcast.5, s32[8,32]{1,0:T(8,128)S(1)} %get-tuple-element.32.slots_ref, f32[8,32]{1,0:T(8,128)S(1)} %bitcast.7, bf16[128,16,640]{2,1,0:T(8,128)(2,1)S(1)} %all_to_all.11.back_ref), custom_call_target="tpu_custom_call" | custom-call | tf_op jit(solution)/shard_map/combine/pallas_call | solution.py:391
  (2 shorter events, 0.0 us)
Async XLA Ops:
  0.6 20.1 %copy-start = (bf16[512,2048]{1,0:T(8,128)(2,1)S(1)}, bf16[512,2048]{1,0:T(8,128)(2,1)}, u32[]{:S(2)}) copy-start(bf16[512,2048]{1,0:T(8,128)(2,1)} %w_ref.3) | copy-start | bytes 6291460
  0.6 20.1 %copy-start.8 = (f32[128]{0:T(128)S(1)}, f32[128]{0:T(128)}, u32[]{:S(2)}) copy-start(f32[128]{0:T(128)} %param.15) | copy-start | bytes 1540
  2.7 9.1 %collective-permute-start.2 = (bf16[4,128,128]{2,1,0:T(8,128)(2,1)S(1)}, bf16[4,128,128]{2,1,0:T(8,128)(2,1)S(1)}, u32[]{:S(2)}, u32[]{:S(2)}) collective-permute-start(bf16[4,128,128]{2,1,0:T(8,128)(2,1)S(1)} %get-tuple-element.22.own_ref), channel_id=1, source_target_pairs={{0,24},{8,16},{16,8},{24,0},{32,56},{40,48},{48,40},{56,32},{64,88... | collective-permute-start | bytes 393224 | tf_op jit(solution)/shard_map/ppermute | solution.py:277
  6.3 5.5 %collective-permute-start.1 = (bf16[4,128,128]{2,1,0:T(8,128)(2,1)S(1)}, bf16[4,128,128]{2,1,0:T(8,128)(2,1)S(1)}, u32[]{:S(2)}, u32[]{:S(2)}) collective-permute-start(bf16[4,128,128]{2,1,0:T(8,128)(2,1)S(1)} %get-tuple-element.22.own_ref), channel_id=1, source_target_pairs={{0,16},{8,24},{16,0},{24,8},{32,48},{40,56},{48,32},{56,40},{64,80... | collective-permute-start | bytes 393224 | tf_op jit(solution)/shard_map/ppermute | solution.py:277
  6.7 6.1 %collective-permute-start = (bf16[4,128,128]{2,1,0:T(8,128)(2,1)S(1)}, bf16[4,128,128]{2,1,0:T(8,128)(2,1)S(1)}, u32[]{:S(2)}, u32[]{:S(2)}) collective-permute-start(bf16[4,128,128]{2,1,0:T(8,128)(2,1)S(1)} %get-tuple-element.22.own_ref), channel_id=1, source_target_pairs={{0,8},{8,0},{16,24},{24,16},{32,40},{40,32},{48,56},{56,48},{64,72... | collective-permute-start | bytes 393224 | tf_op jit(solution)/shard_map/ppermute | solution.py:277
  12.9 5.8 %collective-permute-start.5 = (bf16[4,128,128]{2,1,0:T(8,128)(2,1)S(1)}, bf16[4,128,128]{2,1,0:T(8,128)(2,1)S(1)}, u32[]{:S(2)}, u32[]{:S(2)}) collective-permute-start(bf16[4,128,128]{2,1,0:T(8,128)(2,1)S(1)} %get-tuple-element.24), channel_id=1, source_target_pairs={{0,96},{8,104},{16,112},{24,120},{32,64},{40,72},{48,80},{56,88},{... | collective-permute-start | bytes 393224 | tf_op jit(solution)/shard_map/ppermute | solution.py:316
  15.3 5.4 %collective-permute-start.4 = (bf16[4,128,128]{2,1,0:T(8,128)(2,1)S(1)}, bf16[4,128,128]{2,1,0:T(8,128)(2,1)S(1)}, u32[]{:S(2)}, u32[]{:S(2)}) collective-permute-start(bf16[4,128,128]{2,1,0:T(8,128)(2,1)S(1)} %get-tuple-element.24), channel_id=1, source_target_pairs={{0,64},{8,72},{16,80},{24,88},{32,96},{40,104},{48,112},{56,120},{... | collective-permute-start | bytes 393224 | tf_op jit(solution)/shard_map/ppermute | solution.py:316
  15.9 4.9 %collective-permute-start.3 = (bf16[4,128,128]{2,1,0:T(8,128)(2,1)S(1)}, bf16[4,128,128]{2,1,0:T(8,128)(2,1)S(1)}, u32[]{:S(2)}, u32[]{:S(2)}) collective-permute-start(bf16[4,128,128]{2,1,0:T(8,128)(2,1)S(1)} %get-tuple-element.24), channel_id=1, source_target_pairs={{0,32},{8,40},{16,48},{24,56},{32,0},{40,8},{48,16},{56,24},{64,96... | collective-permute-start | bytes 393224 | tf_op jit(solution)/shard_map/ppermute | solution.py:316
  21.9 10.6 %copy-start.5 = (s32[32,8]{0,1:T(8,128)S(1)}, s32[32,8]{0,1:T(8,128)}, u32[]{:S(2)}) copy-start(s32[32,8]{0,1:T(8,128)} %param.19) | copy-start | bytes 3076
  21.9 19.2 %copy-start.4 = (bf16[32,2048]{1,0:T(8,128)(2,1)S(1)}, bf16[32,2048]{1,0:T(8,128)(2,1)}, u32[]{:S(2)}) copy-start(bf16[32,2048]{1,0:T(8,128)(2,1)} %res_ref.1) | copy-start | bytes 393220
  21.9 19.2 %copy-start.6 = (f32[2048]{0:T(1024)S(1)}, f32[2048]{0:T(1024)}, u32[]{:S(2)}) copy-start(f32[2048]{0:T(1024)} %param.18) | copy-start | bytes 24580
  22.0 5.4 %collective-permute-start.6 = (bf16[4,32,2048]{2,1,0:T(8,128)(2,1)S(1)}, bf16[4,32,2048]{2,1,0:T(8,128)(2,1)S(1)}, u32[]{:S(2)}, u32[]{:S(2)}) collective-permute-start(bf16[4,32,2048]{2,1,0:T(8,128)(2,1)S(1)} %get-tuple-element.26), channel_id=1, source_target_pairs={{0,1},{1,0},{2,3},{3,2},{4,5},{5,4},{6,7},{7,6},{8,9},{9,8},{10,11... | collective-permute-start | bytes 1572872 | tf_op jit(solution)/shard_map/ppermute | solution.py:333
  25.9 59.6 %copy-start.3 = (bf16[1,768,2048]{2,1,0:T(8,128)(2,1)S(1)}, bf16[1,768,2048]{2,1,0:T(8,128)(2,1)}, u32[]{:S(2)}) copy-start(bf16[1,768,2048]{2,1,0:T(8,128)(2,1)} %down_ref.1) | copy-start | bytes 9437188
  27.4 58.0 %copy-start.2 = (bf16[1,2048,768]{2,1,0:T(8,128)(2,1)S(1)}, bf16[1,2048,768]{2,1,0:T(8,128)(2,1)}, u32[]{:S(2)}) copy-start(bf16[1,2048,768]{2,1,0:T(8,128)(2,1)} %up_ref.1) | copy-start | bytes 9437188
  27.5 6.0 %collective-permute-start.7 = (bf16[32,2048]{1,0:T(8,128)(2,1)S(1)}, bf16[32,2048]{1,0:T(8,128)(2,1)S(1)}, u32[]{:S(2)}, u32[]{:S(2)}) collective-permute-start(bf16[32,2048]{1,0:T(8,128)(2,1)S(1)} %get-tuple-element.28), channel_id=1, source_target_pairs={{0,2},{1,3},{2,0},{3,1},{4,6},{5,7},{6,4},{7,5},{8,10},{9,11},{10,... | collective-permute-start | bytes 393224 | tf_op jit(solution)/shard_map/ppermute | solution.py:353
  29.2 9.4 %collective-permute-start.8 = (bf16[32,2048]{1,0:T(8,128)(2,1)S(1)}, bf16[32,2048]{1,0:T(8,128)(2,1)S(1)}, u32[]{:S(2)}, u32[]{:S(2)}) collective-permute-start(bf16[32,2048]{1,0:T(8,128)(2,1)S(1)} %get-tuple-element.29), channel_id=1, source_target_pairs={{0,4},{1,5},{2,6},{3,7},{4,0},{5,1},{6,2},{7,3},{8,12},{9,13},{10,... | collective-permute-start | bytes 393224 | tf_op jit(solution)/shard_map/ppermute | solution.py:353
  32.5 8.6 %collective-permute-start.9 = (bf16[32,2048]{1,0:T(8,128)(2,1)S(1)}, bf16[32,2048]{1,0:T(8,128)(2,1)S(1)}, u32[]{:S(2)}, u32[]{:S(2)}) collective-permute-start(bf16[32,2048]{1,0:T(8,128)(2,1)S(1)} %get-tuple-element.30), channel_id=1, source_target_pairs={{0,6},{1,7},{2,4},{3,5},{4,2},{5,3},{6,0},{7,1},{8,14},{9,15},{10,... | collective-permute-start | bytes 393224 | tf_op jit(solution)/shard_map/ppermute | solution.py:353
  43.3 42.1 %copy-start.1 = (bf16[1,2048,768]{2,1,0:T(8,128)(2,1)S(1)}, bf16[1,2048,768]{2,1,0:T(8,128)(2,1)}, u32[]{:S(2)}) copy-start(bf16[1,2048,768]{2,1,0:T(8,128)(2,1)} %gate_ref.1) | copy-start | bytes 9437188
  93.5 40.3 %copy-start.7 = (f32[32,8]{0,1:T(8,128)S(1)}, f32[32,8]{0,1:T(8,128)}, u32[]{:S(2)}) copy-start(f32[32,8]{0,1:T(8,128)} %param.20) | copy-start | bytes 3076

commit v4 on v3

--- a/solution.py
+++ b/solution.py
@@ -63,33 +63,41 @@
         )
 
 
-def plane_kernel(own_ref, *refs):
-    parts, plane_ref, base_ref = refs[:-3], refs[-2], refs[-1]
-    y = lax.rem(lax.axis_index("seq"), len(parts) + 1)
-    plane = own_ref[...].astype(F32)
-    base = jnp.zeros(own_ref.shape, F32)
+def plane_kernel(ys, own_ref, *refs):
+    others = (len(refs) - 2) // 2
+    parts, sent, base_ref = refs[:others], refs[-1 - others : -1], refs[-1]
+    seq = lax.axis_index("seq")
+    x, y = lax.div(seq, ys), lax.rem(seq, ys)
+    y_first = lax.rem(lax.axis_index("head"), 2) == 0
+    first = jnp.where(y_first, y, x)
+    second = jnp.where(y_first, x, y)
+    own = own_ref[...].astype(F32)
+    total = own
+    before = jnp.zeros(own_ref.shape, F32)
     for k, part in enumerate(parts, 1):
         wide = part[...].astype(F32)
-        plane = plane + wide
-        base = base + jnp.where((y ^ k) < y, wide, 0.0)
-    plane_ref[...] = plane.astype(BF16)
-    base_ref[...] = base
+        total = total + wide
+        before = before + jnp.where((first ^ k) < first, wide, 0.0)
+    base_ref[...] = before
+    later = jnp.where(y_first, total, before + own)
+    sooner = jnp.where(y_first, jnp.zeros_like(before), before)
+    for k, out in enumerate(sent, 1):
+        out[...] = jnp.where((second ^ k) > second, later, sooner).astype(BF16)
 
 
 def project_kernel(
-    heads, hd, parts, ys, q_ref, in_ref, base_ref, s1_ref, s2_ref, s3_ref, gain_ref, w_ref,
+    heads, hd, parts, q_ref, in_ref, base_ref, s1_ref, s2_ref, s3_ref, gain_ref, w_ref,
     normed_ref, theirs_ref,
 ):
     rows = q_ref.shape[0]
     step = rows // parts
     core = lax.rem(lax.axis_index("head"), 2)
-    x = lax.div(lax.axis_index("seq"), ys)
     gain = gain_ref[...]
     for h in range(heads):
         cols = slice(h * hd, (h + 1) * hd)
         state = base_ref[h]
-        for k, part in enumerate((s1_ref, s2_ref, s3_ref), 1):
-            state = state + jnp.where((x ^ k) < x, part[h].astype(F32), 0.0)
+        for part in (s1_ref, s2_ref, s3_ref):
+            state = state + part[h].astype(F32)
         att = in_ref[:, cols] + jnp.dot(
             q_ref[:, cols], state, precision=EXACT, preferred_element_type=F32
         )
@@ -146,11 +154,13 @@
 
 
 def dispatch_kernel(
-    cap, tokens_ref, o0_ref, o1_ref, o2_ref, o3_ref, res_ref, gain_ref, attn_ref, out_ref,
-    wide_ref, tile_ref,
+    cap, tokens_hbm, o0_ref, o1_ref, o2_ref, o3_ref, res_ref, gain_ref, attn_ref, out_ref,
+    wide_ref, tile_ref, tokens_ref, sem,
 ):
     rows, width = res_ref.shape
     per = width // 128
+    fetch = pltpu.make_async_copy(tokens_hbm, tokens_ref, sem)
+    fetch.start()
     total = (
         o0_ref[...] + o1_ref[...].astype(F32) + o2_ref[...].astype(F32) + o3_ref[...].astype(F32)
     )
@@ -163,6 +173,7 @@
         wide_ref[pl.ds(j, rows, stride=per), :] = normed[:, j * 128 : (j + 1) * 128]
     tile_ref[...] = wide_ref[...].astype(BF16).reshape(rows, per, 128)
 
+    fetch.wait()
     for d in range(out_ref.shape[0]):
         for s in range(cap):
             out_ref[d, :, s * 128 : (s + 1) * 128] = tile_ref[tokens_ref[s, d]]
@@ -254,7 +265,7 @@
     width = out_weight.shape[1]
     seqs = lax.axis_size("seq")
     parts = lax.axis_size("head")
-    xs, zs = seqs // ys, parts // 2
+    zs = parts // 2
     peers = seqs * parts
     hidden = expert_gate.shape[2]
     own_rows, top = routed_experts.shape
@@ -273,12 +284,14 @@
         name="totals",
     )(*(in_hbm(part) for part in (attn_queries, attn_keys, attn_values)))
 
-    from_y = [
-        lax.ppermute(
-            totals, "seq", [(i, i ^ k) for i in range(seqs)]
-        )
-        for k in range(1, ys)
-    ]
+    def exchange(value, k, turn):
+        pairs = []
+        for device in range(peers):
+            along_y = (device % 2 == 0) == (turn == 0)
+            pairs.append((device, device ^ (k * parts * (1 if along_y else ys))))
+        return lax.ppermute(value, ("seq", "head"), pairs)
+
+    first = [exchange(totals, k, 0) for k in range(1, ys)]
     within = pl.pallas_call(
         functools.partial(within_kernel, heads, hd),
         out_shape=jax.ShapeDtypeStruct((rows, local), F32),
@@ -301,24 +314,19 @@
         name="routing",
     )(routed)
 
-    plane, base = pl.pallas_call(
-        plane_kernel,
-        out_shape=(
-            jax.ShapeDtypeStruct(state_shape, BF16),
-            jax.ShapeDtypeStruct(state_shape, F32),
-        ),
+    *sent, base = pl.pallas_call(
+        functools.partial(plane_kernel, ys),
+        out_shape=(jax.ShapeDtypeStruct(state_shape, BF16),) * (ys - 1)
+        + (jax.ShapeDtypeStruct(state_shape, F32),),
         in_specs=[VM] * ys + [pl.BlockSpec(memory_space=pl.ANY)],
-        out_specs=(VM, VM),
-        compiler_params=params(2),
+        out_specs=(VM,) * ys,
+        compiler_params=params(4),
         name="plane",
-    )(totals, *from_y, within)
-    from_x = [
-        lax.ppermute(plane, "seq", [(i, i ^ (k * ys)) for i in range(seqs)])
-        for k in range(1, xs)
-    ]
+    )(totals, *first, within)
+    second = [exchange(value, k, 1) for k, value in enumerate(sent, 1)]
 
     normed, theirs = pl.pallas_call(
-        functools.partial(project_kernel, heads, hd, parts, ys),
+        functools.partial(project_kernel, heads, hd, parts),
         out_shape=(
             jax.ShapeDtypeStruct((parts, own_rows, local), BF16),
             jax.ShapeDtypeStruct((zs, own_rows, width), BF16),
@@ -328,7 +336,7 @@
         compiler_params=params(2),
         name="project",
     )(
-        queries, within, base, *from_x, head_gain.reshape(1, hd), out_weight
+        queries, within, base, *second, head_gain.reshape(1, hd), out_weight
     )
     got = lax.ppermute(theirs, "head", [(i, i ^ 1) for i in range(parts)])
     mine = pl.pallas_call(
@@ -360,11 +368,13 @@
             jax.ShapeDtypeStruct((own_rows, width), BF16),
             jax.ShapeDtypeStruct((peers, per, cap * 128), BF16),
         ),
-        in_specs=[SM] + [VM] * 6,
+        in_specs=[pl.BlockSpec(memory_space=pl.ANY)] + [VM] * 6,
         out_specs=(VM, VM),
         scratch_shapes=[
             pltpu.VMEM((own_rows * per, 128), F32),
             pltpu.VMEM((own_rows, per, 128), BF16),
+            pltpu.SMEM((8, peers), jnp.int32),
+            pltpu.SemaphoreType.DMA,
         ],
         compiler_params=params(2),
         name="dispatch",

time: 136 us -> 134 us (0.985)
  blocking collectives: 82.3 us -> 80.7 us
    all_to_all x1, blocking collectives: 42.1 us -> 40.5 us  [shards(): lax.all_to_all(outgoing, ('seq', 'head'), split_axis=0, concat_axis=0, ti...]
where the time goes in v4:
time: 134 us
  blocking collectives  80.7 us (60%)
  Pallas kernels  19.2 us (14%)
  waiting for transfers between devices  16.6 us (12%)
  starting transfers between devices  16.5 us (12%)
    all_to_all x1, blocking collectives, shards(): lax.all_to_all(outgoing, ('seq', 'head'), split_axis=0, concat_axis=0, ti...  40.5 us
    all_to_all x1, blocking collectives, shards(): lax.all_to_all(produced, ('seq', 'head'), split_axis=0, concat_axis=0, ti...  40.2 us
    ppermute x6, starting transfers between devices, exchange(): return lax.ppermute(value, ('seq', 'head'), pairs)  8.05 us
    pallas_call x1, Pallas kernels, shards(): pl.pallas_call(functools.partial(expert_kernel, cap), out_shape=jax.Shape...  8.03 us
    ppermute x6, waiting for transfers between devices, exchange(): return lax.ppermute(value, ('seq', 'head'), pairs)  7.88 us
    ppermute x3, waiting for transfers between devices, shards(): lax.ppermute(blocks[k], 'head', [(i, i ^ 2 * k) for i in range(parts)])  7.62 us
    ppermute x3, starting transfers between devices, shards(): lax.ppermute(blocks[k], 'head', [(i, i ^ 2 * k) for i in range(parts)])  5.02 us
    ppermute x1, starting transfers between devices, shards(): got = lax.ppermute(theirs, 'head', [(i, i ^ 1) for i in range(parts)])  3.47 us
  transfers between devices with their start and end apart: 10, of which 7 were waited for; matrix products, arithmetic and copies ran while one was open for 0% of the time, Pallas kernels for 3%

profile of v4, /device:TPU:1, one launch (start us, length us, event | category | flops | bytes accessed | tf_op | source)
XLA Modules:
  0.0 133.8 jit_solution(10390938709127174329)
XLA Ops:
  0.6 0.0 copy-start
  0.6 0.0 copy-start.8
  0.7 2.0 %totals.1 = (bf16[4,128,128]{2,1,0:T(8,128)(2,1)S(1)}, f32[256,512]{1,0:T(8,128)S(1)}, f32[256,512]{1,0:T(8,128)S(1)}, f32[256,512]{1,0:T(8,128)S(1)}) custom-call(f32[256,512]{1,0:T(8,128)} %q_hbm.1, f32[256,512]{1,0:T(8,128)} %k_hbm.1, f32[256,512]{1,0:T(8,128)} %v_hbm.1), custom_call_target="tpu_custom_call" | custom-call | tf_op jit(solution)/shard_map/totals/pallas_call | solution.py:276
  2.7 3.4 %collective-permute-start.2 = (bf16[4,128,128]{2,1,0:T(8,128)(2,1)S(1)}, bf16[4,128,128]{2,1,0:T(8,128)(2,1)S(1)}, u32[]{:S(2)}, u32[]{:S(2)}) collective-permute-start(bf16[4,128,128]{2,1,0:T(8,128)(2,1)S(1)} %get-tuple-element.24.own_ref), channel_id=1, source_target_pairs={{0,24},{1,97},{2,26},{3,99},{4,28},{5,101},{6,30},{7,103},{8,16},{... | collective-permute-start | bytes 393224 | tf_op jit(solution)/shard_map/ppermute | solution.py:292
  6.1 0.5 collective-permute-start.1
  6.6 0.2 collective-permute-start
  6.7 2.2 %within.1.refs_3_.in_ref = f32[256,512]{1,0:T(8,128)S(1)} custom-call(f32[256,512]{1,0:T(8,128)S(1)} %get-tuple-element.21.q_ref, f32[256,512]{1,0:T(8,128)S(1)} %get-tuple-element.22.k_ref, f32[256,512]{1,0:T(8,128)S(1)} %get-tuple-element.23.v_ref), custom_call_target="tpu_custom_call" | custom-call | flops 805306368 | bytes 2097152 | tf_op jit(solution)/shard_map/within/pallas_call | solution.py:295
  9.0 0.4 collective-permute-done.2.refs_2_
  9.4 2.0 %collective-permute-done.1.refs_1_ = bf16[4,128,128]{2,1,0:T(8,128)(2,1)S(1)} collective-permute-done((bf16[4,128,128]{2,1,0:T(8,128)(2,1)S(1)}, bf16[4,128,128]{2,1,0:T(8,128)(2,1)S(1)}, u32[]{:S(2)}, u32[]{:S(2)}) %collective-permute-start.1) | collective-permute-done | bytes 131104 | tf_op jit(solution)/shard_map/ppermute | solution.py:292
  11.4 0.0 collective-permute-done.refs_0_
  11.4 0.2 plane.1
  11.6 1.4 %collective-permute-start.3 = (bf16[4,128,128]{2,1,0:T(8,128)(2,1)S(1)}, bf16[4,128,128]{2,1,0:T(8,128)(2,1)S(1)}, u32[]{:S(2)}, u32[]{:S(2)}) collective-permute-start(bf16[4,128,128]{2,1,0:T(8,128)(2,1)S(1)} %get-tuple-element.26), channel_id=1, source_target_pairs={{0,32},{1,9},{2,34},{3,11},{4,36},{5,13},{6,38},{7,15},{8,40},{9,1... | collective-permute-start | bytes 393224 | tf_op jit(solution)/shard_map/ppermute | solution.py:292
  13.0 2.6 %collective-permute-start.4 = (bf16[4,128,128]{2,1,0:T(8,128)(2,1)S(1)}, bf16[4,128,128]{2,1,0:T(8,128)(2,1)S(1)}, u32[]{:S(2)}, u32[]{:S(2)}) collective-permute-start(bf16[4,128,128]{2,1,0:T(8,128)(2,1)S(1)} %get-tuple-element.27), channel_id=1, source_target_pairs={{0,64},{1,17},{2,66},{3,19},{4,68},{5,21},{6,70},{7,23},{8,72},{9,... | collective-permute-start | bytes 393224 | tf_op jit(solution)/shard_map/ppermute | solution.py:292
  15.6 0.0 collective-permute-start.5
  15.6 0.0 collective-permute-done.3.s1_ref
  15.6 3.8 %collective-permute-done.4.s2_ref = bf16[4,128,128]{2,1,0:T(8,128)(2,1)S(1)} collective-permute-done((bf16[4,128,128]{2,1,0:T(8,128)(2,1)S(1)}, bf16[4,128,128]{2,1,0:T(8,128)(2,1)S(1)}, u32[]{:S(2)}, u32[]{:S(2)}) %collective-permute-start.4) | collective-permute-done | bytes 131104 | tf_op jit(solution)/shard_map/ppermute | solution.py:292
  19.3 1.7 %collective-permute-done.5.s3_ref = bf16[4,128,128]{2,1,0:T(8,128)(2,1)S(1)} collective-permute-done((bf16[4,128,128]{2,1,0:T(8,128)(2,1)S(1)}, bf16[4,128,128]{2,1,0:T(8,128)(2,1)S(1)}, u32[]{:S(2)}, u32[]{:S(2)}) %collective-permute-start.5) | collective-permute-done | bytes 131104 | tf_op jit(solution)/shard_map/ppermute | solution.py:292
  21.0 0.0 copy-done
  21.0 0.0 copy-done.8
  21.0 1.1 project.1
  22.2 0.0 copy-start.5
  22.2 0.0 copy-start.4
  22.2 0.0 copy-start.6
  22.2 3.5 %collective-permute-start.6 = (bf16[4,32,2048]{2,1,0:T(8,128)(2,1)S(1)}, bf16[4,32,2048]{2,1,0:T(8,128)(2,1)S(1)}, u32[]{:S(2)}, u32[]{:S(2)}) collective-permute-start(bf16[4,32,2048]{2,1,0:T(8,128)(2,1)S(1)} %get-tuple-element.30), channel_id=1, source_target_pairs={{0,1},{1,0},{2,3},{3,2},{4,5},{5,4},{6,7},{7,6},{8,9},{9,8},{10,11... | collective-permute-start | bytes 1572872 | tf_op jit(solution)/shard_map/ppermute | solution.py:341
  25.7 0.5 keep.1.mine_ref
  26.2 1.1 collective-permute-done.6.got_ref
  27.2 0.1 pair.1
  27.3 1.7 %collective-permute-start.7 = (bf16[32,2048]{1,0:T(8,128)(2,1)S(1)}, bf16[32,2048]{1,0:T(8,128)(2,1)S(1)}, u32[]{:S(2)}, u32[]{:S(2)}) collective-permute-start(bf16[32,2048]{1,0:T(8,128)(2,1)S(1)} %get-tuple-element.32), channel_id=1, source_target_pairs={{0,2},{1,3},{2,0},{3,1},{4,6},{5,7},{6,4},{7,5},{8,10},{9,11},{10,... | collective-permute-start | bytes 393224 | tf_op jit(solution)/shard_map/ppermute | solution.py:361
  29.0 3.3 %collective-permute-start.8 = (bf16[32,2048]{1,0:T(8,128)(2,1)S(1)}, bf16[32,2048]{1,0:T(8,128)(2,1)S(1)}, u32[]{:S(2)}, u32[]{:S(2)}) collective-permute-start(bf16[32,2048]{1,0:T(8,128)(2,1)S(1)} %get-tuple-element.33), channel_id=1, source_target_pairs={{0,4},{1,5},{2,6},{3,7},{4,0},{5,1},{6,2},{7,3},{8,12},{9,13},{10,... | collective-permute-start | bytes 393224 | tf_op jit(solution)/shard_map/ppermute | solution.py:361
  32.3 0.0 collective-permute-start.9
  32.3 0.0 copy-done.5
  32.3 1.0 routing.1
  33.3 0.0 collective-permute-done.7.o1_ref
  33.3 5.1 %collective-permute-done.8.o2_ref = bf16[32,2048]{1,0:T(8,128)(2,1)S(1)} collective-permute-done((bf16[32,2048]{1,0:T(8,128)(2,1)S(1)}, bf16[32,2048]{1,0:T(8,128)(2,1)S(1)}, u32[]{:S(2)}, u32[]{:S(2)}) %collective-permute-start.8) | collective-permute-done | bytes 131104 | tf_op jit(solution)/shard_map/ppermute | solution.py:361
  38.4 2.5 %collective-permute-done.9.o3_ref = bf16[32,2048]{1,0:T(8,128)(2,1)S(1)} collective-permute-done((bf16[32,2048]{1,0:T(8,128)(2,1)S(1)}, bf16[32,2048]{1,0:T(8,128)(2,1)S(1)}, u32[]{:S(2)}, u32[]{:S(2)}) %collective-permute-start.9) | collective-permute-done | bytes 131104 | tf_op jit(solution)/shard_map/ppermute | solution.py:361
  40.9 0.0 copy-done.4
  40.9 0.0 copy-done.6
  40.9 2.0 %dispatch.1 = (bf16[32,2048]{1,0:T(8,128)(2,1)}, bf16[128,16,640]{2,1,0:T(8,128)(2,1)S(1)}) custom-call(s32[8,128]{1,0:T(8,128)S(1)} %get-tuple-element.20.tokens_hbm, f32[32,2048]{1,0:T(8,128)S(1)} %get-tuple-element.31.o0_ref, bf16[32,2048]{1,0:T(8,128)(2,1)S(1)} %collective-permute-done.7.o1_ref, bf16[32,2048]{1,0:T(8,128)(2,1)S(1)} %collective-permute-done.8.o2_ref, ...), custom_call_target="tpu_custom_call" | custom-call | tf_op jit(solution)/shard_map/dispatch/pallas_call | solution.py:365
  42.9 0.0 copy-start.1
  43.0 40.5 %all_to_all.10.in_ref = bf16[128,16,640]{2,1,0:T(8,128)(2,1)S(1)} all-to-all(bf16[128,16,640]{2,1,0:T(8,128)(2,1)S(1)} %get-tuple-element.37), channel_id=1, replica_groups=mesh['seq'=16,'head'=8] {'seq','head'}, dimensions={0} | all-to-all | bytes 5242880 | tf_op jit(solution)/shard_map/all_to_all | solution.py:383
  83.4 0.0 copy-done.3
  83.4 0.0 copy-done.2
  83.4 0.0 copy-done.1
  83.4 8.0 %expert.1 = bf16[128,16,640]{2,1,0:T(8,128)(2,1)S(1)} custom-call(bf16[128,16,640]{2,1,0:T(8,128)(2,1)S(1)} %all_to_all.10.in_ref, bf16[1,2048,768]{2,1,0:T(8,128)(2,1)S(1)} %copy-done.1, bf16[1,2048,768]{2,1,0:T(8,128)(2,1)S(1)} %copy-done.2, bf16[1,768,2048]{2,1,0:T(8,128)(2,1)S(1)} %copy-done.3), custom_call_target="tpu_custom_call" | custom-call | tf_op jit(solution)/shard_map/expert/pallas_call | solution.py:385
  91.5 0.0 copy-start.7
  91.5 40.2 %all_to_all.11.back_ref = bf16[128,16,640]{2,1,0:T(8,128)(2,1)S(1)} all-to-all(bf16[128,16,640]{2,1,0:T(8,128)(2,1)S(1)} %expert.1), channel_id=1, replica_groups=mesh['seq'=16,'head'=8] {'seq','head'}, dimensions={0} | all-to-all | bytes 5242880 | tf_op jit(solution)/shard_map/all_to_all | solution.py:399
  131.7 0.0 copy-done.7
  131.7 2.1 %combine.1 = bf16[32,2048]{1,0:T(8,128)(2,1)} custom-call(s32[8,32]{1,0:T(8,128)S(1)} %bitcast.5, s32[8,32]{1,0:T(8,128)S(1)} %get-tuple-element.36.slots_ref, f32[8,32]{1,0:T(8,128)S(1)} %bitcast.7, bf16[128,16,640]{2,1,0:T(8,128)(2,1)S(1)} %all_to_all.11.back_ref), custom_call_target="tpu_custom_call" | custom-call | tf_op jit(solution)/shard_map/combine/pallas_call | solution.py:401
  (2 shorter events, 0.0 us)
Async XLA Ops:
  0.6 20.4 %copy-start = (bf16[512,2048]{1,0:T(8,128)(2,1)S(1)}, bf16[512,2048]{1,0:T(8,128)(2,1)}, u32[]{:S(2)}) copy-start(bf16[512,2048]{1,0:T(8,128)(2,1)} %w_ref.3) | copy-start | bytes 6291460
  0.6 20.4 %copy-start.8 = (f32[128]{0:T(128)S(1)}, f32[128]{0:T(128)}, u32[]{:S(2)}) copy-start(f32[128]{0:T(128)} %param.15) | copy-start | bytes 1540
  2.7 6.7 %collective-permute-start.2 = (bf16[4,128,128]{2,1,0:T(8,128)(2,1)S(1)}, bf16[4,128,128]{2,1,0:T(8,128)(2,1)S(1)}, u32[]{:S(2)}, u32[]{:S(2)}) collective-permute-start(bf16[4,128,128]{2,1,0:T(8,128)(2,1)S(1)} %get-tuple-element.24.own_ref), channel_id=1, source_target_pairs={{0,24},{1,97},{2,26},{3,99},{4,28},{5,101},{6,30},{7,103},{8,16},{... | collective-permute-start | bytes 393224 | tf_op jit(solution)/shard_map/ppermute | solution.py:292
  6.1 5.3 %collective-permute-start.1 = (bf16[4,128,128]{2,1,0:T(8,128)(2,1)S(1)}, bf16[4,128,128]{2,1,0:T(8,128)(2,1)S(1)}, u32[]{:S(2)}, u32[]{:S(2)}) collective-permute-start(bf16[4,128,128]{2,1,0:T(8,128)(2,1)S(1)} %get-tuple-element.24.own_ref), channel_id=1, source_target_pairs={{0,16},{1,65},{2,18},{3,67},{4,20},{5,69},{6,22},{7,71},{8,24},{9,... | collective-permute-start | bytes 393224 | tf_op jit(solution)/shard_map/ppermute | solution.py:292
  6.6 4.8 %collective-permute-start = (bf16[4,128,128]{2,1,0:T(8,128)(2,1)S(1)}, bf16[4,128,128]{2,1,0:T(8,128)(2,1)S(1)}, u32[]{:S(2)}, u32[]{:S(2)}) collective-permute-start(bf16[4,128,128]{2,1,0:T(8,128)(2,1)S(1)} %get-tuple-element.24.own_ref), channel_id=1, source_target_pairs={{0,8},{1,33},{2,10},{3,35},{4,12},{5,37},{6,14},{7,39},{8,0},{9,41... | collective-permute-start | bytes 393224 | tf_op jit(solution)/shard_map/ppermute | solution.py:292
  11.6 4.0 %collective-permute-start.3 = (bf16[4,128,128]{2,1,0:T(8,128)(2,1)S(1)}, bf16[4,128,128]{2,1,0:T(8,128)(2,1)S(1)}, u32[]{:S(2)}, u32[]{:S(2)}) collective-permute-start(bf16[4,128,128]{2,1,0:T(8,128)(2,1)S(1)} %get-tuple-element.26), channel_id=1, source_target_pairs={{0,32},{1,9},{2,34},{3,11},{4,36},{5,13},{6,38},{7,15},{8,40},{9,1... | collective-permute-start | bytes 393224 | tf_op jit(solution)/shard_map/ppermute | solution.py:292
  13.0 6.4 %collective-permute-start.4 = (bf16[4,128,128]{2,1,0:T(8,128)(2,1)S(1)}, bf16[4,128,128]{2,1,0:T(8,128)(2,1)S(1)}, u32[]{:S(2)}, u32[]{:S(2)}) collective-permute-start(bf16[4,128,128]{2,1,0:T(8,128)(2,1)S(1)} %get-tuple-element.27), channel_id=1, source_target_pairs={{0,64},{1,17},{2,66},{3,19},{4,68},{5,21},{6,70},{7,23},{8,72},{9,... | collective-permute-start | bytes 393224 | tf_op jit(solution)/shard_map/ppermute | solution.py:292
  15.6 5.5 %collective-permute-start.5 = (bf16[4,128,128]{2,1,0:T(8,128)(2,1)S(1)}, bf16[4,128,128]{2,1,0:T(8,128)(2,1)S(1)}, u32[]{:S(2)}, u32[]{:S(2)}) collective-permute-start(bf16[4,128,128]{2,1,0:T(8,128)(2,1)S(1)} %get-tuple-element.28), channel_id=1, source_target_pairs={{0,96},{1,25},{2,98},{3,27},{4,100},{5,29},{6,102},{7,31},{8,104},... | collective-permute-start | bytes 393224 | tf_op jit(solution)/shard_map/ppermute | solution.py:292
  22.2 10.2 %copy-start.5 = (s32[32,8]{0,1:T(8,128)S(1)}, s32[32,8]{0,1:T(8,128)}, u32[]{:S(2)}) copy-start(s32[32,8]{0,1:T(8,128)} %param.19) | copy-start | bytes 3076
  22.2 18.7 %copy-start.4 = (bf16[32,2048]{1,0:T(8,128)(2,1)S(1)}, bf16[32,2048]{1,0:T(8,128)(2,1)}, u32[]{:S(2)}) copy-start(bf16[32,2048]{1,0:T(8,128)(2,1)} %res_ref.1) | copy-start | bytes 393220
  22.2 18.7 %copy-start.6 = (f32[2048]{0:T(1024)S(1)}, f32[2048]{0:T(1024)}, u32[]{:S(2)}) copy-start(f32[2048]{0:T(1024)} %param.18) | copy-start | bytes 24580
  22.2 5.0 %collective-permute-start.6 = (bf16[4,32,2048]{2,1,0:T(8,128)(2,1)S(1)}, bf16[4,32,2048]{2,1,0:T(8,128)(2,1)S(1)}, u32[]{:S(2)}, u32[]{:S(2)}) collective-permute-start(bf16[4,32,2048]{2,1,0:T(8,128)(2,1)S(1)} %get-tuple-element.30), channel_id=1, source_target_pairs={{0,1},{1,0},{2,3},{3,2},{4,5},{5,4},{6,7},{7,6},{8,9},{9,8},{10,11... | collective-permute-start | bytes 1572872 | tf_op jit(solution)/shard_map/ppermute | solution.py:341
  25.7 57.8 %copy-start.3 = (bf16[1,768,2048]{2,1,0:T(8,128)(2,1)S(1)}, bf16[1,768,2048]{2,1,0:T(8,128)(2,1)}, u32[]{:S(2)}) copy-start(bf16[1,768,2048]{2,1,0:T(8,128)(2,1)} %down_ref.1) | copy-start | bytes 9437188
  27.2 56.2 %copy-start.2 = (bf16[1,2048,768]{2,1,0:T(8,128)(2,1)S(1)}, bf16[1,2048,768]{2,1,0:T(8,128)(2,1)}, u32[]{:S(2)}) copy-start(bf16[1,2048,768]{2,1,0:T(8,128)(2,1)} %up_ref.1) | copy-start | bytes 9437188
  27.3 6.0 %collective-permute-start.7 = (bf16[32,2048]{1,0:T(8,128)(2,1)S(1)}, bf16[32,2048]{1,0:T(8,128)(2,1)S(1)}, u32[]{:S(2)}, u32[]{:S(2)}) collective-permute-start(bf16[32,2048]{1,0:T(8,128)(2,1)S(1)} %get-tuple-element.32), channel_id=1, source_target_pairs={{0,2},{1,3},{2,0},{3,1},{4,6},{5,7},{6,4},{7,5},{8,10},{9,11},{10,... | collective-permute-start | bytes 393224 | tf_op jit(solution)/shard_map/ppermute | solution.py:361
  29.0 9.4 %collective-permute-start.8 = (bf16[32,2048]{1,0:T(8,128)(2,1)S(1)}, bf16[32,2048]{1,0:T(8,128)(2,1)S(1)}, u32[]{:S(2)}, u32[]{:S(2)}) collective-permute-start(bf16[32,2048]{1,0:T(8,128)(2,1)S(1)} %get-tuple-element.33), channel_id=1, source_target_pairs={{0,4},{1,5},{2,6},{3,7},{4,0},{5,1},{6,2},{7,3},{8,12},{9,13},{10,... | collective-permute-start | bytes 393224 | tf_op jit(solution)/shard_map/ppermute | solution.py:361
  32.3 8.6 %collective-permute-start.9 = (bf16[32,2048]{1,0:T(8,128)(2,1)S(1)}, bf16[32,2048]{1,0:T(8,128)(2,1)S(1)}, u32[]{:S(2)}, u32[]{:S(2)}) collective-permute-start(bf16[32,2048]{1,0:T(8,128)(2,1)S(1)} %get-tuple-element.34), channel_id=1, source_target_pairs={{0,6},{1,7},{2,4},{3,5},{4,2},{5,3},{6,0},{7,1},{8,14},{9,15},{10,... | collective-permute-start | bytes 393224 | tf_op jit(solution)/shard_map/ppermute | solution.py:361
  42.9 40.5 %copy-start.1 = (bf16[1,2048,768]{2,1,0:T(8,128)(2,1)S(1)}, bf16[1,2048,768]{2,1,0:T(8,128)(2,1)}, u32[]{:S(2)}) copy-start(bf16[1,2048,768]{2,1,0:T(8,128)(2,1)} %gate_ref.1) | copy-start | bytes 9437188
  91.5 40.2 %copy-start.7 = (f32[32,8]{0,1:T(8,128)S(1)}, f32[32,8]{0,1:T(8,128)}, u32[]{:S(2)}) copy-start(f32[32,8]{0,1:T(8,128)} %param.20) | copy-start | bytes 3076

commit v5 on v4

--- a/solution.py
+++ b/solution.py
@@ -85,9 +85,8 @@
         out[...] = jnp.where((second ^ k) > second, later, sooner).astype(BF16)
 
 
-def project_kernel(
-    heads, hd, parts, q_ref, in_ref, base_ref, s1_ref, s2_ref, s3_ref, gain_ref, w_ref,
-    normed_ref, theirs_ref,
+def normed_kernel(
+    heads, hd, parts, q_ref, in_ref, base_ref, s1_ref, s2_ref, s3_ref, gain_ref, mine_ref, theirs_ref,
 ):
     rows = q_ref.shape[0]
     step = rows // parts
@@ -103,27 +102,30 @@
         )
         mean = jnp.mean(att * att, axis=-1, keepdims=True)
         norm = (att * lax.rsqrt(mean + 1e-06) * gain).astype(BF16)
-        normed_ref[:, :, cols] = norm.reshape(parts, step, hd)
-    theirs_ref[...] = projected(normed_ref, w_ref, 1 - core).astype(BF16)
-
-
-def projected(normed_ref, w_ref, which):
-    half = normed_ref.shape[0] // 2
-    picked = jnp.concatenate([normed_ref[2 * z + which] for z in range(half)], axis=0)
-    made = jnp.dot(picked, w_ref[...], preferred_element_type=F32)
-    return made.reshape(half, normed_ref.shape[1], w_ref.shape[1])
+        blocks = norm.reshape(parts // 2, 2, step, hd)
+        even, odd = blocks[:, 0], blocks[:, 1]
+        mine_ref[:, :, cols] = jnp.where(core == 0, even, odd)
+        theirs_ref[:, :, cols] = jnp.where(core == 0, odd, even)
+
+
+def projected(normed_ref, w_ref):
+    zs, step, depth = normed_ref.shape
+    made = jnp.dot(
+        normed_ref[...].reshape(zs * step, depth), w_ref[...], preferred_element_type=F32
+    )
+    return made.reshape(zs, step, w_ref.shape[1])
 
 
 def keep_kernel(normed_ref, w_ref, mine_ref):
-    mine_ref[...] = projected(normed_ref, w_ref, lax.rem(lax.axis_index("head"), 2))
-
-
-def pair_kernel(zs, mine_ref, got_ref, *outs):
+    mine_ref[...] = projected(normed_ref, w_ref)
+
+
+def pair_kernel(zs, mine_ref, got_ref, w_ref, *refs):
+    outs, sum_ref = refs[:-1], refs[-1]
     z = lax.div(lax.axis_index("head"), 2)
+    sum_ref[...] = mine_ref[...] + projected(got_ref, w_ref)
     for k in range(zs):
-        block = z ^ k
-        total = mine_ref[block] + got_ref[block].astype(F32)
-        outs[k][...] = total.astype(outs[k].dtype)
+        outs[k][...] = sum_ref[z ^ k].astype(outs[k].dtype)
 
 
 def routing_kernel(cap, routed_ref, slots_ref, tokens_ref):
@@ -291,6 +293,7 @@
             pairs.append((device, device ^ (k * parts * (1 if along_y else ys))))
         return lax.ppermute(value, ("seq", "head"), pairs)
 
+    other_weight = lax.ppermute(out_weight, "head", [(i, i ^ 1) for i in range(parts)])
     first = [exchange(totals, k, 0) for k in range(1, ys)]
     within = pl.pallas_call(
         functools.partial(within_kernel, heads, hd),
@@ -326,18 +329,13 @@
     second = [exchange(value, k, 1) for k, value in enumerate(sent, 1)]
 
     normed, theirs = pl.pallas_call(
-        functools.partial(project_kernel, heads, hd, parts),
-        out_shape=(
-            jax.ShapeDtypeStruct((parts, own_rows, local), BF16),
-            jax.ShapeDtypeStruct((zs, own_rows, width), BF16),
-        ),
-        in_specs=[VM] * 8,
+        functools.partial(normed_kernel, heads, hd, parts),
+        out_shape=(jax.ShapeDtypeStruct((zs, own_rows, local), BF16),) * 2,
+        in_specs=[VM] * 7,
         out_specs=(VM, VM),
         compiler_params=params(2),
-        name="project",
-    )(
-        queries, within, base, *second, head_gain.reshape(1, hd), out_weight
-    )
+        name="normed",
+    )(queries, within, base, *second, head_gain.reshape(1, hd))
     got = lax.ppermute(theirs, "head", [(i, i ^ 1) for i in range(parts)])
     mine = pl.pallas_call(
         keep_kernel,
@@ -352,11 +350,12 @@
         out_shape=tuple(
             jax.ShapeDtypeStruct((own_rows, width), F32 if k == 0 else BF16) for k in range(zs)
         ),
-        in_specs=[VM, VM],
+        in_specs=[VM] * 3,
         out_specs=(VM,) * zs,
-        compiler_params=params(2),
+        scratch_shapes=[pltpu.VMEM((zs, own_rows, width), F32)],
+        compiler_params=params(4),
         name="pair",
-    )(mine, got)
+    )(mine, got, other_weight)
     from_z = [
         lax.ppermute(blocks[k], "head", [(i, i ^ (2 * k)) for i in range(parts)])
         for k in range(1, zs)

time: 134 us -> 133 us (level)
    ppermute x0 -> x1, starting transfers between devices: none -> 1.5 us  [shards(): lax.ppermute(out_weight, 'head', [(i, i ^ 1) for i in range(parts)])]
  transfers between devices with their start and end apart: 10 -> 11, of which waited for: 7 -> 7; matrix products, arithmetic and copies ran while one was open for 0% -> 0% of each run, Pallas kernels for 3% -> 5%
where the time goes in v5:
time: 133 us
  blocking collectives  80.7 us (61%)
  Pallas kernels  19 us (14%)
  starting transfers between devices  16.6 us (12%)
  waiting for transfers between devices  16 us (12%)
    all_to_all x1, blocking collectives, shards(): lax.all_to_all(outgoing, ('seq', 'head'), split_axis=0, concat_axis=0, ti...  40.5 us
    all_to_all x1, blocking collectives, shards(): lax.all_to_all(produced, ('seq', 'head'), split_axis=0, concat_axis=0, ti...  40.2 us
    pallas_call x1, Pallas kernels, shards(): pl.pallas_call(functools.partial(expert_kernel, cap), out_shape=jax.Shape...  8.03 us
    ppermute x6, waiting for transfers between devices, exchange(): return lax.ppermute(value, ('seq', 'head'), pairs)  7.91 us
    ppermute x3, waiting for transfers between devices, shards(): lax.ppermute(blocks[k], 'head', [(i, i ^ 2 * k) for i in range(parts)])  7.63 us
    ppermute x6, starting transfers between devices, exchange(): return lax.ppermute(value, ('seq', 'head'), pairs)  7.27 us
    ppermute x3, starting transfers between devices, shards(): lax.ppermute(blocks[k], 'head', [(i, i ^ 2 * k) for i in range(parts)])  5.02 us
    ppermute x1, starting transfers between devices, shards(): got = lax.ppermute(theirs, 'head', [(i, i ^ 1) for i in range(parts)])  2.81 us
  transfers between devices with their start and end apart: 11, of which 7 were waited for; matrix products, arithmetic and copies ran while one was open for 0% of the time, Pallas kernels for 5%

profile of v5, /device:TPU:1, one launch (start us, length us, event | category | flops | bytes accessed | tf_op | source)
XLA Modules:
  0.0 133.2 jit_solution(9112666178681393463)
XLA Ops:
  0.6 0.0 copy-start.8
  0.6 1.5 %collective-permute-start.7 = (bf16[512,2048]{1,0:T(8,128)(2,1)}, bf16[512,2048]{1,0:T(8,128)(2,1)S(1)}, u32[]{:S(2)}, u32[]{:S(2)}) collective-permute-start(bf16[512,2048]{1,0:T(8,128)(2,1)} %w_ref.1), channel_id=1, source_target_pairs={{0,1},{1,0},{2,3},{3,2},{4,5},{5,4},{6,7},{7,6},{8,9},{9,8},{10,11... | collective-permute-start | bytes 6291464 | tf_op jit(solution)/shard_map/ppermute | solution.py:296
  2.1 1.9 %totals.1 = (bf16[4,128,128]{2,1,0:T(8,128)(2,1)S(1)}, f32[256,512]{1,0:T(8,128)S(1)}, f32[256,512]{1,0:T(8,128)S(1)}, f32[256,512]{1,0:T(8,128)S(1)}) custom-call(f32[256,512]{1,0:T(8,128)} %q_hbm.1, f32[256,512]{1,0:T(8,128)} %k_hbm.1, f32[256,512]{1,0:T(8,128)} %v_hbm.1), custom_call_target="tpu_custom_call" | custom-call | tf_op jit(solution)/shard_map/totals/pallas_call | solution.py:278
  4.0 2.6 %collective-permute-start.2 = (bf16[4,128,128]{2,1,0:T(8,128)(2,1)S(1)}, bf16[4,128,128]{2,1,0:T(8,128)(2,1)S(1)}, u32[]{:S(2)}, u32[]{:S(2)}) collective-permute-start(bf16[4,128,128]{2,1,0:T(8,128)(2,1)S(1)} %get-tuple-element.24.own_ref), channel_id=1, source_target_pairs={{0,24},{1,97},{2,26},{3,99},{4,28},{5,101},{6,30},{7,103},{8,16},{... | collective-permute-start | bytes 393224 | tf_op jit(solution)/shard_map/ppermute | solution.py:294
  6.6 0.5 collective-permute-start.1
  7.2 0.2 collective-permute-start
  7.3 0.0 copy-start.3
  7.4 2.2 %within.1.refs_3_.in_ref = f32[256,512]{1,0:T(8,128)S(1)} custom-call(f32[256,512]{1,0:T(8,128)S(1)} %get-tuple-element.21.q_ref, f32[256,512]{1,0:T(8,128)S(1)} %get-tuple-element.22.k_ref, f32[256,512]{1,0:T(8,128)S(1)} %get-tuple-element.23.v_ref), custom_call_target="tpu_custom_call" | custom-call | flops 805306368 | bytes 2097152 | tf_op jit(solution)/shard_map/within/pallas_call | solution.py:298
  9.6 0.4 collective-permute-done.2.refs_2_
  10.0 2.3 %collective-permute-done.1.refs_1_ = bf16[4,128,128]{2,1,0:T(8,128)(2,1)S(1)} collective-permute-done((bf16[4,128,128]{2,1,0:T(8,128)(2,1)S(1)}, bf16[4,128,128]{2,1,0:T(8,128)(2,1)S(1)}, u32[]{:S(2)}, u32[]{:S(2)}) %collective-permute-start.1) | collective-permute-done | bytes 131104 | tf_op jit(solution)/shard_map/ppermute | solution.py:294
  12.3 0.0 collective-permute-done.refs_0_
  12.3 0.2 plane.1
  12.5 1.1 collective-permute-start.3
  13.6 2.6 %collective-permute-start.4 = (bf16[4,128,128]{2,1,0:T(8,128)(2,1)S(1)}, bf16[4,128,128]{2,1,0:T(8,128)(2,1)S(1)}, u32[]{:S(2)}, u32[]{:S(2)}) collective-permute-start(bf16[4,128,128]{2,1,0:T(8,128)(2,1)S(1)} %get-tuple-element.27), channel_id=1, source_target_pairs={{0,64},{1,17},{2,66},{3,19},{4,68},{5,21},{6,70},{7,23},{8,72},{9,... | collective-permute-start | bytes 393224 | tf_op jit(solution)/shard_map/ppermute | solution.py:294
  16.2 0.2 collective-permute-start.5
  16.4 0.0 collective-permute-done.3.s1_ref
  16.4 3.5 %collective-permute-done.4.s2_ref = bf16[4,128,128]{2,1,0:T(8,128)(2,1)S(1)} collective-permute-done((bf16[4,128,128]{2,1,0:T(8,128)(2,1)S(1)}, bf16[4,128,128]{2,1,0:T(8,128)(2,1)S(1)}, u32[]{:S(2)}, u32[]{:S(2)}) %collective-permute-start.4) | collective-permute-done | bytes 131104 | tf_op jit(solution)/shard_map/ppermute | solution.py:294
  19.9 1.7 %collective-permute-done.5.s3_ref = bf16[4,128,128]{2,1,0:T(8,128)(2,1)S(1)} collective-permute-done((bf16[4,128,128]{2,1,0:T(8,128)(2,1)S(1)}, bf16[4,128,128]{2,1,0:T(8,128)(2,1)S(1)}, u32[]{:S(2)}, u32[]{:S(2)}) %collective-permute-start.5) | collective-permute-done | bytes 131104 | tf_op jit(solution)/shard_map/ppermute | solution.py:294
  21.6 0.0 copy-done.8
  21.6 0.7 normed.1
  22.4 2.8 %collective-permute-start.6 = (bf16[4,32,512]{2,1,0:T(8,128)(2,1)S(1)}, bf16[4,32,512]{2,1,0:T(8,128)(2,1)S(1)}, u32[]{:S(2)}, u32[]{:S(2)}) collective-permute-start(bf16[4,32,512]{2,1,0:T(8,128)(2,1)S(1)} %get-tuple-element.30), channel_id=1, source_target_pairs={{0,1},{1,0},{2,3},{3,2},{4,5},{5,4},{6,7},{7,6},{8,9},{9,8},{10,11... | collective-permute-start | bytes 393224 | tf_op jit(solution)/shard_map/ppermute | solution.py:339
  25.2 0.0 copy-done.3
  25.2 0.0 copy-start.2
  25.2 0.5 keep.1.mine_ref
  25.7 0.5 collective-permute-done.6.got_ref
  26.2 0.0 collective-permute-done.7.w_ref
  26.2 0.5 pair.1
  26.7 1.7 %collective-permute-start.8 = (bf16[32,2048]{1,0:T(8,128)(2,1)S(1)}, bf16[32,2048]{1,0:T(8,128)(2,1)S(1)}, u32[]{:S(2)}, u32[]{:S(2)}) collective-permute-start(bf16[32,2048]{1,0:T(8,128)(2,1)S(1)} %get-tuple-element.32), channel_id=1, source_target_pairs={{0,2},{1,3},{2,0},{3,1},{4,6},{5,7},{6,4},{7,5},{8,10},{9,11},{10,... | collective-permute-start | bytes 393224 | tf_op jit(solution)/shard_map/ppermute | solution.py:360
  28.4 3.3 %collective-permute-start.9 = (bf16[32,2048]{1,0:T(8,128)(2,1)S(1)}, bf16[32,2048]{1,0:T(8,128)(2,1)S(1)}, u32[]{:S(2)}, u32[]{:S(2)}) collective-permute-start(bf16[32,2048]{1,0:T(8,128)(2,1)S(1)} %get-tuple-element.33), channel_id=1, source_target_pairs={{0,4},{1,5},{2,6},{3,7},{4,0},{5,1},{6,2},{7,3},{8,12},{9,13},{10,... | collective-permute-start | bytes 393224 | tf_op jit(solution)/shard_map/ppermute | solution.py:360
  31.7 0.0 collective-permute-start.10
  31.7 0.0 copy-done.5
  31.7 1.0 routing.1
  32.7 0.0 collective-permute-done.8.o1_ref
  32.7 5.1 %collective-permute-done.9.o2_ref = bf16[32,2048]{1,0:T(8,128)(2,1)S(1)} collective-permute-done((bf16[32,2048]{1,0:T(8,128)(2,1)S(1)}, bf16[32,2048]{1,0:T(8,128)(2,1)S(1)}, u32[]{:S(2)}, u32[]{:S(2)}) %collective-permute-start.9) | collective-permute-done | bytes 131104 | tf_op jit(solution)/shard_map/ppermute | solution.py:360
  37.8 2.5 %collective-permute-done.10.o3_ref = bf16[32,2048]{1,0:T(8,128)(2,1)S(1)} collective-permute-done((bf16[32,2048]{1,0:T(8,128)(2,1)S(1)}, bf16[32,2048]{1,0:T(8,128)(2,1)S(1)}, u32[]{:S(2)}, u32[]{:S(2)}) %collective-permute-start.10) | collective-permute-done | bytes 131104 | tf_op jit(solution)/shard_map/ppermute | solution.py:360
  40.3 0.0 copy-done.4
  40.3 0.0 copy-done.6
  40.3 2.0 %dispatch.1 = (bf16[32,2048]{1,0:T(8,128)(2,1)}, bf16[128,16,640]{2,1,0:T(8,128)(2,1)S(1)}) custom-call(s32[8,128]{1,0:T(8,128)S(1)} %get-tuple-element.20.tokens_hbm, f32[32,2048]{1,0:T(8,128)S(1)} %get-tuple-element.31.o0_ref, bf16[32,2048]{1,0:T(8,128)(2,1)S(1)} %collective-permute-done.8.o1_ref, bf16[32,2048]{1,0:T(8,128)(2,1)S(1)} %collective-permute-done.9.o2_ref, ...), custom_call_target="tpu_custom_call" | custom-call | tf_op jit(solution)/shard_map/dispatch/pallas_call | solution.py:364
  42.3 0.0 copy-start
  42.3 40.5 %all_to_all.10.in_ref = bf16[128,16,640]{2,1,0:T(8,128)(2,1)S(1)} all-to-all(bf16[128,16,640]{2,1,0:T(8,128)(2,1)S(1)} %get-tuple-element.37), channel_id=1, replica_groups=mesh['seq'=16,'head'=8] {'seq','head'}, dimensions={0} | all-to-all | bytes 5242880 | tf_op jit(solution)/shard_map/all_to_all | solution.py:382
  82.8 0.0 copy-done.2
  82.8 0.0 copy-done.1
  82.8 0.0 copy-done
  82.8 8.0 %expert.1 = bf16[128,16,640]{2,1,0:T(8,128)(2,1)S(1)} custom-call(bf16[128,16,640]{2,1,0:T(8,128)(2,1)S(1)} %all_to_all.10.in_ref, bf16[1,2048,768]{2,1,0:T(8,128)(2,1)S(1)} %copy-done, bf16[1,2048,768]{2,1,0:T(8,128)(2,1)S(1)} %copy-done.1, bf16[1,768,2048]{2,1,0:T(8,128)(2,1)S(1)} %copy-done.2), custom_call_target="tpu_custom_call" | custom-call | tf_op jit(solution)/shard_map/expert/pallas_call | solution.py:384
  90.9 0.0 copy-start.7
  90.9 40.2 %all_to_all.11.back_ref = bf16[128,16,640]{2,1,0:T(8,128)(2,1)S(1)} all-to-all(bf16[128,16,640]{2,1,0:T(8,128)(2,1)S(1)} %expert.1), channel_id=1, replica_groups=mesh['seq'=16,'head'=8] {'seq','head'}, dimensions={0} | all-to-all | bytes 5242880 | tf_op jit(solution)/shard_map/all_to_all | solution.py:398
  131.1 0.0 copy-done.7
  131.1 2.1 %combine.1 = bf16[32,2048]{1,0:T(8,128)(2,1)} custom-call(s32[8,32]{1,0:T(8,128)S(1)} %bitcast.5, s32[8,32]{1,0:T(8,128)S(1)} %get-tuple-element.36.slots_ref, f32[8,32]{1,0:T(8,128)S(1)} %bitcast.7, bf16[128,16,640]{2,1,0:T(8,128)(2,1)S(1)} %all_to_all.11.back_ref), custom_call_target="tpu_custom_call" | custom-call | tf_op jit(solution)/shard_map/combine/pallas_call | solution.py:400
  (4 shorter events, 0.0 us)
Async XLA Ops:
  0.6 21.0 %copy-start.8 = (f32[128]{0:T(128)S(1)}, f32[128]{0:T(128)}, u32[]{:S(2)}) copy-start(f32[128]{0:T(128)} %param.15) | copy-start | bytes 1540
  0.6 25.5 %collective-permute-start.7 = (bf16[512,2048]{1,0:T(8,128)(2,1)}, bf16[512,2048]{1,0:T(8,128)(2,1)S(1)}, u32[]{:S(2)}, u32[]{:S(2)}) collective-permute-start(bf16[512,2048]{1,0:T(8,128)(2,1)} %w_ref.1), channel_id=1, source_target_pairs={{0,1},{1,0},{2,3},{3,2},{4,5},{5,4},{6,7},{7,6},{8,9},{9,8},{10,11... | collective-permute-start | bytes 6291464 | tf_op jit(solution)/shard_map/ppermute | solution.py:296
  4.0 6.0 %collective-permute-start.2 = (bf16[4,128,128]{2,1,0:T(8,128)(2,1)S(1)}, bf16[4,128,128]{2,1,0:T(8,128)(2,1)S(1)}, u32[]{:S(2)}, u32[]{:S(2)}) collective-permute-start(bf16[4,128,128]{2,1,0:T(8,128)(2,1)S(1)} %get-tuple-element.24.own_ref), channel_id=1, source_target_pairs={{0,24},{1,97},{2,26},{3,99},{4,28},{5,101},{6,30},{7,103},{8,16},{... | collective-permute-start | bytes 393224 | tf_op jit(solution)/shard_map/ppermute | solution.py:294
  6.6 5.6 %collective-permute-start.1 = (bf16[4,128,128]{2,1,0:T(8,128)(2,1)S(1)}, bf16[4,128,128]{2,1,0:T(8,128)(2,1)S(1)}, u32[]{:S(2)}, u32[]{:S(2)}) collective-permute-start(bf16[4,128,128]{2,1,0:T(8,128)(2,1)S(1)} %get-tuple-element.24.own_ref), channel_id=1, source_target_pairs={{0,16},{1,65},{2,18},{3,67},{4,20},{5,69},{6,22},{7,71},{8,24},{9,... | collective-permute-start | bytes 393224 | tf_op jit(solution)/shard_map/ppermute | solution.py:294
  7.2 5.1 %collective-permute-start = (bf16[4,128,128]{2,1,0:T(8,128)(2,1)S(1)}, bf16[4,128,128]{2,1,0:T(8,128)(2,1)S(1)}, u32[]{:S(2)}, u32[]{:S(2)}) collective-permute-start(bf16[4,128,128]{2,1,0:T(8,128)(2,1)S(1)} %get-tuple-element.24.own_ref), channel_id=1, source_target_pairs={{0,8},{1,33},{2,10},{3,35},{4,12},{5,37},{6,14},{7,39},{8,0},{9,41... | collective-permute-start | bytes 393224 | tf_op jit(solution)/shard_map/ppermute | solution.py:294
  7.3 17.8 %copy-start.3 = (bf16[512,2048]{1,0:T(8,128)(2,1)S(1)}, bf16[512,2048]{1,0:T(8,128)(2,1)}, u32[]{:S(2)}) copy-start(bf16[512,2048]{1,0:T(8,128)(2,1)} %w_ref.1) | copy-start | bytes 6291460
  12.5 3.9 %collective-permute-start.3 = (bf16[4,128,128]{2,1,0:T(8,128)(2,1)S(1)}, bf16[4,128,128]{2,1,0:T(8,128)(2,1)S(1)}, u32[]{:S(2)}, u32[]{:S(2)}) collective-permute-start(bf16[4,128,128]{2,1,0:T(8,128)(2,1)S(1)} %get-tuple-element.26), channel_id=1, source_target_pairs={{0,32},{1,9},{2,34},{3,11},{4,36},{5,13},{6,38},{7,15},{8,40},{9,1... | collective-permute-start | bytes 393224 | tf_op jit(solution)/shard_map/ppermute | solution.py:294
  13.6 6.4 %collective-permute-start.4 = (bf16[4,128,128]{2,1,0:T(8,128)(2,1)S(1)}, bf16[4,128,128]{2,1,0:T(8,128)(2,1)S(1)}, u32[]{:S(2)}, u32[]{:S(2)}) collective-permute-start(bf16[4,128,128]{2,1,0:T(8,128)(2,1)S(1)} %get-tuple-element.27), channel_id=1, source_target_pairs={{0,64},{1,17},{2,66},{3,19},{4,68},{5,21},{6,70},{7,23},{8,72},{9,... | collective-permute-start | bytes 393224 | tf_op jit(solution)/shard_map/ppermute | solution.py:294
  16.2 5.5 %collective-permute-start.5 = (bf16[4,128,128]{2,1,0:T(8,128)(2,1)S(1)}, bf16[4,128,128]{2,1,0:T(8,128)(2,1)S(1)}, u32[]{:S(2)}, u32[]{:S(2)}) collective-permute-start(bf16[4,128,128]{2,1,0:T(8,128)(2,1)S(1)} %get-tuple-element.28), channel_id=1, source_target_pairs={{0,96},{1,25},{2,98},{3,27},{4,100},{5,29},{6,102},{7,31},{8,104},... | collective-permute-start | bytes 393224 | tf_op jit(solution)/shard_map/ppermute | solution.py:294
  22.4 3.8 %collective-permute-start.6 = (bf16[4,32,512]{2,1,0:T(8,128)(2,1)S(1)}, bf16[4,32,512]{2,1,0:T(8,128)(2,1)S(1)}, u32[]{:S(2)}, u32[]{:S(2)}) collective-permute-start(bf16[4,32,512]{2,1,0:T(8,128)(2,1)S(1)} %get-tuple-element.30), channel_id=1, source_target_pairs={{0,1},{1,0},{2,3},{3,2},{4,5},{5,4},{6,7},{7,6},{8,9},{9,8},{10,11... | collective-permute-start | bytes 393224 | tf_op jit(solution)/shard_map/ppermute | solution.py:339
  25.2 6.5 %copy-start.5 = (s32[32,8]{0,1:T(8,128)S(1)}, s32[32,8]{0,1:T(8,128)}, u32[]{:S(2)}) copy-start(s32[32,8]{0,1:T(8,128)} %param.19) | copy-start | bytes 3076
  25.2 15.1 %copy-start.4 = (bf16[32,2048]{1,0:T(8,128)(2,1)S(1)}, bf16[32,2048]{1,0:T(8,128)(2,1)}, u32[]{:S(2)}) copy-start(bf16[32,2048]{1,0:T(8,128)(2,1)} %res_ref.1) | copy-start | bytes 393220
  25.2 15.1 %copy-start.6 = (f32[2048]{0:T(1024)S(1)}, f32[2048]{0:T(1024)}, u32[]{:S(2)}) copy-start(f32[2048]{0:T(1024)} %param.18) | copy-start | bytes 24580
  25.2 57.6 %copy-start.2 = (bf16[1,768,2048]{2,1,0:T(8,128)(2,1)S(1)}, bf16[1,768,2048]{2,1,0:T(8,128)(2,1)}, u32[]{:S(2)}) copy-start(bf16[1,768,2048]{2,1,0:T(8,128)(2,1)} %down_ref.1) | copy-start | bytes 9437188
  26.2 56.6 %copy-start.1 = (bf16[1,2048,768]{2,1,0:T(8,128)(2,1)S(1)}, bf16[1,2048,768]{2,1,0:T(8,128)(2,1)}, u32[]{:S(2)}) copy-start(bf16[1,2048,768]{2,1,0:T(8,128)(2,1)} %up_ref.1) | copy-start | bytes 9437188
  26.7 6.0 %collective-permute-start.8 = (bf16[32,2048]{1,0:T(8,128)(2,1)S(1)}, bf16[32,2048]{1,0:T(8,128)(2,1)S(1)}, u32[]{:S(2)}, u32[]{:S(2)}) collective-permute-start(bf16[32,2048]{1,0:T(8,128)(2,1)S(1)} %get-tuple-element.32), channel_id=1, source_target_pairs={{0,2},{1,3},{2,0},{3,1},{4,6},{5,7},{6,4},{7,5},{8,10},{9,11},{10,... | collective-permute-start | bytes 393224 | tf_op jit(solution)/shard_map/ppermute | solution.py:360
  28.4 9.4 %collective-permute-start.9 = (bf16[32,2048]{1,0:T(8,128)(2,1)S(1)}, bf16[32,2048]{1,0:T(8,128)(2,1)S(1)}, u32[]{:S(2)}, u32[]{:S(2)}) collective-permute-start(bf16[32,2048]{1,0:T(8,128)(2,1)S(1)} %get-tuple-element.33), channel_id=1, source_target_pairs={{0,4},{1,5},{2,6},{3,7},{4,0},{5,1},{6,2},{7,3},{8,12},{9,13},{10,... | collective-permute-start | bytes 393224 | tf_op jit(solution)/shard_map/ppermute | solution.py:360
  31.7 8.6 %collective-permute-start.10 = (bf16[32,2048]{1,0:T(8,128)(2,1)S(1)}, bf16[32,2048]{1,0:T(8,128)(2,1)S(1)}, u32[]{:S(2)}, u32[]{:S(2)}) collective-permute-start(bf16[32,2048]{1,0:T(8,128)(2,1)S(1)} %get-tuple-element.34), channel_id=1, source_target_pairs={{0,6},{1,7},{2,4},{3,5},{4,2},{5,3},{6,0},{7,1},{8,14},{9,15},{10,... | collective-permute-start | bytes 393224 | tf_op jit(solution)/shard_map/ppermute | solution.py:360
  42.3 40.5 %copy-start = (bf16[1,2048,768]{2,1,0:T(8,128)(2,1)S(1)}, bf16[1,2048,768]{2,1,0:T(8,128)(2,1)}, u32[]{:S(2)}) copy-start(bf16[1,2048,768]{2,1,0:T(8,128)(2,1)} %gate_ref.1) | copy-start | bytes 9437188
  90.9 40.2 %copy-start.7 = (f32[32,8]{0,1:T(8,128)S(1)}, f32[32,8]{0,1:T(8,128)}, u32[]{:S(2)}) copy-start(f32[32,8]{0,1:T(8,128)} %param.20) | copy-start | bytes 3076

commit v6 on v5

--- a/solution.py
+++ b/solution.py
@@ -124,8 +124,10 @@
     outs, sum_ref = refs[:-1], refs[-1]
     z = lax.div(lax.axis_index("head"), 2)
     sum_ref[...] = mine_ref[...] + projected(got_ref, w_ref)
+    core = lax.rem(lax.axis_index("head"), 2)
     for k in range(zs):
-        outs[k][...] = sum_ref[z ^ k].astype(outs[k].dtype)
+        along = jnp.where(core == 0, k, (zs - k) % zs)
+        outs[k][...] = sum_ref[z ^ along].astype(outs[k].dtype)
 
 
 def routing_kernel(cap, routed_ref, slots_ref, tokens_ref):
@@ -357,7 +359,9 @@
         name="pair",
     )(mine, got, other_weight)
     from_z = [
-        lax.ppermute(blocks[k], "head", [(i, i ^ (2 * k)) for i in range(parts)])
+        lax.ppermute(
+            blocks[k], "head", [(i, i ^ (2 * (k if i % 2 == 0 else zs - k))) for i in range(parts)]
+        )
         for k in range(1, zs)
     ]
 

time: 133 us -> 132 us (level)
  waiting for transfers between devices: 16 us -> 13.8 us
  blocking collectives: 80.7 us -> 82.3 us
    ppermute x3, waiting for transfers between devices: 7.63 us -> 5.39 us  [shards(): lax.ppermute(blocks[k], 'head', [(i, i ^ 2 * (k if i % 2 == 0 else zs - k...]
    all_to_all x1, blocking collectives: 40.5 us -> 42.1 us  [shards(): lax.all_to_all(outgoing, ('seq', 'head'), split_axis=0, concat_axis=0, ti...]
where the time goes in v6:
time: 132 us
  blocking collectives  82.3 us (62%)
  Pallas kernels  19 us (14%)
  starting transfers between devices  16.1 us (12%)
  waiting for transfers between devices  13.8 us (10%)
    all_to_all x1, blocking collectives, shards(): lax.all_to_all(outgoing, ('seq', 'head'), split_axis=0, concat_axis=0, ti...  42.1 us
    all_to_all x1, blocking collectives, shards(): lax.all_to_all(produced, ('seq', 'head'), split_axis=0, concat_axis=0, ti...  40.2 us
    pallas_call x1, Pallas kernels, shards(): pl.pallas_call(functools.partial(expert_kernel, cap), out_shape=jax.Shape...  8.03 us
    ppermute x6, waiting for transfers between devices, exchange(): return lax.ppermute(value, ('seq', 'head'), pairs)  7.91 us
    ppermute x6, starting transfers between devices, exchange(): return lax.ppermute(value, ('seq', 'head'), pairs)  7.27 us
    ppermute x3, waiting for transfers between devices, shards(): lax.ppermute(blocks[k], 'head', [(i, i ^ 2 * (k if i % 2 == 0 else zs - k...  5.39 us
    ppermute x3, starting transfers between devices, shards(): lax.ppermute(blocks[k], 'head', [(i, i ^ 2 * (k if i % 2 == 0 else zs - k...  4.51 us
    ppermute x1, starting transfers between devices, shards(): got = lax.ppermute(theirs, 'head', [(i, i ^ 1) for i in range(parts)])  2.81 us
  transfers between devices with their start and end apart: 11, of which 7 were waited for; matrix products, arithmetic and copies ran while one was open for 0% of the time, Pallas kernels for 5%

profile of v6, /device:TPU:1, one launch (start us, length us, event | category | flops | bytes accessed | tf_op | source)
XLA Modules:
  0.0 132.0 jit_solution(17629229936635422494)
XLA Ops:
  0.6 0.0 copy-start.8
  0.6 1.5 %collective-permute-start.7 = (bf16[512,2048]{1,0:T(8,128)(2,1)}, bf16[512,2048]{1,0:T(8,128)(2,1)S(1)}, u32[]{:S(2)}, u32[]{:S(2)}) collective-permute-start(bf16[512,2048]{1,0:T(8,128)(2,1)} %w_ref.1), channel_id=1, source_target_pairs={{0,1},{1,0},{2,3},{3,2},{4,5},{5,4},{6,7},{7,6},{8,9},{9,8},{10,11... | collective-permute-start | bytes 6291464 | tf_op jit(solution)/shard_map/ppermute | solution.py:298
  2.1 1.9 %totals.1 = (bf16[4,128,128]{2,1,0:T(8,128)(2,1)S(1)}, f32[256,512]{1,0:T(8,128)S(1)}, f32[256,512]{1,0:T(8,128)S(1)}, f32[256,512]{1,0:T(8,128)S(1)}) custom-call(f32[256,512]{1,0:T(8,128)} %q_hbm.1, f32[256,512]{1,0:T(8,128)} %k_hbm.1, f32[256,512]{1,0:T(8,128)} %v_hbm.1), custom_call_target="tpu_custom_call" | custom-call | tf_op jit(solution)/shard_map/totals/pallas_call | solution.py:280
  4.0 2.6 %collective-permute-start.2 = (bf16[4,128,128]{2,1,0:T(8,128)(2,1)S(1)}, bf16[4,128,128]{2,1,0:T(8,128)(2,1)S(1)}, u32[]{:S(2)}, u32[]{:S(2)}) collective-permute-start(bf16[4,128,128]{2,1,0:T(8,128)(2,1)S(1)} %get-tuple-element.24.own_ref), channel_id=1, source_target_pairs={{0,24},{1,97},{2,26},{3,99},{4,28},{5,101},{6,30},{7,103},{8,16},{... | collective-permute-start | bytes 393224 | tf_op jit(solution)/shard_map/ppermute | solution.py:296
  6.6 0.5 collective-permute-start.1
  7.2 0.2 collective-permute-start
  7.3 0.0 copy-start.3
  7.4 2.2 %within.1.refs_3_.in_ref = f32[256,512]{1,0:T(8,128)S(1)} custom-call(f32[256,512]{1,0:T(8,128)S(1)} %get-tuple-element.21.q_ref, f32[256,512]{1,0:T(8,128)S(1)} %get-tuple-element.22.k_ref, f32[256,512]{1,0:T(8,128)S(1)} %get-tuple-element.23.v_ref), custom_call_target="tpu_custom_call" | custom-call | flops 805306368 | bytes 2097152 | tf_op jit(solution)/shard_map/within/pallas_call | solution.py:300
  9.6 0.4 collective-permute-done.2.refs_2_
  10.0 2.3 %collective-permute-done.1.refs_1_ = bf16[4,128,128]{2,1,0:T(8,128)(2,1)S(1)} collective-permute-done((bf16[4,128,128]{2,1,0:T(8,128)(2,1)S(1)}, bf16[4,128,128]{2,1,0:T(8,128)(2,1)S(1)}, u32[]{:S(2)}, u32[]{:S(2)}) %collective-permute-start.1) | collective-permute-done | bytes 131104 | tf_op jit(solution)/shard_map/ppermute | solution.py:296
  12.3 0.0 collective-permute-done.refs_0_
  12.3 0.2 plane.1
  12.5 1.1 collective-permute-start.3
  13.6 2.6 %collective-permute-start.4 = (bf16[4,128,128]{2,1,0:T(8,128)(2,1)S(1)}, bf16[4,128,128]{2,1,0:T(8,128)(2,1)S(1)}, u32[]{:S(2)}, u32[]{:S(2)}) collective-permute-start(bf16[4,128,128]{2,1,0:T(8,128)(2,1)S(1)} %get-tuple-element.27), channel_id=1, source_target_pairs={{0,64},{1,17},{2,66},{3,19},{4,68},{5,21},{6,70},{7,23},{8,72},{9,... | collective-permute-start | bytes 393224 | tf_op jit(solution)/shard_map/ppermute | solution.py:296
  16.2 0.2 collective-permute-start.5
  16.4 0.0 collective-permute-done.3.s1_ref
  16.4 3.5 %collective-permute-done.4.s2_ref = bf16[4,128,128]{2,1,0:T(8,128)(2,1)S(1)} collective-permute-done((bf16[4,128,128]{2,1,0:T(8,128)(2,1)S(1)}, bf16[4,128,128]{2,1,0:T(8,128)(2,1)S(1)}, u32[]{:S(2)}, u32[]{:S(2)}) %collective-permute-start.4) | collective-permute-done | bytes 131104 | tf_op jit(solution)/shard_map/ppermute | solution.py:296
  19.9 1.7 %collective-permute-done.5.s3_ref = bf16[4,128,128]{2,1,0:T(8,128)(2,1)S(1)} collective-permute-done((bf16[4,128,128]{2,1,0:T(8,128)(2,1)S(1)}, bf16[4,128,128]{2,1,0:T(8,128)(2,1)S(1)}, u32[]{:S(2)}, u32[]{:S(2)}) %collective-permute-start.5) | collective-permute-done | bytes 131104 | tf_op jit(solution)/shard_map/ppermute | solution.py:296
  21.6 0.0 copy-done.8
  21.6 0.7 normed.1
  22.4 2.8 %collective-permute-start.6 = (bf16[4,32,512]{2,1,0:T(8,128)(2,1)S(1)}, bf16[4,32,512]{2,1,0:T(8,128)(2,1)S(1)}, u32[]{:S(2)}, u32[]{:S(2)}) collective-permute-start(bf16[4,32,512]{2,1,0:T(8,128)(2,1)S(1)} %get-tuple-element.30), channel_id=1, source_target_pairs={{0,1},{1,0},{2,3},{3,2},{4,5},{5,4},{6,7},{7,6},{8,9},{9,8},{10,11... | collective-permute-start | bytes 393224 | tf_op jit(solution)/shard_map/ppermute | solution.py:341
  25.2 0.0 copy-done.3
  25.2 0.0 copy-start.2
  25.2 0.5 keep.1.mine_ref
  25.7 0.5 collective-permute-done.6.got_ref
  26.2 0.0 collective-permute-done.7.w_ref
  26.2 0.5 pair.1
  26.7 3.8 %collective-permute-start.8 = (bf16[32,2048]{1,0:T(8,128)(2,1)S(1)}, bf16[32,2048]{1,0:T(8,128)(2,1)S(1)}, u32[]{:S(2)}, u32[]{:S(2)}) collective-permute-start(bf16[32,2048]{1,0:T(8,128)(2,1)S(1)} %get-tuple-element.32), channel_id=1, source_target_pairs={{0,2},{1,7},{2,0},{3,5},{4,6},{5,3},{6,4},{7,1},{8,10},{9,15},{10,... | collective-permute-start | bytes 393224 | tf_op jit(solution)/shard_map/ppermute | solution.py:362
  30.5 0.0 collective-permute-start.9
  30.5 0.7 collective-permute-start.10
  31.2 0.0 copy-done.5
  31.2 1.0 routing.1
  32.2 3.8 %collective-permute-done.8.o1_ref = bf16[32,2048]{1,0:T(8,128)(2,1)S(1)} collective-permute-done((bf16[32,2048]{1,0:T(8,128)(2,1)S(1)}, bf16[32,2048]{1,0:T(8,128)(2,1)S(1)}, u32[]{:S(2)}, u32[]{:S(2)}) %collective-permute-start.8) | collective-permute-done | bytes 131104 | tf_op jit(solution)/shard_map/ppermute | solution.py:362
  35.9 1.6 %collective-permute-done.9.o2_ref = bf16[32,2048]{1,0:T(8,128)(2,1)S(1)} collective-permute-done((bf16[32,2048]{1,0:T(8,128)(2,1)S(1)}, bf16[32,2048]{1,0:T(8,128)(2,1)S(1)}, u32[]{:S(2)}, u32[]{:S(2)}) %collective-permute-start.9) | collective-permute-done | bytes 131104 | tf_op jit(solution)/shard_map/ppermute | solution.py:362
  37.5 0.0 collective-permute-done.10.o3_ref
  37.5 0.0 copy-done.4
  37.5 0.0 copy-done.6
  37.6 2.0 %dispatch.1 = (bf16[32,2048]{1,0:T(8,128)(2,1)}, bf16[128,16,640]{2,1,0:T(8,128)(2,1)S(1)}) custom-call(s32[8,128]{1,0:T(8,128)S(1)} %get-tuple-element.20.tokens_hbm, f32[32,2048]{1,0:T(8,128)S(1)} %get-tuple-element.31.o0_ref, bf16[32,2048]{1,0:T(8,128)(2,1)S(1)} %collective-permute-done.8.o1_ref, bf16[32,2048]{1,0:T(8,128)(2,1)S(1)} %collective-permute-done.9.o2_ref, ...), custom_call_target="tpu_custom_call" | custom-call | tf_op jit(solution)/shard_map/dispatch/pallas_call | solution.py:368
  39.6 0.0 copy-start
  39.6 42.1 %all_to_all.10.in_ref = bf16[128,16,640]{2,1,0:T(8,128)(2,1)S(1)} all-to-all(bf16[128,16,640]{2,1,0:T(8,128)(2,1)S(1)} %get-tuple-element.37), channel_id=1, replica_groups=mesh['seq'=16,'head'=8] {'seq','head'}, dimensions={0} | all-to-all | bytes 5242880 | tf_op jit(solution)/shard_map/all_to_all | solution.py:386
  81.7 0.0 copy-done.2
  81.7 0.0 copy-done.1
  81.7 0.0 copy-done
  81.7 8.0 %expert.1 = bf16[128,16,640]{2,1,0:T(8,128)(2,1)S(1)} custom-call(bf16[128,16,640]{2,1,0:T(8,128)(2,1)S(1)} %all_to_all.10.in_ref, bf16[1,2048,768]{2,1,0:T(8,128)(2,1)S(1)} %copy-done, bf16[1,2048,768]{2,1,0:T(8,128)(2,1)S(1)} %copy-done.1, bf16[1,768,2048]{2,1,0:T(8,128)(2,1)S(1)} %copy-done.2), custom_call_target="tpu_custom_call" | custom-call | tf_op jit(solution)/shard_map/expert/pallas_call | solution.py:388
  89.7 0.0 copy-start.7
  89.7 40.2 %all_to_all.11.back_ref = bf16[128,16,640]{2,1,0:T(8,128)(2,1)S(1)} all-to-all(bf16[128,16,640]{2,1,0:T(8,128)(2,1)S(1)} %expert.1), channel_id=1, replica_groups=mesh['seq'=16,'head'=8] {'seq','head'}, dimensions={0} | all-to-all | bytes 5242880 | tf_op jit(solution)/shard_map/all_to_all | solution.py:402
  130.0 0.0 copy-done.7
  130.0 2.1 %combine.1 = bf16[32,2048]{1,0:T(8,128)(2,1)} custom-call(s32[8,32]{1,0:T(8,128)S(1)} %bitcast.5, s32[8,32]{1,0:T(8,128)S(1)} %get-tuple-element.36.slots_ref, f32[8,32]{1,0:T(8,128)S(1)} %bitcast.7, bf16[128,16,640]{2,1,0:T(8,128)(2,1)S(1)} %all_to_all.11.back_ref), custom_call_target="tpu_custom_call" | custom-call | tf_op jit(solution)/shard_map/combine/pallas_call | solution.py:404
  (4 shorter events, 0.0 us)
Async XLA Ops:
  0.6 21.0 %copy-start.8 = (f32[128]{0:T(128)S(1)}, f32[128]{0:T(128)}, u32[]{:S(2)}) copy-start(f32[128]{0:T(128)} %param.15) | copy-start | bytes 1540
  0.6 25.5 %collective-permute-start.7 = (bf16[512,2048]{1,0:T(8,128)(2,1)}, bf16[512,2048]{1,0:T(8,128)(2,1)S(1)}, u32[]{:S(2)}, u32[]{:S(2)}) collective-permute-start(bf16[512,2048]{1,0:T(8,128)(2,1)} %w_ref.1), channel_id=1, source_target_pairs={{0,1},{1,0},{2,3},{3,2},{4,5},{5,4},{6,7},{7,6},{8,9},{9,8},{10,11... | collective-permute-start | bytes 6291464 | tf_op jit(solution)/shard_map/ppermute | solution.py:298
  4.0 6.0 %collective-permute-start.2 = (bf16[4,128,128]{2,1,0:T(8,128)(2,1)S(1)}, bf16[4,128,128]{2,1,0:T(8,128)(2,1)S(1)}, u32[]{:S(2)}, u32[]{:S(2)}) collective-permute-start(bf16[4,128,128]{2,1,0:T(8,128)(2,1)S(1)} %get-tuple-element.24.own_ref), channel_id=1, source_target_pairs={{0,24},{1,97},{2,26},{3,99},{4,28},{5,101},{6,30},{7,103},{8,16},{... | collective-permute-start | bytes 393224 | tf_op jit(solution)/shard_map/ppermute | solution.py:296
  6.6 5.6 %collective-permute-start.1 = (bf16[4,128,128]{2,1,0:T(8,128)(2,1)S(1)}, bf16[4,128,128]{2,1,0:T(8,128)(2,1)S(1)}, u32[]{:S(2)}, u32[]{:S(2)}) collective-permute-start(bf16[4,128,128]{2,1,0:T(8,128)(2,1)S(1)} %get-tuple-element.24.own_ref), channel_id=1, source_target_pairs={{0,16},{1,65},{2,18},{3,67},{4,20},{5,69},{6,22},{7,71},{8,24},{9,... | collective-permute-start | bytes 393224 | tf_op jit(solution)/shard_map/ppermute | solution.py:296
  7.2 5.1 %collective-permute-start = (bf16[4,128,128]{2,1,0:T(8,128)(2,1)S(1)}, bf16[4,128,128]{2,1,0:T(8,128)(2,1)S(1)}, u32[]{:S(2)}, u32[]{:S(2)}) collective-permute-start(bf16[4,128,128]{2,1,0:T(8,128)(2,1)S(1)} %get-tuple-element.24.own_ref), channel_id=1, source_target_pairs={{0,8},{1,33},{2,10},{3,35},{4,12},{5,37},{6,14},{7,39},{8,0},{9,41... | collective-permute-start | bytes 393224 | tf_op jit(solution)/shard_map/ppermute | solution.py:296
  7.3 17.8 %copy-start.3 = (bf16[512,2048]{1,0:T(8,128)(2,1)S(1)}, bf16[512,2048]{1,0:T(8,128)(2,1)}, u32[]{:S(2)}) copy-start(bf16[512,2048]{1,0:T(8,128)(2,1)} %w_ref.1) | copy-start | bytes 6291460
  12.5 3.9 %collective-permute-start.3 = (bf16[4,128,128]{2,1,0:T(8,128)(2,1)S(1)}, bf16[4,128,128]{2,1,0:T(8,128)(2,1)S(1)}, u32[]{:S(2)}, u32[]{:S(2)}) collective-permute-start(bf16[4,128,128]{2,1,0:T(8,128)(2,1)S(1)} %get-tuple-element.26), channel_id=1, source_target_pairs={{0,32},{1,9},{2,34},{3,11},{4,36},{5,13},{6,38},{7,15},{8,40},{9,1... | collective-permute-start | bytes 393224 | tf_op jit(solution)/shard_map/ppermute | solution.py:296
  13.6 6.4 %collective-permute-start.4 = (bf16[4,128,128]{2,1,0:T(8,128)(2,1)S(1)}, bf16[4,128,128]{2,1,0:T(8,128)(2,1)S(1)}, u32[]{:S(2)}, u32[]{:S(2)}) collective-permute-start(bf16[4,128,128]{2,1,0:T(8,128)(2,1)S(1)} %get-tuple-element.27), channel_id=1, source_target_pairs={{0,64},{1,17},{2,66},{3,19},{4,68},{5,21},{6,70},{7,23},{8,72},{9,... | collective-permute-start | bytes 393224 | tf_op jit(solution)/shard_map/ppermute | solution.py:296
  16.2 5.5 %collective-permute-start.5 = (bf16[4,128,128]{2,1,0:T(8,128)(2,1)S(1)}, bf16[4,128,128]{2,1,0:T(8,128)(2,1)S(1)}, u32[]{:S(2)}, u32[]{:S(2)}) collective-permute-start(bf16[4,128,128]{2,1,0:T(8,128)(2,1)S(1)} %get-tuple-element.28), channel_id=1, source_target_pairs={{0,96},{1,25},{2,98},{3,27},{4,100},{5,29},{6,102},{7,31},{8,104},... | collective-permute-start | bytes 393224 | tf_op jit(solution)/shard_map/ppermute | solution.py:296
  22.4 3.8 %collective-permute-start.6 = (bf16[4,32,512]{2,1,0:T(8,128)(2,1)S(1)}, bf16[4,32,512]{2,1,0:T(8,128)(2,1)S(1)}, u32[]{:S(2)}, u32[]{:S(2)}) collective-permute-start(bf16[4,32,512]{2,1,0:T(8,128)(2,1)S(1)} %get-tuple-element.30), channel_id=1, source_target_pairs={{0,1},{1,0},{2,3},{3,2},{4,5},{5,4},{6,7},{7,6},{8,9},{9,8},{10,11... | collective-permute-start | bytes 393224 | tf_op jit(solution)/shard_map/ppermute | solution.py:341
  25.2 6.0 %copy-start.5 = (s32[32,8]{0,1:T(8,128)S(1)}, s32[32,8]{0,1:T(8,128)}, u32[]{:S(2)}) copy-start(s32[32,8]{0,1:T(8,128)} %param.19) | copy-start | bytes 3076
  25.2 12.4 %copy-start.4 = (bf16[32,2048]{1,0:T(8,128)(2,1)S(1)}, bf16[32,2048]{1,0:T(8,128)(2,1)}, u32[]{:S(2)}) copy-start(bf16[32,2048]{1,0:T(8,128)(2,1)} %res_ref.1) | copy-start | bytes 393220
  25.2 12.4 %copy-start.6 = (f32[2048]{0:T(1024)S(1)}, f32[2048]{0:T(1024)}, u32[]{:S(2)}) copy-start(f32[2048]{0:T(1024)} %param.18) | copy-start | bytes 24580
  25.2 56.5 %copy-start.2 = (bf16[1,768,2048]{2,1,0:T(8,128)(2,1)S(1)}, bf16[1,768,2048]{2,1,0:T(8,128)(2,1)}, u32[]{:S(2)}) copy-start(bf16[1,768,2048]{2,1,0:T(8,128)(2,1)} %down_ref.1) | copy-start | bytes 9437188
  26.2 55.5 %copy-start.1 = (bf16[1,2048,768]{2,1,0:T(8,128)(2,1)S(1)}, bf16[1,2048,768]{2,1,0:T(8,128)(2,1)}, u32[]{:S(2)}) copy-start(bf16[1,2048,768]{2,1,0:T(8,128)(2,1)} %up_ref.1) | copy-start | bytes 9437188
  26.7 9.2 %collective-permute-start.8 = (bf16[32,2048]{1,0:T(8,128)(2,1)S(1)}, bf16[32,2048]{1,0:T(8,128)(2,1)S(1)}, u32[]{:S(2)}, u32[]{:S(2)}) collective-permute-start(bf16[32,2048]{1,0:T(8,128)(2,1)S(1)} %get-tuple-element.32), channel_id=1, source_target_pairs={{0,2},{1,7},{2,0},{3,5},{4,6},{5,3},{6,4},{7,1},{8,10},{9,15},{10,... | collective-permute-start | bytes 393224 | tf_op jit(solution)/shard_map/ppermute | solution.py:362
  30.5 7.0 %collective-permute-start.9 = (bf16[32,2048]{1,0:T(8,128)(2,1)S(1)}, bf16[32,2048]{1,0:T(8,128)(2,1)S(1)}, u32[]{:S(2)}, u32[]{:S(2)}) collective-permute-start(bf16[32,2048]{1,0:T(8,128)(2,1)S(1)} %get-tuple-element.33), channel_id=1, source_target_pairs={{0,4},{1,5},{2,6},{3,7},{4,0},{5,1},{6,2},{7,3},{8,12},{9,13},{10,... | collective-permute-start | bytes 393224 | tf_op jit(solution)/shard_map/ppermute | solution.py:362
  30.5 7.0 %collective-permute-start.10 = (bf16[32,2048]{1,0:T(8,128)(2,1)S(1)}, bf16[32,2048]{1,0:T(8,128)(2,1)S(1)}, u32[]{:S(2)}, u32[]{:S(2)}) collective-permute-start(bf16[32,2048]{1,0:T(8,128)(2,1)S(1)} %get-tuple-element.34), channel_id=1, source_target_pairs={{0,6},{1,3},{2,4},{3,1},{4,2},{5,7},{6,0},{7,5},{8,14},{9,11},{10,... | collective-permute-start | bytes 393224 | tf_op jit(solution)/shard_map/ppermute | solution.py:362
  39.6 42.1 %copy-start = (bf16[1,2048,768]{2,1,0:T(8,128)(2,1)S(1)}, bf16[1,2048,768]{2,1,0:T(8,128)(2,1)}, u32[]{:S(2)}) copy-start(bf16[1,2048,768]{2,1,0:T(8,128)(2,1)} %gate_ref.1) | copy-start | bytes 9437188
  89.7 40.2 %copy-start.7 = (f32[32,8]{0,1:T(8,128)S(1)}, f32[32,8]{0,1:T(8,128)}, u32[]{:S(2)}) copy-start(f32[32,8]{0,1:T(8,128)} %param.20) | copy-start | bytes 3076
